TPU v7x, 32 devices: a whole 2x2x4 slice. The times are simulated.
32 devices in a mesh: dp: 16 (over z, x, core), head: 2 (over y).
Axes of the slice: x: 2, y: 2, z: 4, core: 2. Of those that a mesh axis runs over, the one named last changes fastest.
Arguments:
- hidden_in: bfloat16 [49152, 768], P('dp'), may hold values from -6 to 6
- w_query: bfloat16 [768, 768], P(None, 'head'), may hold values from -0.21875 to 0.21875
- b_query: float32 [768], P('head'), may hold values from -3 to 3
- w_key: bfloat16 [768, 768], P(None, 'head'), may hold values from -0.21875 to 0.21875
- w_value: bfloat16 [768, 768], P(None, 'head'), may hold values from -0.21875 to 0.21875
- b_value: float32 [768], P('head'), may hold values from -3 to 3
- w_out: bfloat16 [768, 768], replicated, may hold values from -2.5 to 2.5
- b_out: float32 [768], replicated, may hold values from -3 to 3
- gain_one: float32 [768], replicated, may hold values from 0.5 to 1.5
- shift_one: float32 [768], replicated, may hold values from -3 to 3
- w_up: bfloat16 [768, 3072], replicated, may hold values from -0.21875 to 0.21875
- b_up: float32 [3072], replicated, may hold values from -3 to 3
- w_down: bfloat16 [3072, 768], replicated, may hold values from -0.109375 to 0.109375
- b_down: float32 [768], replicated, may hold values from -3 to 3
- gain_two: float32 [768], replicated, may hold values from 0.5 to 1.5
- shift_two: float32 [768], replicated, may hold values from -3 to 3
- seq_length: int32 [16], P('dp'), may hold values from 1024 to 1536, as said below
- block_perm: int32 [96, 12], P('dp', 'head'), may hold values from 0 to 2, as said below
- cotangent: bfloat16 [49152, 768], P(('dp', 'head')), may hold values from -6 to 6
Outputs:
- block_out: bfloat16 [49152, 768], P(('dp', 'head'))
- input_grad: float32 [49152, 768], P(('dp', 'head'))
- grad_query: float32 [768, 768], P(None, 'head')
- grad_query_bias: float32 [768], P('head')
- grad_key: float32 [768, 768], P(None, 'head')
- grad_value: float32 [768, 768], P(None, 'head')
- grad_value_bias: float32 [768], P('head')
- grad_out: float32 [768, 768], P(None, 'head')
- grad_out_bias: float32 [768], P('head')
- grad_gain_one: float32 [768], P('head')
- grad_shift_one: float32 [768], P('head')
- grad_up: float32 [768, 3072], P(None, 'head')
- grad_up_bias: float32 [3072], P('head')
- grad_down: float32 [3072, 768], P(None, 'head')
- grad_down_bias: float32 [768], P('head')
- grad_gain_two: float32 [768], P('head')
- grad_shift_two: float32 [768], P('head')
Inputs may be any that keep to these rules, and one draw needn't show every extreme that they name: `seq_length`: every sequence of one index of dp has the same length, 1024 or 1536; some index has each. `block_perm`: for each head, the entries of the blocks of one sequence are the numbers 0 to (its blocks - 1), each once.
All inputs are finite; a program needn't handle non-finite values.
Results may differ from a plain program's by a relative error of at most 0.014.
Values may be sent and summed in bfloat16 or wider, within the bound.
No kernel may reach another device: no remote copies, remote signals or barrier semaphores. Data moves between devices by JAX's collectives and lax.ppermute only.
A program may use at most 192 MiB of HBM per device.

v0:
```python
from functools import partial

import jax
import jax.numpy as jnp
from jax import lax
from jax.sharding import PartitionSpec as P

HEAD_DIM = 64
BLOCK = 512


norm_epsilon = 1e-05


def norm_forward(summed, gain, shift):
    average = jnp.mean(summed, axis=-1, keepdims=True)
    centred = summed - average
    variance = jnp.mean(centred * centred, axis=-1, keepdims=True)
    inverse = lax.rsqrt(variance + norm_epsilon)
    normed = centred * inverse
    return (normed * gain + shift, normed, inverse)


def norm_backward(incoming, normed, inverse, gain):
    scaled = incoming * gain
    first_mean = jnp.mean(scaled, axis=-1, keepdims=True)
    second_mean = jnp.mean(scaled * normed, axis=-1, keepdims=True)
    grad_input = inverse * (scaled - first_mean - normed * second_mean)
    return (grad_input, jnp.sum(incoming * normed, axis=0), jnp.sum(incoming, axis=0))


def by_head(matrix, block_count, local_heads):
    return matrix.reshape(block_count, BLOCK, local_heads, HEAD_DIM).transpose(2, 0, 1, 3)


def from_head(stacked):
    local_heads = stacked.shape[0]
    block_count = stacked.shape[1]
    return stacked.transpose(1, 2, 0, 3).reshape(block_count * BLOCK, local_heads * HEAD_DIM)


def attend_head(inputs):
    query_matrix, key_rows, value_rows, chosen = inputs
    selected_keys = key_rows[chosen]
    selected_values = value_rows[chosen]
    scores = jnp.einsum(
        "alj,axj->alx", query_matrix, selected_keys, preferred_element_type=jnp.float32
    ) * HEAD_DIM ** (-0.5)
    top_score = jnp.max(scores, axis=-1, keepdims=True)
    exponent = jnp.exp(scores - top_score)
    row_total = jnp.sum(exponent, axis=-1, keepdims=True)
    probabilities_reduced = (exponent / row_total).astype(jnp.bfloat16)
    layer_output = jnp.einsum(
        "ivo,ion->ivn", probabilities_reduced, selected_values, preferred_element_type=jnp.float32
    )
    return (layer_output.astype(jnp.bfloat16), (top_score + jnp.log(row_total))[..., 0])


def attend_back(inputs):
    query_matrix, key_rows, value_rows, chosen, log_total, output_gradient = inputs
    selected_keys = key_rows[chosen]
    selected_values = value_rows[chosen]
    scores = jnp.einsum(
        "alj,axj->alx", query_matrix, selected_keys, preferred_element_type=jnp.float32
    ) * HEAD_DIM ** (-0.5)
    probs_full = jnp.exp(scores - log_total[..., None])
    probabilities_reduced = probs_full.astype(jnp.bfloat16)
    grad_probs = jnp.einsum(
        "alj,axj->alx", output_gradient, selected_values, preferred_element_type=jnp.float32
    )
    inner_sum = jnp.sum(probs_full * grad_probs, axis=-1, keepdims=True)
    score_gradient = (probs_full * (grad_probs - inner_sum) * HEAD_DIM ** (-0.5)).astype(
        jnp.bfloat16
    )
    grad_queries = jnp.einsum(
        "ivo,ion->ivn", score_gradient, selected_keys, preferred_element_type=jnp.float32
    )
    grad_key_sel = jnp.einsum(
        "pug,puv->pgv", score_gradient, query_matrix, preferred_element_type=jnp.float32
    )
    grad_value_sel = jnp.einsum(
        "pug,puv->pgv", probabilities_reduced, output_gradient, preferred_element_type=jnp.float32
    )
    grad_keys = jnp.zeros(key_rows.shape, jnp.float32).at[chosen].add(grad_key_sel)
    grad_values = jnp.zeros(value_rows.shape, jnp.float32).at[chosen].add(grad_value_sel)
    return (
        grad_queries.astype(jnp.bfloat16),
        grad_keys.astype(jnp.bfloat16),
        grad_values.astype(jnp.bfloat16),
    )


def body(
    hidden_in,
    w_query,
    b_query,
    w_key,
    w_value,
    b_value,
    w_out,
    b_out,
    gain_one,
    shift_one,
    w_up,
    b_up,
    w_down,
    b_down,
    gain_two,
    shift_two,
    seq_length,
    block_perm,
    cotangent,
):
    block_count = hidden_in.shape[0] // BLOCK
    local_heads = w_query.shape[1] // HEAD_DIM
    per_seq = seq_length[0] // BLOCK
    position = jnp.arange(block_count, dtype=jnp.int32)
    chosen = (position // per_seq * per_seq)[:, None] + block_perm % per_seq
    query_matrix = (
        jnp.dot(hidden_in, w_query, preferred_element_type=jnp.float32) + b_query
    ).astype(jnp.bfloat16)
    key_rows = jnp.dot(hidden_in, w_key, preferred_element_type=jnp.float32).astype(jnp.bfloat16)
    value_rows = (jnp.dot(hidden_in, w_value, preferred_element_type=jnp.float32) + b_value).astype(
        jnp.bfloat16
    )
    head_queries = by_head(query_matrix, block_count, local_heads)
    head_keys = by_head(key_rows, block_count, local_heads)
    head_values = by_head(value_rows, block_count, local_heads)
    head_out, log_total = lax.map(attend_head, (head_queries, head_keys, head_values, chosen.T))
    attended = from_head(head_out)
    mixed_rows = lax.all_to_all(attended, "head", split_axis=0, concat_axis=1, tiled=True)
    rows_own = hidden_in.shape[0] // lax.axis_size("head")
    residual = lax.dynamic_slice_in_dim(
        hidden_in, lax.axis_index("head") * rows_own, rows_own, 0
    ).astype(jnp.float32)
    branch = jnp.dot(mixed_rows, w_out, preferred_element_type=jnp.float32) + b_out
    normed_one_out, normed_one, inverse_one = norm_forward(residual + branch, gain_one, shift_one)
    up_in = normed_one_out.astype(jnp.bfloat16)
    pre_act = jnp.dot(up_in, w_up, preferred_element_type=jnp.float32) + b_up
    gelu_value, gelu_pull = jax.vjp(partial(jax.nn.gelu, approximate=False), pre_act)
    acted_low = gelu_value.astype(jnp.bfloat16)
    ffn_out = jnp.dot(acted_low, w_down, preferred_element_type=jnp.float32) + b_down
    block_value, normed_two, inverse_two = norm_forward(
        normed_one_out + ffn_out, gain_two, shift_two
    )
    block_out = block_value.astype(jnp.bfloat16)
    grad_second, grad_gain_two, grad_shift_two = norm_backward(
        cotangent.astype(jnp.float32), normed_two, inverse_two, gain_two
    )
    grad_ffn = grad_second.astype(jnp.bfloat16)
    grad_down = jnp.einsum("tf,td->fd", acted_low, grad_ffn, preferred_element_type=jnp.float32)
    grad_down_bias = jnp.sum(grad_ffn.astype(jnp.float32), axis=0)
    grad_acted = jnp.einsum("td,fd->tf", grad_ffn, w_down, preferred_element_type=jnp.float32)
    grad_pre = gelu_pull(grad_acted)[0].astype(jnp.bfloat16)
    grad_up = jnp.einsum("td,tf->df", up_in, grad_pre, preferred_element_type=jnp.float32)
    grad_up_bias = jnp.sum(grad_pre.astype(jnp.float32), axis=0)
    grad_normed = (
        jnp.einsum("tf,df->td", grad_pre, w_up, preferred_element_type=jnp.float32) + grad_second
    )
    grad_first, grad_gain_one, grad_shift_one = norm_backward(
        grad_normed, normed_one, inverse_one, gain_one
    )
    grad_branch = grad_first.astype(jnp.bfloat16)
    grad_out = jnp.einsum("tc,td->cd", mixed_rows, grad_branch, preferred_element_type=jnp.float32)
    grad_out_bias = jnp.sum(grad_branch.astype(jnp.float32), axis=0)
    grad_mixed = jnp.einsum(
        "td,cd->tc", grad_branch, w_out, preferred_element_type=jnp.float32
    ).astype(jnp.bfloat16)
    (
        grad_out,
        grad_up,
        grad_down,
        grad_out_bias,
        grad_up_bias,
        grad_down_bias,
        grad_gain_one,
        grad_shift_one,
        grad_gain_two,
        grad_shift_two,
    ) = (
        lax.psum_scatter(grad_out, "head", scatter_dimension=1, tiled=True),
        lax.psum_scatter(grad_up, "head", scatter_dimension=1, tiled=True),
        lax.psum_scatter(grad_down, "head", scatter_dimension=1, tiled=True),
        lax.psum_scatter(grad_out_bias, "head", scatter_dimension=0, tiled=True),
        lax.psum_scatter(grad_up_bias, "head", scatter_dimension=0, tiled=True),
        lax.psum_scatter(grad_down_bias, "head", scatter_dimension=0, tiled=True),
        lax.psum_scatter(grad_gain_one, "head", scatter_dimension=0, tiled=True),
        lax.psum_scatter(grad_shift_one, "head", scatter_dimension=0, tiled=True),
        lax.psum_scatter(grad_gain_two, "head", scatter_dimension=0, tiled=True),
        lax.psum_scatter(grad_shift_two, "head", scatter_dimension=0, tiled=True),
    )
    grad_heads = lax.all_to_all(grad_mixed, "head", split_axis=1, concat_axis=0, tiled=True)
    grad_head_out = by_head(grad_heads, block_count, local_heads)
    head_grad_q, head_grad_k, head_grad_v = lax.map(
        attend_back, (head_queries, head_keys, head_values, chosen.T, log_total, grad_head_out)
    )
    grad_queries = from_head(head_grad_q)
    grad_keys = from_head(head_grad_k)
    grad_values = from_head(head_grad_v)
    grad_query = jnp.einsum(
        "tc,td->cd", hidden_in, grad_queries, preferred_element_type=jnp.float32
    )
    grad_query_bias = jnp.sum(grad_queries.astype(jnp.float32), axis=0)
    grad_key = jnp.einsum("tc,td->cd", hidden_in, grad_keys, preferred_element_type=jnp.float32)
    grad_value = jnp.einsum("tc,td->cd", hidden_in, grad_values, preferred_element_type=jnp.float32)
    grad_value_bias = jnp.sum(grad_values.astype(jnp.float32), axis=0)
    partial_input = jnp.einsum(
        "td,cd->tc", grad_queries, w_query, preferred_element_type=jnp.float32
    )
    partial_input = partial_input + jnp.einsum(
        "td,cd->tc", grad_keys, w_key, preferred_element_type=jnp.float32
    )
    partial_input = partial_input + jnp.einsum(
        "td,cd->tc", grad_values, w_value, preferred_element_type=jnp.float32
    )
    input_grad = (
        lax.psum_scatter(partial_input, "head", scatter_dimension=0, tiled=True) + grad_first
    )
    (
        grad_query,
        grad_query_bias,
        grad_key,
        grad_value,
        grad_value_bias,
        grad_out,
        grad_up,
        grad_down,
        grad_out_bias,
        grad_up_bias,
        grad_down_bias,
        grad_gain_one,
        grad_shift_one,
        grad_gain_two,
        grad_shift_two,
    ) = lax.psum(
        (
            grad_query,
            grad_query_bias,
            grad_key,
            grad_value,
            grad_value_bias,
            grad_out,
            grad_up,
            grad_down,
            grad_out_bias,
            grad_up_bias,
            grad_down_bias,
            grad_gain_one,
            grad_shift_one,
            grad_gain_two,
            grad_shift_two,
        ),
        "dp",
    )
    return (
        block_out,
        input_grad,
        grad_query,
        grad_query_bias,
        grad_key,
        grad_value,
        grad_value_bias,
        grad_out,
        grad_out_bias,
        grad_gain_one,
        grad_shift_one,
        grad_up,
        grad_up_bias,
        grad_down,
        grad_down_bias,
        grad_gain_two,
        grad_shift_two,
    )


def solution(mesh):
    placed = (
        P("dp", None),
        P(None, "head"),
        P("head"),
        P(None, "head"),
        P(None, "head"),
        P("head"),
        P(),
        P(),
        P(),
        P(),
        P(),
        P(),
        P(),
        P(),
        P(),
        P(),
        P("dp"),
        P("dp", "head"),
        P(("dp", "head"), None),
    )
    return jax.shard_map(
        body,
        mesh=mesh,
        in_specs=placed,
        out_specs=(
            P(("dp", "head"), None),
            P(("dp", "head"), None),
            P(None, "head"),
            P("head"),
            P(None, "head"),
            P(None, "head"),
            P("head"),
            P(None, "head"),
            P("head"),
            P("head"),
            P("head"),
            P(None, "head"),
            P("head"),
            P(None, "head"),
            P("head"),
            P("head"),
            P("head"),
        ),
        check_vma=False,
    )
```

profile of v0, /device:TPU:0, one launch (start us, length us, event | category | flops | bytes accessed | tf_op | source)
XLA Modules:
  0.0 1120.7 jit_solution(13168503347304208831)
XLA Ops:
  8.9 6.6 add_convert_fusion.2
  26.7 6.4 add_convert_fusion.3
  44.0 6.4 convolution_convert_fusion
  63.0 82.7 %while.26 = (s32[]{:T(128)}, bf16[6,6,512,64]{2,3,1,0:T(8,128)(2,1)}, f32[6,6,512]{2,1,0:T(8,128)}, bf16[6,6,512,64]{2,3,1,0:T(8,128)(2,1)}, bf16[6,6,512,64]{2,...) while((s32[]{:T(128)}, bf16[6,6,512,64]{2,3,1,0:T(8,128)(2,1)}, ...), condition=%wide.region_3.4_spmd, body=%wide.region_0.3_spmd.sunk | while | flops 417003520 | bytes 48867056 | solution.py:129
  72.3 4.9 fusion.163
  86.0 4.9 fusion.163
  99.7 4.9 fusion.163
  113.4 4.9 fusion.163
  127.1 4.9 fusion.163
  140.8 4.9 fusion.163
  151.1 5.8 all_to_all.26
  158.6 4.9 all-to-all-start
  172.4 20.3 %all-to-all-done = bf16[2,1536,384]{1,2,0:T(8,128)(2,1)} async-done(((bf16[2,1536,384]{1,2,0:T(8,128)(2,1)}), bf16[2,1536,384]{1,2,0:T(8,128)(2,1)}, u32[]{:S(2)}, u32[]{:S(2)}) %all-to-all-start) | async-done | bytes 2359328 | tf_op jit(solution)/shard_map/all_to_all | solution.py:131
  198.4 49.7 %multiply_convert_fusion.1 = (bf16[1536,3072]{1,0:T(8,128)(2,1)}, f32[1536,3072]{1,0:T(8,128)}, f32[1536,3072]{1,0:T(8,128)}) fusion(f32[3072]{0:T(1024)S(1)} %copy-done.32, bf16[768,3072]{1,0:T(8,128)(2,1)} %param.33, bf16[1536,768]{0,1:T(8,128)(2,1)S(1)} %fusion.91.clone.4), kind=kOutput, calls=%fused_computation.78 | convolution fusion | flops 7559184384 | bytes 54276096 | tf_op jit(solution)/shard_map/dot_general | solution.py:139
  248.1 14.1 %fusion.95 = (f32[1536]{0:T(1024)S(1)}, f32[1536,768]{0,1:T(8,128)}) fusion(f32[768]{0:T(1024)S(1)} %copy-done.34, bf16[1536,3072]{1,0:T(8,128)(2,1)} %get-tuple-element.267, bf16[3072,768]{1,0:T(8,128)(2,1)} %param.35, f32[768]{0:T(1024)S(1)} %copy-done.30, f32[768]{0:T(1024)S(1)} %copy-done.24, f32[1536]{0:T(1024)S(1)} %add_rsqrt_fusion.1, ...), kind=kOutput, calls=%fused_computation.149 | convolution fusion | flops 7256013312 | bytes 23620608 | tf_op jit(solution)/shard_map/dot_general | solution.py:142
  273.5 27.1 %convert_reduce_fusion = (f32[3072]{0:T(1024)}, bf16[1536,3072]{1,0:T(8,128)(2,1)}) fusion(f32[1536,3072]{1,0:T(8,128)} %get-tuple-element.268, bf16[1536,768]{0,1:T(8,128)(2,1)} %get-tuple-element.264, bf16[3072,768]{1,0:T(8,128)(2,1)} %param.35, f32[1536,3072]{1,0:T(8,128)} %get-tuple-element.278, f32[3072]{0:T(1024)S(1)} %copy-done.32), kind=kOutput, calls=%fused_computation.76 | convolution fusion | flops 7327970304 | bytes 54288384 | tf_op jit(solution)/shard_map/td,fd->tf/dot_general | solution.py:153
  300.6 15.7 %multiply_reduce_fusion.2 = (f32[768]{0:T(1024)}, f32[1536]{0:T(1024)S(1)}, f32[1536]{0:T(1024)S(1)}, f32[768]{0:T(1024)}, f32[1536,768]{0,1:T(8,128)S(1)}) fusion(f32[1536,768]{0,1:T(8,128)S(1)} %get-tuple-element.277, f32[1536]{0:T(1024)S(1)} %add_rsqrt_fusion.1, f32[1536]{0:T(1024)S(1)} %broadcast_multiply_fusion.5, f32[768]{0:T(1024)S(1)} %copy-done.24, ...), kind=kOutput, calls=%fused_computation.104 | convolution fusion | flops 7268985856 | bytes 30732288 | tf_op jit(solution)/shard_map/tf,df->td/dot_general | solution.py:158
  320.7 5.1 fusion.85
  325.8 13.8 %fusion.88 = f32[768,3072]{1,0:T(8,128)} fusion(bf16[1536,3072]{1,0:T(8,128)(2,1)} %get-tuple-element.283, f32[1536,768]{0,1:T(8,128)} %copy-done.3, f32[768]{0:T(1024)S(1)} %copy-done.30, f32[768]{0:T(1024)S(1)} %copy-done.24, f32[1536]{0:T(1024)S(1)} %add_rsqrt_fusion.1, f32[1536]{0:T(1024)S(1)} %broadcast_multiply_fusion.5), kind=kOutput, calls=%fused_computation.146 | convolution fusion | flops 7253655552 | bytes 23611392 | tf_op jit(solution)/shard_map/td,tf->df/dot_general | solution.py:155
  341.3 12.4 %fusion.96 = f32[3072,768]{1,0:T(8,128)} fusion(bf16[1536,3072]{1,0:T(8,128)(2,1)} %get-tuple-element.267, bf16[1536,768]{0,1:T(8,128)(2,1)S(1)} %copy-done.14), kind=kOutput, calls=%fused_computation.150 | convolution fusion | flops 7247757312 | bytes 21233664 | tf_op jit(solution)/shard_map/tf,td->fd/dot_general | solution.py:151
  358.2 48.5 %all_to_all.35 = bf16[1536,2,384]{0,2,1:T(8,128)(2,1)S(1)} all-to-all(bf16[1536,2,384]{0,2,1:T(8,128)(2,1)S(1)} %bitcast.212), channel_id=1, replica_groups=mesh['dp'=16,'head'=2] {'head'}, dimensions={1} | all-to-all | bytes 4718592 | tf_op jit(solution)/shard_map/all_to_all | solution.py:192
  421.4 275.2 %while.27 = (s32[]{:T(128)}, bf16[6,6,512,64]{2,3,1,0:T(8,128)(2,1)}, bf16[6,6,512,64]{2,3,1,0:T(8,128)(2,1)}, bf16[6,6,512,64]{2,3,1,0:T(8,128)(2,1)}, bf16[6,6...) while((s32[]{:T(128)}, ...), condition=%wide.region_16.17_spmd, body=%wide.region_12.16_spmd.sunk | while | flops 1040654336 | bytes 87403984 | solution.py:194
  429.9 4.9 fusion.176
  435.5 11.7 %fusion.179 = f32[6,512,64]{1,2,0:T(8,128)S(1)} fusion(f32[6,512,512]{1,2,0:T(8,128)} %fusion.175, f32[6,512,512]{1,2,0:T(8,128)} %fusion.176, f32[6,512]{1,0:T(8,128)S(1)} %dynamic-slice_bitcast_fusion.12, bf16[6,6,512,64]{2,3,1,0:T(8,128)(2,1)} %get-tuple-element.454, s32[]{:T(128)} %get-tuple-element.438), kind=kOutput, calls=%fused_computation.33.clone.1 | convolution fusion | flops 215485952 | bytes 26378752 | tf_op jit(solution)/shard_map/while/body/eval_jaxpr/pug,puv->pgv/dot_general | solution.py:78
  454.8 12.5 %fusion.177 = bf16[6,6,512,64]{2,3,1,0:T(8,128)(2,1)} fusion(bf16[6,6,512,64]{2,3,1,0:T(8,128)(2,1)} %get-tuple-element.439, s32[]{:T(128)} %get-tuple-element.438, bf16[6,512,64]{1,2,0:T(8,128)(2,1)} %copy-done.2, f32[6,512,512]{1,2,0:T(8,128)} %fusion.175, f32[6,512,512]{1,2,0:T(8,128)} %fusion.176, f32[6,512]{1,0:T(8,128)S(1)} %dynamic-slice_bitcast_fusion.12), kind=kOutput, calls=%fused_computation.44.clone.1 | convolution fusion | flops 215682560 | bytes 25985536 | tf_op jit(solution)/shard_map/while/body/eval_jaxpr/ivo,ion->ivn/dot_general | solution.py:75
  481.5 11.5 %fusion.179 = f32[6,512,64]{1,2,0:T(8,128)S(1)} fusion(f32[6,512,512]{1,2,0:T(8,128)} %fusion.175, f32[6,512,512]{1,2,0:T(8,128)} %fusion.176, f32[6,512]{1,0:T(8,128)S(1)} %dynamic-slice_bitcast_fusion.12, bf16[6,6,512,64]{2,3,1,0:T(8,128)(2,1)} %get-tuple-element.454, s32[]{:T(128)} %get-tuple-element.438), kind=kOutput, calls=%fused_computation.33.clone.1 | convolution fusion | flops 215485952 | bytes 26378752 | tf_op jit(solution)/shard_map/while/body/eval_jaxpr/pug,puv->pgv/dot_general | solution.py:78
  500.6 12.2 %fusion.177 = bf16[6,6,512,64]{2,3,1,0:T(8,128)(2,1)} fusion(bf16[6,6,512,64]{2,3,1,0:T(8,128)(2,1)} %get-tuple-element.439, s32[]{:T(128)} %get-tuple-element.438, bf16[6,512,64]{1,2,0:T(8,128)(2,1)} %copy-done.2, f32[6,512,512]{1,2,0:T(8,128)} %fusion.175, f32[6,512,512]{1,2,0:T(8,128)} %fusion.176, f32[6,512]{1,0:T(8,128)S(1)} %dynamic-slice_bitcast_fusion.12), kind=kOutput, calls=%fused_computation.44.clone.1 | convolution fusion | flops 215682560 | bytes 25985536 | tf_op jit(solution)/shard_map/while/body/eval_jaxpr/ivo,ion->ivn/dot_general | solution.py:75
  521.4 4.9 fusion.176
  527.1 12.0 %fusion.179 = f32[6,512,64]{1,2,0:T(8,128)S(1)} fusion(f32[6,512,512]{1,2,0:T(8,128)} %fusion.175, f32[6,512,512]{1,2,0:T(8,128)} %fusion.176, f32[6,512]{1,0:T(8,128)S(1)} %dynamic-slice_bitcast_fusion.12, bf16[6,6,512,64]{2,3,1,0:T(8,128)(2,1)} %get-tuple-element.454, s32[]{:T(128)} %get-tuple-element.438), kind=kOutput, calls=%fused_computation.33.clone.1 | convolution fusion | flops 215485952 | bytes 26378752 | tf_op jit(solution)/shard_map/while/body/eval_jaxpr/pug,puv->pgv/dot_general | solution.py:78
  546.9 12.7 %fusion.177 = bf16[6,6,512,64]{2,3,1,0:T(8,128)(2,1)} fusion(bf16[6,6,512,64]{2,3,1,0:T(8,128)(2,1)} %get-tuple-element.439, s32[]{:T(128)} %get-tuple-element.438, bf16[6,512,64]{1,2,0:T(8,128)(2,1)} %copy-done.2, f32[6,512,512]{1,2,0:T(8,128)} %fusion.175, f32[6,512,512]{1,2,0:T(8,128)} %fusion.176, f32[6,512]{1,0:T(8,128)S(1)} %dynamic-slice_bitcast_fusion.12), kind=kOutput, calls=%fused_computation.44.clone.1 | convolution fusion | flops 215682560 | bytes 25985536 | tf_op jit(solution)/shard_map/while/body/eval_jaxpr/ivo,ion->ivn/dot_general | solution.py:75
  568.2 4.9 fusion.176
  573.8 11.7 %fusion.179 = f32[6,512,64]{1,2,0:T(8,128)S(1)} fusion(f32[6,512,512]{1,2,0:T(8,128)} %fusion.175, f32[6,512,512]{1,2,0:T(8,128)} %fusion.176, f32[6,512]{1,0:T(8,128)S(1)} %dynamic-slice_bitcast_fusion.12, bf16[6,6,512,64]{2,3,1,0:T(8,128)(2,1)} %get-tuple-element.454, s32[]{:T(128)} %get-tuple-element.438), kind=kOutput, calls=%fused_computation.33.clone.1 | convolution fusion | flops 215485952 | bytes 26378752 | tf_op jit(solution)/shard_map/while/body/eval_jaxpr/pug,puv->pgv/dot_general | solution.py:78
  593.1 12.3 %fusion.177 = bf16[6,6,512,64]{2,3,1,0:T(8,128)(2,1)} fusion(bf16[6,6,512,64]{2,3,1,0:T(8,128)(2,1)} %get-tuple-element.439, s32[]{:T(128)} %get-tuple-element.438, bf16[6,512,64]{1,2,0:T(8,128)(2,1)} %copy-done.2, f32[6,512,512]{1,2,0:T(8,128)} %fusion.175, f32[6,512,512]{1,2,0:T(8,128)} %fusion.176, f32[6,512]{1,0:T(8,128)S(1)} %dynamic-slice_bitcast_fusion.12), kind=kOutput, calls=%fused_computation.44.clone.1 | convolution fusion | flops 215682560 | bytes 25985536 | tf_op jit(solution)/shard_map/while/body/eval_jaxpr/ivo,ion->ivn/dot_general | solution.py:75
  619.6 11.4 %fusion.179 = f32[6,512,64]{1,2,0:T(8,128)S(1)} fusion(f32[6,512,512]{1,2,0:T(8,128)} %fusion.175, f32[6,512,512]{1,2,0:T(8,128)} %fusion.176, f32[6,512]{1,0:T(8,128)S(1)} %dynamic-slice_bitcast_fusion.12, bf16[6,6,512,64]{2,3,1,0:T(8,128)(2,1)} %get-tuple-element.454, s32[]{:T(128)} %get-tuple-element.438), kind=kOutput, calls=%fused_computation.33.clone.1 | convolution fusion | flops 215485952 | bytes 26378752 | tf_op jit(solution)/shard_map/while/body/eval_jaxpr/pug,puv->pgv/dot_general | solution.py:78
  638.6 12.2 %fusion.177 = bf16[6,6,512,64]{2,3,1,0:T(8,128)(2,1)} fusion(bf16[6,6,512,64]{2,3,1,0:T(8,128)(2,1)} %get-tuple-element.439, s32[]{:T(128)} %get-tuple-element.438, bf16[6,512,64]{1,2,0:T(8,128)(2,1)} %copy-done.2, f32[6,512,512]{1,2,0:T(8,128)} %fusion.175, f32[6,512,512]{1,2,0:T(8,128)} %fusion.176, f32[6,512]{1,0:T(8,128)S(1)} %dynamic-slice_bitcast_fusion.12), kind=kOutput, calls=%fused_computation.44.clone.1 | convolution fusion | flops 215682560 | bytes 25985536 | tf_op jit(solution)/shard_map/while/body/eval_jaxpr/ivo,ion->ivn/dot_general | solution.py:75
  659.3 4.9 fusion.176
  664.9 11.4 %fusion.179 = f32[6,512,64]{1,2,0:T(8,128)S(1)} fusion(f32[6,512,512]{1,2,0:T(8,128)} %fusion.175, f32[6,512,512]{1,2,0:T(8,128)} %fusion.176, f32[6,512]{1,0:T(8,128)S(1)} %dynamic-slice_bitcast_fusion.12, bf16[6,6,512,64]{2,3,1,0:T(8,128)(2,1)} %get-tuple-element.454, s32[]{:T(128)} %get-tuple-element.438), kind=kOutput, calls=%fused_computation.33.clone.1 | convolution fusion | flops 215485952 | bytes 26378752 | tf_op jit(solution)/shard_map/while/body/eval_jaxpr/pug,puv->pgv/dot_general | solution.py:78
  683.9 12.2 %fusion.177 = bf16[6,6,512,64]{2,3,1,0:T(8,128)(2,1)} fusion(bf16[6,6,512,64]{2,3,1,0:T(8,128)(2,1)} %get-tuple-element.439, s32[]{:T(128)} %get-tuple-element.438, bf16[6,512,64]{1,2,0:T(8,128)(2,1)} %copy-done.2, f32[6,512,512]{1,2,0:T(8,128)} %fusion.175, f32[6,512,512]{1,2,0:T(8,128)} %fusion.176, f32[6,512]{1,0:T(8,128)S(1)} %dynamic-slice_bitcast_fusion.12), kind=kOutput, calls=%fused_computation.44.clone.1 | convolution fusion | flops 215682560 | bytes 25985536 | tf_op jit(solution)/shard_map/while/body/eval_jaxpr/ivo,ion->ivn/dot_general | solution.py:75
  713.0 6.9 add_add_fusion
  719.9 6.2 convolution_bitcast_fusion
  726.1 5.8 convolution_bitcast_fusion.1
  737.6 9.9 all-reduce.9
  762.7 57.9 %all-reduce.7 = (f32[384]{0:T(512)}, f32[384]{0:T(512)}, f32[384]{0:T(512)}, f32[384]{0:T(512)}, f32[384]{0:T(512)}, /*index=5*/f32[1536]{0:T(1024)}, f32[384]{0:T(512)}, f32[384]{0:T(512)}, f32[384]{0:T(512)}) all-reduce(f32[384]{0:T(512)S(1)} %reduce_sum.184, f32[384]{0:T(512)S(1)} %reduce_sum.186, ...), channel_id=1, replica_groups=mesh['dp'=16,'head'=2] {'dp'}, use_global_device_ids=true, to_apply=%region_20.21 | all-reduce | flops 4608 | bytes 36864 | tf_op jit(solution)/shard_map/psum | solution.py:235
  820.6 11.2 reduce-scatter.5.cloned.1.call-done
  831.7 6.9 add.239
  838.7 6.0 copy.118
  844.7 253.6 %all-reduce.12.cloned.1.call-done = (f32[768,384]{0,1:T(8,128)}, f32[768,384]{0,1:T(8,128)}, f32[768,384]{0,1:T(8,128)}, f32[768,384]{1,0:T(8,128)}, f32[768,1536]{1,0:T(8,128)}, /*index=5*/f32[3072,384]{1,0:T(8,128)}) async-done(((f32[768,384]{0,1:T(8,128)}, f32[768,384]{0,1:T(8,128)}, f32[768,384]{0,1:T(8,128)}, f32[768,384]{1,0:T(8,128)}, f32[768,1536]{1,0:T(8,128)}, /*index=5*/f32[3072,384]{1,0:T(8,128)}), ...) | async-done | bytes 14155792 | tf_op jit(solution)/shard_map/psum | solution.py:235
  1106.2 5.5 copy.173
  (326 shorter events, 302.7 us)
Async XLA Ops:
  7.2 185.5 %copy-start = (bf16[768,768]{1,0:T(8,128)(2,1)S(1)}, bf16[768,768]{1,0:T(8,128)(2,1)}, u32[]{:S(2)}) copy-start(bf16[768,768]{1,0:T(8,128)(2,1)} %param.29) | copy-start | bytes 3538948
  18.6 8.1 copy-start.35
  22.4 4.3 copy-start.17
  39.8 4.2 copy-start.19
  67.4 2.7 copy-start.1
  81.1 2.7 copy-start.1
  94.8 2.7 copy-start.1
  108.5 2.7 copy-start.1
  122.2 2.7 copy-start.1
  135.9 2.7 copy-start.1
  158.6 34.1 %all-to-all-start = ((bf16[2,1536,384]{1,2,0:T(8,128)(2,1)}), bf16[2,1536,384]{1,2,0:T(8,128)(2,1)}, u32[]{:S(2)}, u32[]{:S(2)}) async-start(bf16[2,1536,384]{1,2,0:T(8,128)(2,1)} %copy.102), calls=%async_computation | async-start | bytes 4718592 | tf_op jit(solution)/shard_map/all_to_all | solution.py:131
  163.5 571.4 %reduce-scatter.7.cloned.1.call-start = ((), (), s32[]{:S(2)}) async-start(), calls=%async_computation.7 | async-start | bytes 3538944 | tf_op jit(solution)/shard_map/reduce_scatter | solution.py:181
  165.4 27.3 %copy-start.33 = (f32[768]{0:T(1024)S(1)}, f32[768]{0:T(1024)}, u32[]{:S(2)}) copy-start(f32[768]{0:T(1024)} %param.30) | copy-start | bytes 9220
  168.0 24.7 %copy-start.13 = (bf16[1536,768]{0,1:T(8,128)(2,1)S(1)}, bf16[1536,768]{0,1:T(8,128)(2,1)}, u32[]{:S(2)}) copy-start(bf16[1536,768]{0,1:T(8,128)(2,1)} %copy.131) | copy-start | bytes 7077892
  196.9 119.5 %copy-start.3 = (f32[1536,768]{0,1:T(8,128)}, f32[1536,768]{0,1:T(8,128)S(1)}, u32[]{:S(2)}) copy-start(f32[1536,768]{0,1:T(8,128)S(1)} %get-tuple-element.277) | copy-start | bytes 14155780
  198.4 49.7 %copy-start.34 = (f32[768]{0:T(1024)S(1)}, f32[768]{0:T(1024)}, u32[]{:S(2)}) copy-start(f32[768]{0:T(1024)} %param.36) | copy-start | bytes 9220
  248.1 17.2 %copy-start.6 = (bf16[1536,768]{0,1:T(8,128)(2,1)S(1)}, bf16[1536,768]{0,1:T(8,128)(2,1)}, u32[]{:S(2)}) copy-start(bf16[1536,768]{0,1:T(8,128)(2,1)} %copy.104) | copy-start | bytes 7077892
  262.2 3.8 copy-start.4
  262.2 3.8 copy-start.23
  265.2 3.8 copy-start.29
  325.8 409.2 %reduce-scatter.9.cloned.1.call-start = ((), (), s32[]{:S(2)}) async-start(), calls=%async_computation.8 | async-start | bytes 14155776 | tf_op jit(solution)/shard_map/reduce_scatter | solution.py:182
  339.7 395.3 %reduce-scatter.11.cloned.1.call-start = ((), (), s32[]{:S(2)}) async-start(), calls=%async_computation.9 | async-start | bytes 14155776 | tf_op jit(solution)/shard_map/reduce_scatter | solution.py:183
  353.7 478.0 %reduce-scatter.5.cloned.1.call-start = ((), (), s32[]{:S(2)}) async-start(), calls=%async_computation.6 | async-start | bytes 14155776 | tf_op jit(solution)/shard_map/reduce_scatter | solution.py:217
  422.0 25.3 %copy-start.22 = (s32[6]{0:T(128)}, s32[6]{0:T(128)S(1)}, u32[]{:S(2)}) copy-start(s32[6]{0:T(128)S(1)} %fusion.174) | copy-start | bytes 76 | tf_op jit(solution)/shard_map/while
  429.9 5.6 copy-start.2
  468.0 25.1 %copy-start.22 = (s32[6]{0:T(128)}, s32[6]{0:T(128)S(1)}, u32[]{:S(2)}) copy-start(s32[6]{0:T(128)S(1)} %fusion.174) | copy-start | bytes 76 | tf_op jit(solution)/shard_map/while
  475.9 5.6 copy-start.2
  513.5 25.6 %copy-start.22 = (s32[6]{0:T(128)}, s32[6]{0:T(128)S(1)}, u32[]{:S(2)}) copy-start(s32[6]{0:T(128)S(1)} %fusion.174) | copy-start | bytes 76 | tf_op jit(solution)/shard_map/while
  521.4 5.7 copy-start.2
  560.3 25.3 %copy-start.22 = (s32[6]{0:T(128)}, s32[6]{0:T(128)S(1)}, u32[]{:S(2)}) copy-start(s32[6]{0:T(128)S(1)} %fusion.174) | copy-start | bytes 76 | tf_op jit(solution)/shard_map/while
  568.2 5.6 copy-start.2
  606.1 24.9 %copy-start.22 = (s32[6]{0:T(128)}, s32[6]{0:T(128)S(1)}, u32[]{:S(2)}) copy-start(s32[6]{0:T(128)S(1)} %fusion.174) | copy-start | bytes 76 | tf_op jit(solution)/shard_map/while
  614.0 5.6 copy-start.2
  651.5 24.9 %copy-start.22 = (s32[6]{0:T(128)}, s32[6]{0:T(128)S(1)}, u32[]{:S(2)}) copy-start(s32[6]{0:T(128)S(1)} %fusion.174) | copy-start | bytes 76 | tf_op jit(solution)/shard_map/while
  659.3 5.6 copy-start.2
  696.5 5.8 copy-start.8
  704.9 5.3 copy-start.9
  707.5 2.6 copy-start.11
  710.2 2.8 copy-start.21
  719.8 378.5 %all-reduce.12.cloned.1.call-start = ((), (), s32[]{:S(2)}) async-start(), calls=%async_computation.10 | async-start | bytes 28311552 | tf_op jit(solution)/shard_map/psum | solution.py:235
  719.9 6.2 copy-start.10
  719.9 12.0 %slice-start.2 = ((s8[4718592]{0:T(1024)(128)(4,1)}), s8[4194304]{0:T(1024)(128)(4,1)S(1)}, s32[]{:S(2)}) async-start(s8[4718592]{0:T(1024)(128)(4,1)} %bitcast.213), calls=%async_computation.13 | async-start | bytes 8388608
  726.1 5.8 copy-start.12
  726.1 5.8 slice-start.3
  1098.4 5.5 copy-start.16
  1098.4 6.8 copy-start.15
  1105.2 6.5 slice-start
  1106.2 5.5 slice-start.1
  (13 other events, 25.1 us)
Sparse Core Ops, SparseCore 0:
  325.9 35.2 reduce-scatter.6
  363.6 127.2 reduce-scatter.8
  493.3 110.7 reduce-scatter.10
  720.0 111.7 reduce-scatter.4
  838.1 260.1 all-reduce.11
where the time goes:
time: 1130 us; the launch traced here: 1120 us
  matrix products  460 us (41%)
  waiting for transfers between devices  285 us (25%)
  local copies, waits for them, and re-layouts  178 us (16%)
  blocking collectives  116 us (10%)
  other arithmetic  58.3 us (5%)
  between operations  16.5 us (1%)
    psum x1, waiting for transfers between devices, body(): lax.psum((grad_query, grad_query_bias, grad_key, grad_value, grad_value_b...  254 us
    dot_general x6, matrix products, attend_back(): jnp.einsum('ivo,ion->ivn', score_gradient, selected_keys, preferred_eleme...  74.2 us
    dot_general x6, matrix products, attend_back(): jnp.einsum('pug,puv->pgv', score_gradient, query_matrix, preferred_elemen...  69.6 us
    psum x1, blocking collectives, body(): lax.psum((grad_query, grad_query_bias, grad_key, grad_value, grad_value_b...  57.9 us
    unnamed x96, local copies, waits for them, and re-layouts  53.2 us
    dot_general x1, matrix products, body(): pre_act = jnp.dot(up_in, w_up, preferred_element_type=jnp.float32) + b_up  49.7 us
    all_to_all x1, blocking collectives, body(): lax.all_to_all(grad_mixed, 'head', split_axis=1, concat_axis=0, tiled=True)  48.5 us
    dot_general x6, matrix products, attend_head(): jnp.einsum('ivo,ion->ivn', probabilities_reduced, selected_values, prefer...  29.6 us
  transfers between devices with their start and end apart: 6, of which 3 were waited for; matrix products, arithmetic and copies ran while one was open for 35% of the time, Pallas kernels for 0%

commit v1 on v0

v1 whole, which is shorter than its diff:
```python
import functools
import math

import jax
import jax.numpy as jnp
from jax import lax
from jax.experimental import pallas as pl
from jax.experimental.pallas import tpu as pltpu
from jax.sharding import PartitionSpec as P

HEAD_DIM = 64
BLOCK = 512
PAIR = 2 * HEAD_DIM
EPS = 1e-5
LOG2E = math.log2(math.e)
EXP_SCALE = LOG2E / math.sqrt(HEAD_DIM)
SCALE = 1.0 / math.sqrt(HEAD_DIM)
VMEM_LIMIT = 60 * 1024 * 1024
bf16, f32 = jnp.bfloat16, jnp.float32
NT = (((1,), (1,)), ((), ()))
TN = (((0,), (0,)), ((), ()))


def dot(left, right, dims=None):
    if dims is None:
        return jnp.dot(left, right, preferred_element_type=f32)
    return lax.dot_general(left, right, dims, preferred_element_type=f32)


def params():
    return pltpu.CompilerParams(vmem_limit_bytes=VMEM_LIMIT)


def cost(flops, moved, transcendentals=0):
    return pl.CostEstimate(
        flops=int(flops), bytes_accessed=int(moved), transcendentals=int(transcendentals)
    )


def whole(shape):
    return pl.BlockSpec(shape, lambda *_: (0,) * len(shape), pipeline_mode=pl.Buffered(1))


def colsum(values):
    return jnp.sum(values, axis=0, keepdims=True)


def attend_steps(
    own, heads, info, x_ref, weight, bq_ref, bv_ref, att_ref, qaug_ref, k_ref, v_ref, q_scr
):
    step = pl.program_id(0)

    @pl.when(step <= own)
    def _():
        x = x_ref[...]
        k_ref[step] = dot(x, weight(1)).astype(bf16)
        v_ref[step] = (dot(x, weight(2)) + bv_ref[...]).astype(bf16)

        @pl.when(step < own)
        def _():
            q_scr[step] = (dot(x, weight(0)) + bq_ref[...]).astype(bf16)

    @pl.when(step > own)
    def _():
        i = step - own - 1
        lane = lax.broadcasted_iota(jnp.int32, (BLOCK, PAIR), 1)
        low = lane < HEAD_DIM
        for pair in range(heads // 2):
            cols = slice(pair * PAIR, pair * PAIR + PAIR)
            q = q_scr[i, :, cols]
            outs = []
            for a in range(2):
                c = info[own + 1 + i * heads + 2 * pair + a]
                mine = low if a == 0 else jnp.logical_not(low)
                base = HEAD_DIM if a == 0 else 0
                k = k_ref[c, :, cols]
                v = v_ref[c, :, cols]
                s = dot(jnp.where(mine, q, jnp.zeros_like(q)), k, NT)
                m = jnp.max(s, axis=1, keepdims=True)
                p = jnp.exp2((s - m) * EXP_SCALE).astype(bf16)
                o = dot(p, jnp.where(mine, v, jnp.ones_like(v)))
                total = m + jnp.log2(o) * (1.0 / EXP_SCALE)
                hi = total.astype(bf16).astype(f32)
                rest = total - hi
                mid = rest.astype(bf16).astype(f32)
                aug = jnp.where(
                    lane == base,
                    hi,
                    jnp.where(lane == base + 1, mid, jnp.where(lane == base + 2, rest - mid, 0.0)),
                )
                qaug_ref[i, 2 * pair + a] = jnp.where(mine, q, aug.astype(bf16))
                outs.append(o / pltpu.roll(o, HEAD_DIM, 1))
            att_ref[:, cols] = jnp.where(low, outs[0], outs[1]).astype(bf16)


def attend_own_kernel(own, heads, info, x, wq, wk, wv, bq, bv, att, qaug, k, v, q_scr):
    refs = (wq, wk, wv)
    attend_steps(
        own, heads, info, x, lambda n: refs[n][...], bq, bv, att, qaug, k, v, q_scr
    )


def attend_other_kernel(own, heads, info, x, near, far, bq, bv, _, att, qaug, k, v, w, q_scr):
    rows = near.shape[1]

    @pl.when(pl.program_id(0) == 0)
    def _():
        core = info[own + 1 + own * heads]
        for n in range(3):
            w[n, pl.ds(pl.multiple_of(core * rows, rows), rows), :] = near[n]
            w[n, pl.ds(pl.multiple_of((1 - core) * rows, rows), rows), :] = far[n]

    attend_steps(own, heads, info, x, lambda n: w[n], bq, bv, att, qaug, k, v, q_scr)


def attend(info, side, x, weights, bq, bv, own, att=None):
    D = x.shape[1]
    half = bq.shape[1]
    heads = half // HEAD_DIM
    last = own
    in_specs = [
        pl.BlockSpec((BLOCK, D), lambda s, n: (n[jnp.minimum(s, last)], 0)),
        *[whole(w.shape) for w in weights],
        whole((1, half)),
        whole((1, half)),
    ]
    where = own + 1 + own * heads + 1 + side
    out_specs = [
        pl.BlockSpec((BLOCK, half), lambda s, n: (jnp.maximum(s - last - 1, 0), n[where])),
        whole((own, heads, BLOCK, PAIR)),
        whole((own + 1, BLOCK, half)),
        whole((own + 1, BLOCK, half)),
    ]
    out_shape = [
        jax.ShapeDtypeStruct((own * BLOCK, 2 * half), bf16),
        jax.ShapeDtypeStruct((own, heads, BLOCK, PAIR), bf16),
        jax.ShapeDtypeStruct((own + 1, BLOCK, half), bf16),
        jax.ShapeDtypeStruct((own + 1, BLOCK, half), bf16),
    ]
    operands = [info, x, *weights, bq, bv]
    aliases = {}
    if att is None:
        body = attend_own_kernel
    else:
        body = attend_other_kernel
        in_specs.append(pl.BlockSpec(memory_space=pl.ANY))
        operands.append(att)
        aliases = {len(operands) - 1: 0}
        out_specs.append(whole((3, D, half)))
        out_shape.append(jax.ShapeDtypeStruct((3, D, half), bf16))
    pairs = own * heads
    return pl.pallas_call(
        functools.partial(body, own, heads),
        grid_spec=pltpu.PrefetchScalarGridSpec(
            num_scalar_prefetch=1,
            grid=(2 * own + 1,),
            in_specs=in_specs,
            out_specs=out_specs,
            scratch_shapes=[pltpu.VMEM((own, BLOCK, half), bf16)],
        ),
        out_shape=out_shape,
        input_output_aliases=aliases,
        compiler_params=params(),
        cost_estimate=cost(20e9 * pairs / 18, 16e6),
        name="attend_forward",
    )(*operands)


def attend_back_kernel(
    own, heads, info, qaug_ref, k_ref, v_ref, att_ref, do_ref, dq_ref, dk_ref, dv_ref, bias_ref
):
    i = pl.program_id(0)
    lane = lax.broadcasted_iota(jnp.int32, (BLOCK, PAIR), 1)
    low = lane < HEAD_DIM

    @pl.when(i == 0)
    def _():
        dk_ref[...] = jnp.zeros_like(dk_ref)
        dv_ref[...] = jnp.zeros_like(dv_ref)
        bias_ref[...] = jnp.zeros_like(bias_ref)

    for pair in range(heads // 2):
        cols = slice(pair * PAIR, pair * PAIR + PAIR)
        do = do_ref[:, cols]
        prod = do.astype(f32) * att_ref[:, cols].astype(f32)
        dqs = []
        for a in range(2):
            c = info[own + 1 + i * heads + 2 * pair + a]
            mine = low if a == 0 else jnp.logical_not(low)
            base = HEAD_DIM if a == 0 else 0
            delta = jnp.sum(jnp.where(mine, prod, 0.0), axis=1, keepdims=True)
            hi = delta.astype(bf16).astype(f32)
            aug = jnp.where(lane == base, hi, jnp.where(lane == base + 1, delta - hi, 0.0))
            doaug = jnp.where(mine, do, aug.astype(bf16))
            k = k_ref[c, :, cols]
            v = v_ref[c, :, cols]
            extra = jnp.where((lane >= base) & (lane < base + 3), -1.0, 0.0).astype(bf16)
            q = qaug_ref[i, 2 * pair + a]
            p = jnp.exp2(dot(jnp.where(mine, k, extra), q, NT) * EXP_SCALE)
            ds = (p * dot(jnp.where(mine, v, extra), doaug, NT)).astype(bf16)
            dv = dot(p.astype(bf16), do).astype(bf16)
            dk = (dot(ds, q) * SCALE).astype(bf16)
            dqs.append(dot(ds, k, TN) * SCALE)
            dk_ref[c, :, cols] = jnp.where(mine, dk, dk_ref[c, :, cols])
            dv_ref[c, :, cols] = jnp.where(mine, dv, dv_ref[c, :, cols])
            bias_ref[1:2, cols] += colsum(jnp.where(mine, dv.astype(f32), 0.0))
        dq = jnp.where(low, dqs[0], dqs[1]).astype(bf16)
        dq_ref[:, cols] = dq
        bias_ref[0:1, cols] += colsum(dq.astype(f32))


def attend_back(info, side, qaug, k, v, att, do, own):
    heads = qaug.shape[1]
    half = k.shape[2]
    where = own + 1 + own * heads + 1 + side
    kv = (own + 1, BLOCK, half)
    rows = pl.BlockSpec((BLOCK, half), lambda s, n: (s, n[where]))
    pairs = own * heads
    return pl.pallas_call(
        functools.partial(attend_back_kernel, own, heads),
        grid_spec=pltpu.PrefetchScalarGridSpec(
            num_scalar_prefetch=1,
            grid=(own,),
            in_specs=[
                pl.BlockSpec((1, heads, BLOCK, PAIR), lambda s, n: (s, 0, 0, 0))
                if False
                else whole(qaug.shape),
                whole(kv),
                whole(kv),
                rows,
                rows,
            ],
            out_specs=[
                pl.BlockSpec((BLOCK, half), lambda s, n: (s, 0)),
                whole(kv),
                whole(kv),
                whole((8, half)),
            ],
        ),
        out_shape=[
            jax.ShapeDtypeStruct((own * BLOCK, half), bf16),
            jax.ShapeDtypeStruct(kv, bf16),
            jax.ShapeDtypeStruct(kv, bf16),
            jax.ShapeDtypeStruct((8, half), f32),
        ],
        compiler_params=params(),
        cost_estimate=cost(20e9 * pairs / 18, 16e6),
        name="attend_backward",
    )(info, qaug, k, v, att, do)


def norm_terms(z):
    mean = jnp.mean(z, axis=1, keepdims=True)
    centred = z - mean
    variance = jnp.mean(centred * centred, axis=1, keepdims=True)
    inverse = lax.rsqrt(variance + EPS)
    return centred * inverse, inverse


def norm_back(incoming, normed, inverse, gain):
    scaled = incoming * gain
    first = jnp.mean(scaled, axis=1, keepdims=True)
    second = jnp.mean(scaled * normed, axis=1, keepdims=True)
    return inverse * (scaled - first - normed * second)


ERF_P = 0.3275911 * math.sqrt(0.5)
ERF_A = tuple(
    0.5 * a for a in (0.254829592, -0.284496736, 1.421413741, -1.453152027, 1.061405429)
)


def gelu_parts(v):
    e = jnp.exp2(v * v * (-0.5 * LOG2E))
    d = 1.0 + ERF_P * jnp.abs(v)
    t = pl.reciprocal(d, approx=True)
    t = t * (2.0 - d * t)
    poly = ERF_A[4]
    for a in ERF_A[3::-1]:
        poly = a + t * poly
    tail = t * poly * e
    cdf = jnp.where(v < 0, tail, 1.0 - tail)
    return v * cdf, cdf + v * e * (1.0 / math.sqrt(2 * math.pi))


def middle_kernel(
    chunk,
    info,
    att_ref,
    x_ref,
    cot_ref,
    wo_ref,
    bo_ref,
    g1_ref,
    s1_ref,
    wu_ref,
    bu_ref,
    wd_ref,
    bd_ref,
    g2_ref,
    s2_ref,
    out_ref,
    upin_ref,
    acted_ref,
    gpre_ref,
    gffn_ref,
    gbr_ref,
    gatt_ref,
    gfirst_ref,
    vec_ref,
    slope_scr,
):
    i = pl.program_id(0)
    D, ff = wu_ref.shape
    branch = dot(att_ref[...], wo_ref[...]) + bo_ref[...]
    n1, inv1 = norm_terms(x_ref[...].astype(f32) + branch)
    y1 = n1 * g1_ref[...] + s1_ref[...]
    upin = y1.astype(bf16)
    upin_ref[...] = upin
    ffn = bd_ref[...]
    for f in range(0, ff, chunk):
        cols = slice(f, f + chunk)
        value, slope = gelu_parts(dot(upin, wu_ref[:, cols]) + bu_ref[:, cols])
        act = value.astype(bf16)
        acted_ref[:, cols] = act
        slope_scr[:, cols] = slope
        ffn = ffn + dot(act, wd_ref[cols, :])
    n2, inv2 = norm_terms(y1 + ffn)
    out_ref[...] = (n2 * g2_ref[...] + s2_ref[...]).astype(bf16)
    e = cot_ref[...].astype(f32)
    gsecond = norm_back(e, n2, inv2, g2_ref[...])
    gffn = gsecond.astype(bf16)
    gffn_ref[...] = gffn

    @pl.when(i == 0)
    def _():
        vec_ref[...] = jnp.zeros_like(vec_ref)

    gnormed = gsecond
    for f in range(0, ff, chunk):
        cols = slice(f, f + chunk)
        gp = (dot(gffn, wd_ref[cols, :], NT) * slope_scr[:, cols]).astype(bf16)
        gpre_ref[:, cols] = gp
        sums = colsum(gp.astype(f32))
        for w in range(0, chunk, D):
            row = 8 + (f + w) // D
            vec_ref[row : row + 1, :] += sums[:, w : w + D]
        gnormed = gnormed + dot(gp, wu_ref[:, cols], NT)
    gfirst = norm_back(gnormed, n1, inv1, g1_ref[...])
    gfirst_ref[...] = gfirst
    gbr = gfirst.astype(bf16)
    gbr_ref[...] = gbr
    gatt_ref[...] = dot(gbr, wo_ref[...], NT).astype(bf16)
    for row, values in enumerate(
        (gbr.astype(f32), gnormed * n1, gnormed, gffn.astype(f32), e * n2, e)
    ):
        vec_ref[row : row + 1, :] += colsum(values)


def middle(info, where, att, x, cot, consts, tile=BLOCK):
    R, D = att.shape
    FF = consts[4].shape[1]
    tiles = R // tile
    row = lambda width: pl.BlockSpec((tile, width), lambda s, n: (s, 0))
    low = jax.ShapeDtypeStruct((R, D), bf16)
    wide = jax.ShapeDtypeStruct((R, FF), bf16)
    return pl.pallas_call(
        functools.partial(middle_kernel, D),
        grid_spec=pltpu.PrefetchScalarGridSpec(
            num_scalar_prefetch=1,
            grid=(tiles,),
            in_specs=[
                row(D),
                pl.BlockSpec((tile, D), lambda s, n: (s + n[where] * tiles, 0)),
                row(D),
                *[whole(c.shape) for c in consts],
            ],
            out_specs=[row(D), row(D), row(FF), row(FF), row(D), row(D), row(D), row(D)]
            + [whole((16, D))],
            scratch_shapes=[pltpu.VMEM((tile, FF), f32)],
        ),
        out_shape=[low, low, wide, wide, low, low, low, jax.ShapeDtypeStruct((R, D), f32)]
        + [jax.ShapeDtypeStruct((16, D), f32)],
        compiler_params=params(),
        cost_estimate=cost(60e9, 60e6),
        name="middle",
    )(info, att, x, cot, *consts)


def weight_kernel(flip, n_init, info, left_ref, right_ref, *refs):
    out_ref = refs[n_init]
    product = dot(left_ref[...], right_ref[...], TN)
    if flip:
        product = product.T
    for init in refs[:n_init]:
        product = product + init[...].astype(f32)
    out_ref[...] = product.astype(bf16)


def weight_grad(left, right, left_block, right_block, m, n, inits=(), flip=False, tile=None):
    K = left.shape[0]
    tile = tile or n
    steps = n // tile
    place = jnp.stack([left_block, right_block]).astype(jnp.int32)
    if flip:
        shape = (n, m)
        out_spec = pl.BlockSpec((tile, m), lambda s, p: (s, 0))
    else:
        shape = (m, n)
        out_spec = pl.BlockSpec((m, tile), lambda s, p: (0, s))
    return pl.pallas_call(
        functools.partial(weight_kernel, flip, len(inits)),
        grid_spec=pltpu.PrefetchScalarGridSpec(
            num_scalar_prefetch=1,
            grid=(steps,),
            in_specs=[
                pl.BlockSpec((K, m), lambda s, p: (0, p[0])),
                pl.BlockSpec((K, tile), lambda s, p: (0, p[1] * steps + s)),
                *[out_spec for _ in inits],
            ],
            out_specs=out_spec,
        ),
        out_shape=jax.ShapeDtypeStruct(shape, bf16),
        compiler_params=params(),
        cost_estimate=cost(3 * K * m * n, 2 * (K * m + K * n + m * n)),
        name="weight_grad",
    )(place, left, right, *inits)


def qkv_weight_kernel(own, n_init, info, x_ref, q_ref, k_ref, v_ref, *refs):
    out_ref = refs[n_init]
    half = q_ref.shape[1]
    s = pl.program_id(0)
    x = x_ref[...]

    @pl.when(s == 0)
    def _():
        out_ref[...] = jnp.zeros_like(out_ref)
        for init in refs[:n_init]:
            out_ref[...] += init[...].astype(f32)

    @pl.when(s < own)
    def _():
        out_ref[:, :half] += dot(x, q_ref[...], TN)

    out_ref[:, half : 2 * half] += dot(x, k_ref[0], TN)
    out_ref[:, 2 * half :] += dot(x, v_ref[0], TN)


def qkv_weight(info, core_block, x, dq, dk, dv, own, inits=()):
    half = dq.shape[1]
    D = x.shape[1]
    m = D // 2
    info = jnp.concatenate([info, core_block[None]])
    at = info.shape[0] - 1

    def kernel(info, x_ref, q_ref, k_ref, v_ref, *refs):
        n_init = len(inits)
        out_ref, acc = refs[n_init], refs[n_init + 1]
        qkv_weight_kernel(own, n_init, info, x_ref, q_ref, k_ref, v_ref, *refs[:n_init], acc)

        @pl.when(pl.program_id(0) == own)
        def _():
            out_ref[...] = acc[...].astype(bf16)

    return pl.pallas_call(
        kernel,
        grid_spec=pltpu.PrefetchScalarGridSpec(
            num_scalar_prefetch=1,
            grid=(own + 1,),
            in_specs=[
                pl.BlockSpec((BLOCK, m), lambda s, n: (n[s], n[at])),
                pl.BlockSpec((BLOCK, half), lambda s, n: (jnp.minimum(s, own - 1), 0)),
                pl.BlockSpec((1, BLOCK, half), lambda s, n: (s, 0, 0)),
                pl.BlockSpec((1, BLOCK, half), lambda s, n: (s, 0, 0)),
                *[whole((m, 3 * half)) for _ in inits],
            ],
            out_specs=whole((m, 3 * half)),
            scratch_shapes=[pltpu.VMEM((m, 3 * half), f32)],
        ),
        out_shape=jax.ShapeDtypeStruct((m, 3 * half), bf16),
        compiler_params=params(),
        cost_estimate=cost(3 * 2048 * m * 3 * half, 12e6),
        name="qkv_weight",
    )(info, x, dq, dk, dv, *inits)


def foreign_kernel(*refs):
    (ka, va, kb, vb, wka, wva, wb, out_ref) = refs
    total = dot(ka[0], wka[...], NT) + dot(va[0], wva[...], NT)
    total = total + dot(kb[0], wb[1], NT) + dot(vb[0], wb[2], NT)
    out_ref[...] = total.astype(bf16)


def foreign_grad(dkv, weights, other, own):
    D, half = weights[0].shape
    block = pl.BlockSpec((1, BLOCK, half), lambda s: (own, 0, 0))
    return pl.pallas_call(
        foreign_kernel,
        grid=(1,),
        in_specs=[block] * 4 + [whole((D, half))] * 2 + [whole(other.shape)],
        out_specs=pl.BlockSpec((BLOCK, D), lambda s: (0, 0)),
        out_shape=jax.ShapeDtypeStruct((BLOCK, D), bf16),
        compiler_params=params(),
        cost_estimate=cost(3 * BLOCK * D * 4 * half, 8e6),
        name="foreign_grad",
    )(*dkv, weights[1], weights[2], other)


def input_kernel(boundary, info, qa, ka, va, qb, kb, vb, wq, wk, wv, wb, first, recv, out_ref):
    total = first[...] + dot(qa[...], wq[...], NT) + dot(ka[0], wk[...], NT)
    total = total + dot(va[0], wv[...], NT) + dot(qb[...], wb[0], NT)
    total = total + dot(kb[0], wb[1], NT) + dot(vb[0], wb[2], NT)
    edge = pl.program_id(0) == info[boundary]

    @pl.when(edge)
    def _():
        out_ref[...] = total + recv[...].astype(f32)

    @pl.when(jnp.logical_not(edge))
    def _():
        out_ref[...] = total


def input_grad_of(info, boundary, mine, others, weights, other, first, recv, own):
    D, half = weights[0].shape
    row = pl.BlockSpec((BLOCK, half), lambda s, n: (s, 0))
    stacked = pl.BlockSpec((1, BLOCK, half), lambda s, n: (s, 0, 0))
    wide = pl.BlockSpec((BLOCK, D), lambda s, n: (s, 0))
    return pl.pallas_call(
        functools.partial(input_kernel, boundary),
        grid_spec=pltpu.PrefetchScalarGridSpec(
            num_scalar_prefetch=1,
            grid=(own,),
            in_specs=[row, stacked, stacked, row, stacked, stacked]
            + [whole((D, half))] * 3
            + [whole(other.shape), wide, whole((BLOCK, D))],
            out_specs=wide,
        ),
        out_shape=jax.ShapeDtypeStruct(first.shape, f32),
        compiler_params=params(),
        cost_estimate=cost(3 * own * BLOCK * D * 6 * half, 16e6),
        name="input_grad",
    )(info, *mine, *others, *weights, other, first, recv)


def flip_head(value):
    return lax.ppermute(value, "head", [(0, 1), (1, 0)])


def flip_dp(value, bit):
    size = lax.axis_size("dp")
    return lax.ppermute(value, "dp", [(i, i ^ (1 << bit)) for i in range(size)])


def sum_low(left, right):
    return (left.astype(f32) + right.astype(f32)).astype(bf16)


def bit_of(bit):
    return (lax.axis_index("dp") >> bit) & 1


def dp_bits():
    return range(1, (lax.axis_size("dp") - 1).bit_length())


def scatter_sum(part):
    for bit in dp_bits():
        rows = part.shape[0] // 2
        own = bit_of(bit)
        sent = lax.dynamic_slice_in_dim(part, (1 - own) * rows, rows, 0)
        kept = lax.dynamic_slice_in_dim(part, own * rows, rows, 0)
        part = sum_low(kept, flip_dp(sent, bit))
    return part


def join(mine, theirs, own, axis):
    first = jnp.where(own == 0, mine, theirs)
    second = jnp.where(own == 0, theirs, mine)
    return jnp.concatenate([first, second], axis=axis)


def gather_back(part, axis):
    for bit in reversed(dp_bits()):
        part = join(part, flip_dp(part, bit), bit_of(bit), 0)
    return join(part, flip_dp(part, 0), bit_of(0), axis).astype(f32)


def sum_all(value, with_head=True):
    if with_head:
        value = value + flip_head(value)
    for bit in range((lax.axis_size("dp") - 1).bit_length()):
        value = value + flip_dp(value, bit)
    return value


def body(
    hidden_in,
    w_query,
    b_query,
    w_key,
    w_value,
    b_value,
    w_out,
    b_out,
    gain_one,
    shift_one,
    w_up,
    b_up,
    w_down,
    b_down,
    gain_two,
    shift_two,
    seq_length,
    block_perm,
    cotangent,
):
    D, half = w_query.shape
    heads = half // HEAD_DIM
    blocks = hidden_in.shape[0] // BLOCK
    own = blocks // 2
    head = lax.axis_index("head")
    core = bit_of(0)

    rows = D // 2
    low_rows = [
        lax.dynamic_slice_in_dim(w, core * rows, rows, 0) for w in (w_query, w_key, w_value)
    ]
    near = flip_head(jnp.stack(low_rows))
    far = flip_dp(near, 0)
    small = flip_head(
        jnp.concatenate([b_query, b_value, block_perm.astype(f32).reshape(-1)])
    )
    other_bq, other_bv = small[:half], small[half : 2 * half]
    other_perm = small[2 * half :].astype(jnp.int32).reshape(block_perm.shape)

    per_seq = seq_length[0] // BLOCK
    first_block = head * own
    position = first_block + jnp.arange(own, dtype=jnp.int32)
    foreign = jnp.where(head == 0, own, own - 1)
    fetched = jnp.concatenate([position, foreign[None]])
    boundary_block = jnp.where(head == 0, own - 1, 0)

    def places(perm):
        mine = lax.dynamic_slice_in_dim(perm, first_block, own, 0)
        chosen = (position // per_seq * per_seq)[:, None] + mine % per_seq
        local = chosen - first_block
        local = jnp.where((local >= 0) & (local < own), local, own)
        tail = jnp.stack([core, head, 1 - head, boundary_block])
        return jnp.concatenate([fetched, local.reshape(-1), tail]).astype(jnp.int32)

    info_a, info_b = places(block_perm), places(other_perm)
    at_head = own + 1 + own * heads + 1
    at_boundary = at_head + 2

    weights = (w_query, w_key, w_value)
    vec = lambda v: v.reshape(1, -1)
    att, q_a, k_a, v_a = attend(
        info_a, 0, hidden_in, weights, vec(b_query), vec(b_value), own
    )
    att, q_b, k_b, v_b, w_b = attend(
        info_b, 1, hidden_in, (near, far), vec(other_bq), vec(other_bv), own, att
    )
    consts = (
        w_out,
        vec(b_out),
        vec(gain_one),
        vec(shift_one),
        w_up,
        vec(b_up),
        w_down,
        vec(b_down),
        vec(gain_two),
        vec(shift_two),
    )
    block_out, upin, acted, gpre, gffn, gbr, gatt, gfirst, vectors = middle(
        info_a, at_head, att, hidden_in, cotangent, consts
    )

    FF = w_up.shape[1]
    theirs, sibling = 1 - head, 1 - core

    def up(y, c, inits=()):
        return weight_grad(upin, gpre, jnp.int32(0), 2 * y + c, D, FF // 4, inits)

    def down(y, c, inits=()):
        return weight_grad(
            gffn, acted, y, c, D // 2, FF // 2, inits, flip=True, tile=FF // 4
        )

    def out(y, c, inits=()):
        return weight_grad(gbr, att, y, c, D // 2, D // 2, inits, flip=True)

    def reduce(part):
        sent = flip_dp(part(theirs, sibling), 0)
        sent = flip_head(part(theirs, core, (sent,)))
        kept = flip_dp(part(head, sibling), 0)
        kept = part(head, core, (kept,))
        return scatter_sum(sum_low(kept, sent))

    down_piece = reduce(down)
    up_piece = reduce(up)
    out_piece = reduce(out)
    vectors = sum_all(vectors)

    dq_b, dk_b, dv_b, bias_b = attend_back(info_b, 1, q_b, k_b, v_b, att, gatt, own)
    part = flip_dp(qkv_weight(info_b, sibling, hidden_in, dq_b, dk_b, dv_b, own), 0)
    part = qkv_weight(info_b, core, hidden_in, dq_b, dk_b, dv_b, own, (part,))
    from_other = flip_head(part)
    bias_other = flip_head(bias_b)

    dq_a, dk_a, dv_a, bias_a = attend_back(info_a, 0, q_a, k_a, v_a, att, gatt, own)
    received = flip_head(foreign_grad((dk_a, dv_a, dk_b, dv_b), weights, w_b, own))
    part = flip_dp(qkv_weight(info_a, sibling, hidden_in, dq_a, dk_a, dv_a, own), 0)
    part = qkv_weight(info_a, core, hidden_in, dq_a, dk_a, dv_a, own, (part, from_other))
    qkv_piece = scatter_sum(part)
    bias = sum_all(bias_a + bias_other, with_head=False)
    input_grad = input_grad_of(
        info_a,
        at_boundary,
        (dq_a, dk_a, dv_a),
        (dq_b, dk_b, dv_b),
        weights,
        w_b,
        gfirst,
        received,
        own,
    )

    grad_down = gather_back(down_piece, 0)
    grad_up = gather_back(up_piece, 1)
    grad_out = gather_back(out_piece, 0)
    grad_qkv = gather_back(qkv_piece, 0)

    def own_half(values):
        values = values.reshape(-1)
        n = values.shape[0] // 2
        return lax.dynamic_slice_in_dim(values, head * n, n, 0)

    return (
        block_out,
        input_grad,
        grad_qkv[:, :half],
        bias[0],
        grad_qkv[:, half : 2 * half],
        grad_qkv[:, 2 * half :],
        bias[1],
        grad_out,
        own_half(vectors[0]),
        own_half(vectors[1]),
        own_half(vectors[2]),
        grad_up,
        own_half(vectors[8 : 8 + FF // D]),
        grad_down,
        own_half(vectors[3]),
        own_half(vectors[4]),
        own_half(vectors[5]),
    )


def solution(mesh):
    rows = P(("dp", "head"), None)
    cols = P(None, "head")
    piece = P("head")
    return jax.shard_map(
        body,
        mesh=mesh,
        in_specs=(
            P("dp", None),
            cols,
            piece,
            cols,
            cols,
            piece,
            *[P()] * 10,
            P("dp"),
            P("dp", "head"),
            rows,
        ),
        out_specs=(
            rows,
            rows,
            cols,
            piece,
            cols,
            cols,
            piece,
            cols,
            piece,
            piece,
            piece,
            cols,
            piece,
            cols,
            piece,
            piece,
            piece,
        ),
        check_vma=False,
    )
```

time: 1130 us -> 465 us (0.41)
  matrix products: 460 us -> 0 us
  Pallas kernels: 0 us -> 256 us
  waiting for transfers between devices: 285 us -> 101 us
  local copies, waits for them, and re-layouts: 178 us -> 24.9 us
  blocking collectives: 116 us -> 0 us
  starting transfers between devices: 5.12 us -> 50 us
  other arithmetic: 58.3 us -> 22.4 us
  between operations: 16.5 us -> 2.31 us
    dot_general x60 -> x0, matrix products: 460 us -> none  [the longest x6 74.2 us: attend_back(): jnp.einsum('ivo,ion->ivn', score_gradient, selected_keys, preferred_eleme...]
    pallas_call x0 -> x23, Pallas kernels: none -> 256 us  [the longest x12 65.9 us: weight_grad(): pl.pallas_call(functools.partial(weight_kernel, flip, len(inits)), grid_s...]
    psum x1 -> x0, waiting for transfers between devices: 254 us -> none  [body(): lax.psum((grad_query, grad_query_bias, grad_key, grad_value, grad_value_b...]
    ppermute x0 -> x54, waiting for transfers between devices: none -> 101 us  [the longest x45 74.7 us: flip_dp(): return lax.ppermute(value, 'dp', [(i, i ^ 1 << bit) for i in range(size)])]
    psum x1 -> x0, blocking collectives: 57.9 us -> none  [body(): lax.psum((grad_query, grad_query_bias, grad_key, grad_value, grad_value_b...]
    ppermute x0 -> x54, starting transfers between devices: none -> 50 us  [the longest x45 40.3 us: flip_dp(): return lax.ppermute(value, 'dp', [(i, i ^ 1 << bit) for i in range(size)])]
    unnamed x96 -> x44, local copies, waits for them, and re-layouts: 53.2 us -> 4.06 us
    all_to_all x1 -> x0, blocking collectives: 48.5 us -> none  [body(): lax.all_to_all(grad_mixed, 'head', split_axis=1, concat_axis=0, tiled=True)]
  transfers between devices with their start and end apart: 6 -> 54, of which waited for: 3 -> 18; matrix products, arithmetic and copies ran while one was open for 35% -> 8% of each run, Pallas kernels for 0% -> 35%
where the time goes in v1:
time: 465 us; the launch traced here: 456 us
  Pallas kernels  256 us (55%)
  waiting for transfers between devices  101 us (22%)
  starting transfers between devices  50 us (11%)
  local copies, waits for them, and re-layouts  24.9 us (5%)
  other arithmetic  22.4 us (5%)
    ppermute x45, waiting for transfers between devices, flip_dp(): return lax.ppermute(value, 'dp', [(i, i ^ 1 << bit) for i in range(size)])  74.7 us
    pallas_call x12, Pallas kernels, weight_grad(): pl.pallas_call(functools.partial(weight_kernel, flip, len(inits)), grid_s...  65.9 us
    pallas_call x1, Pallas kernels, middle(): pl.pallas_call(functools.partial(middle_kernel, D), grid_spec=pltpu.Prefe...  63.4 us
    ppermute x45, starting transfers between devices, flip_dp(): return lax.ppermute(value, 'dp', [(i, i ^ 1 << bit) for i in range(size)])  40.3 us
    pallas_call x2, Pallas kernels, attend(): pl.pallas_call(functools.partial(body, own, heads), grid_spec=pltpu.Prefe...  39.4 us
    pallas_call x2, Pallas kernels, attend_back(): pl.pallas_call(functools.partial(attend_back_kernel, own, heads), grid_sp...  37.2 us
    pallas_call x4, Pallas kernels, qkv_weight(): pl.pallas_call(kernel, grid_spec=pltpu.PrefetchScalarGridSpec(num_scalar_...  30.9 us
    ppermute x9, waiting for transfers between devices, flip_head(): return lax.ppermute(value, 'head', [(0, 1), (1, 0)])  25.8 us
  transfers between devices with their start and end apart: 54, of which 18 were waited for; matrix products, arithmetic and copies ran while one was open for 8% of the time, Pallas kernels for 35%

profile of v1, /device:TPU:0, one launch (start us, length us, event | category | flops | bytes accessed | tf_op | source)
XLA Modules:
  0.0 456.0 jit_solution(12604616838890003967)
XLA Ops:
  2.1 3.0 collective-permute-start
  18.3 10.3 %collective-permute-done.1.near = bf16[3,384,384]{2,1,0:T(8,128)(2,1)S(1)} collective-permute-done((bf16[3,384,384]{2,1,0:T(8,128)(2,1)S(1)}, bf16[3,384,384]{2,1,0:T(8,128)(2,1)S(1)}, u32[]{:S(2)}, u32[]{:S(2)}) %collective-permute-start.1) | collective-permute-done | bytes 884768 | tf_op jit(solution)/shard_map/ppermute | solution.py:548
  28.6 19.3 %attend_forward.2 = (bf16[1536,768]{1,0:T(8,128)(2,1)}, bf16[3,6,512,128]{3,2,1,0:T(8,128)(2,1)}, bf16[4,512,384]{2,1,0:T(8,128)(2,1)}, bf16[4,512,384]{2,1,0:T(8,128)(2,1)}) custom-call(s32[26]{0:T(128)} %concatenate.76.info, bf16[3072,768]{1,0:T(8,128)(2,1)} %x_ref.9, bf16[768,384]{1,0:T(8,128)(2,1)} %wq.3, bf16[768,384]{1,0:T(8,128)(2,1)} %wk.3, ...), custom_call_target="tpu_custom_call" | custom-call | flops 20000000000 | bytes 16000000 | tf_op jit(solution)/shard_map/attend_forward/pallas_call | solution.py:152
  53.3 20.1 %attend_forward.3 = (bf16[1536,768]{1,0:T(8,128)(2,1)}, bf16[3,6,512,128]{3,2,1,0:T(8,128)(2,1)}, bf16[4,512,384]{2,1,0:T(8,128)(2,1)}, bf16[4,512,384]{2,1,0:T(8,128)(2,1)}, bf16[3,768,384]{2,1,0:T(8,128)(2,1)}) custom-call(s32[26]{0:T(128)} %concatenate.78.info, bf16[3072,768]{1,0:T(8,128)(2,1)} %x_ref.9, ...), custom_call_target="tpu_custom_call", output_to_operand_aliasing={{0}: (6, {})} | custom-call | flops 20000000000 | bytes 16000000 | tf_op jit(solution)/shard_map/attend_forward/pallas_call | solution.py:152
  73.4 63.4 %middle.1 = (bf16[1536,768]{1,0:T(8,128)(2,1)}, bf16[1536,768]{1,0:T(8,128)(2,1)}, bf16[1536,3072]{1,0:T(8,128)(2,1)}, bf16[1536,3072]{1,0:T(8,128)(2,1)}, bf16[...) custom-call(s32[26]{0:T(128)} %concatenate.76.info, ...), custom_call_target="tpu_custom_call" | custom-call | flops 60000002048 | bytes 60000000 | tf_op jit(solution)/shard_map/middle/pallas_call | solution.py:367
  136.8 5.9 %weight_grad.20 = bf16[1536,384]{1,0:T(8,128)(2,1)} custom-call(s32[2]{0:T(128)} %pad_add_fusion.6.info, bf16[1536,768]{1,0:T(8,128)(2,1)} %get-tuple-element.67.left_ref, bf16[1536,3072]{1,0:T(8,128)(2,1)} %get-tuple-element.68.right_ref), custom_call_target="tpu_custom_call" | custom-call | flops 2717908992 | bytes 7077888 | tf_op jit(solution)/shard_map/weight_grad/pallas_call | solution.py:411
  142.7 5.9 %weight_grad.22 = bf16[1536,384]{1,0:T(8,128)(2,1)} custom-call(s32[2]{0:T(128)} %pad_add_fusion.7.info, bf16[1536,768]{1,0:T(8,128)(2,1)} %get-tuple-element.67.left_ref, bf16[1536,3072]{1,0:T(8,128)(2,1)} %get-tuple-element.68.right_ref), custom_call_target="tpu_custom_call" | custom-call | flops 2717908992 | bytes 7077888 | tf_op jit(solution)/shard_map/weight_grad/pallas_call | solution.py:411
  149.1 6.2 %weight_grad.16 = bf16[768,768]{1,0:T(8,128)(2,1)} custom-call(s32[2]{0:T(128)} %get-tuple-element.117.info, bf16[1536,768]{1,0:T(8,128)(2,1)} %get-tuple-element.65.left_ref, bf16[1536,3072]{1,0:T(8,128)(2,1)} %get-tuple-element.66.right_ref), custom_call_target="tpu_custom_call" | custom-call | flops 2717908992 | bytes 5898240 | tf_op jit(solution)/shard_map/weight_grad/pallas_call | solution.py:411
  155.3 6.2 %weight_grad.18 = bf16[768,768]{1,0:T(8,128)(2,1)} custom-call(s32[2]{0:T(128)} %get-tuple-element.116.info, bf16[1536,768]{1,0:T(8,128)(2,1)} %get-tuple-element.65.left_ref, bf16[1536,3072]{1,0:T(8,128)(2,1)} %get-tuple-element.66.right_ref), custom_call_target="tpu_custom_call" | custom-call | flops 2717908992 | bytes 5898240 | tf_op jit(solution)/shard_map/weight_grad/pallas_call | solution.py:411
  161.9 3.9 weight_grad.14
  165.8 18.5 %attend_backward.3 = (bf16[1536,384]{1,0:T(8,128)(2,1)}, bf16[4,512,384]{2,1,0:T(8,128)(2,1)}, bf16[4,512,384]{2,1,0:T(8,128)(2,1)}, f32[8,384]{1,0:T(8,128)}) custom-call(s32[26]{0:T(128)} %concatenate.78.info, bf16[3,6,512,128]{3,2,1,0:T(8,128)(2,1)} %get-tuple-element.53.qaug_ref, bf16[4,512,384]{2,1,0:T(8,128)(2,1)} %get-tuple-element.54.k_ref, ...), custom_call_target="tpu_custom_call" | custom-call | flops 20000000000 | bytes 16000000 | tf_op jit(solution)/shard_map/attend_backward/pallas_call | solution.py:219
  186.0 18.7 %attend_backward.2 = (bf16[1536,384]{1,0:T(8,128)(2,1)}, bf16[4,512,384]{2,1,0:T(8,128)(2,1)}, bf16[4,512,384]{2,1,0:T(8,128)(2,1)}, f32[8,384]{1,0:T(8,128)}) custom-call(s32[26]{0:T(128)} %concatenate.76.info, bf16[3,6,512,128]{3,2,1,0:T(8,128)(2,1)} %get-tuple-element.46.qaug_ref, bf16[4,512,384]{2,1,0:T(8,128)(2,1)} %get-tuple-element.47.k_ref, ...), custom_call_target="tpu_custom_call" | custom-call | flops 20000000000 | bytes 16000000 | tf_op jit(solution)/shard_map/attend_backward/pallas_call | solution.py:219
  205.7 3.9 weight_grad.12
  212.2 4.0 weight_grad.15
  216.7 7.3 %qkv_weight.5 = bf16[384,1152]{1,0:T(8,128)(2,1)} custom-call(s32[27]{0:T(128)} %concatenate.82.info, bf16[3072,768]{1,0:T(8,128)(2,1)} %x_ref.9, bf16[1536,384]{1,0:T(8,128)(2,1)} %get-tuple-element.56.qb.q_ref, bf16[4,512,384]{2,1,0:T(8,128)(2,1)} %get-tuple-element.57.refs_2_.kb.k_ref, bf16[4,512,384]{2,1,0:T(8,128)(2,1)} %get-tuple-element.58.refs_3_.vb.v_ref), custom_call_target="tpu_custom_call" | custom-call | flops 2717908992 | bytes 12000000 | tf_op jit(solution)/shard_map/qkv_weight/pallas_call | solution.py:466
  226.5 4.0 weight_grad.13
  233.1 7.7 %qkv_weight.4 = bf16[384,1152]{1,0:T(8,128)(2,1)} custom-call(s32[27]{0:T(128)} %concatenate.80.info, bf16[3072,768]{1,0:T(8,128)(2,1)} %x_ref.9, bf16[1536,384]{1,0:T(8,128)(2,1)} %get-tuple-element.50.qa.q_ref, bf16[4,512,384]{2,1,0:T(8,128)(2,1)} %get-tuple-element.51.refs_0_.ka.k_ref, bf16[4,512,384]{2,1,0:T(8,128)(2,1)} %get-tuple-element.52.refs_1_.va.v_ref), custom_call_target="tpu_custom_call" | custom-call | flops 2717908992 | bytes 12000000 | tf_op jit(solution)/shard_map/qkv_weight/pallas_call | solution.py:466
  240.7 2.6 collective-permute-start.18
  245.6 5.1 %foreign_grad.1 = bf16[512,768]{1,0:T(8,128)(2,1)} custom-call(bf16[4,512,384]{2,1,0:T(8,128)(2,1)} %get-tuple-element.51.refs_0_.ka.k_ref, bf16[4,512,384]{2,1,0:T(8,128)(2,1)} %get-tuple-element.52.refs_1_.va.v_ref, bf16[4,512,384]{2,1,0:T(8,128)(2,1)} %get-tuple-element.57.refs_2_.kb.k_ref, bf16[4,512,384]{2,1,0:T(8,128)(2,1)} %get-tuple-element.58.refs_3_.vb.v_ref, ...), custom_call_target="tpu_custom_call" | custom-call | flops 1811939328 | bytes 8000000 | tf_op jit(solution)/shard_map/foreign_grad/pallas_call | solution.py:498
  251.3 2.7 collective-permute-start.24
  254.5 3.1 collective-permute-done.33
  265.9 7.8 %qkv_weight.6 = bf16[384,1152]{1,0:T(8,128)(2,1)} custom-call(s32[27]{0:T(128)} %concatenate.81.info, bf16[3072,768]{1,0:T(8,128)(2,1)} %x_ref.9, bf16[1536,384]{1,0:T(8,128)(2,1)} %get-tuple-element.56.qb.q_ref, bf16[4,512,384]{2,1,0:T(8,128)(2,1)} %get-tuple-element.57.refs_2_.kb.k_ref, bf16[4,512,384]{2,1,0:T(8,128)(2,1)} %get-tuple-element.58.refs_3_.vb.v_ref, ...), custom_call_target="tpu_custom_call" | custom-call | flops 2717908992 | bytes 12000000 | tf_op jit(solution)/shard_map/qkv_weight/pallas_call | solution.py:466
  274.2 9.9 %collective-permute-done.3.recv = bf16[512,768]{1,0:T(8,128)(2,1)} collective-permute-done((bf16[512,768]{1,0:T(8,128)(2,1)}, bf16[512,768]{1,0:T(8,128)(2,1)}, u32[]{:S(2)}, u32[]{:S(2)}) %collective-permute-start.3) | collective-permute-done | bytes 786464 | tf_op jit(solution)/shard_map/ppermute | solution.py:548
  284.8 13.9 %input_grad.1 = f32[1536,768]{1,0:T(8,128)} custom-call(s32[26]{0:T(128)} %concatenate.76.info, bf16[1536,384]{1,0:T(8,128)(2,1)} %get-tuple-element.50.qa.q_ref, bf16[4,512,384]{2,1,0:T(8,128)(2,1)} %get-tuple-element.51.refs_0_.ka.k_ref, bf16[4,512,384]{2,1,0:T(8,128)(2,1)} %get-tuple-element.52.refs_1_.va.v_ref, ...), custom_call_target="tpu_custom_call" | custom-call | flops 8153726976 | bytes 16000000 | tf_op jit(solution)/shard_map/input_grad/pallas_call | solution.py:530
  301.0 6.3 %weight_grad.23 = bf16[1536,384]{1,0:T(8,128)(2,1)} custom-call(s32[2]{0:T(128)} %pad_add_fusion.4.info, bf16[1536,768]{1,0:T(8,128)(2,1)} %get-tuple-element.67.left_ref, bf16[1536,3072]{1,0:T(8,128)(2,1)} %get-tuple-element.68.right_ref, bf16[1536,384]{1,0:T(8,128)(2,1)} %copy-done.5), custom_call_target="tpu_custom_call" | custom-call | flops 2717908992 | bytes 7077888 | tf_op jit(solution)/shard_map/weight_grad/pallas_call | solution.py:411
  307.3 6.5 %weight_grad.19 = bf16[768,768]{1,0:T(8,128)(2,1)} custom-call(s32[2]{0:T(128)} %pad_add_fusion.1.info, bf16[1536,768]{1,0:T(8,128)(2,1)} %get-tuple-element.65.left_ref, bf16[1536,3072]{1,0:T(8,128)(2,1)} %get-tuple-element.66.right_ref, bf16[768,768]{1,0:T(8,128)(2,1)} %collective-permute-done.35.refs_0_), custom_call_target="tpu_custom_call" | custom-call | flops 2717908992 | bytes 5898240 | tf_op jit(solution)/shard_map/weight_grad/pallas_call | solution.py:411
  315.9 8.2 %qkv_weight.7 = bf16[384,1152]{1,0:T(8,128)(2,1)} custom-call(s32[27]{0:T(128)} %concatenate.79.info, bf16[3072,768]{1,0:T(8,128)(2,1)} %x_ref.9, bf16[1536,384]{1,0:T(8,128)(2,1)} %get-tuple-element.50.qa.q_ref, bf16[4,512,384]{2,1,0:T(8,128)(2,1)} %get-tuple-element.51.refs_0_.ka.k_ref, bf16[4,512,384]{2,1,0:T(8,128)(2,1)} %get-tuple-element.52.refs_1_.va.v_ref, ...), custom_call_target="tpu_custom_call" | custom-call | flops 2717908992 | bytes 12000000 | tf_op jit(solution)/shard_map/qkv_weight/pallas_call | solution.py:466
  327.2 6.4 %weight_grad.21 = bf16[1536,384]{1,0:T(8,128)(2,1)} custom-call(s32[2]{0:T(128)} %pad_add_fusion.5.info, bf16[1536,768]{1,0:T(8,128)(2,1)} %get-tuple-element.67.left_ref, bf16[1536,3072]{1,0:T(8,128)(2,1)} %get-tuple-element.68.right_ref, bf16[1536,384]{1,0:T(8,128)(2,1)} %collective-permute-done.44.refs_0_), custom_call_target="tpu_custom_call" | custom-call | flops 2717908992 | bytes 7077888 | tf_op jit(solution)/shard_map/weight_grad/pallas_call | solution.py:411
  333.7 6.6 %weight_grad.17 = bf16[768,768]{1,0:T(8,128)(2,1)} custom-call(s32[2]{0:T(128)} %pad_add_fusion.3.info, bf16[1536,768]{1,0:T(8,128)(2,1)} %get-tuple-element.65.left_ref, bf16[1536,3072]{1,0:T(8,128)(2,1)} %get-tuple-element.66.right_ref, bf16[768,768]{1,0:T(8,128)(2,1)} %collective-permute-done.34.refs_0_), custom_call_target="tpu_custom_call" | custom-call | flops 2717908992 | bytes 5898240 | tf_op jit(solution)/shard_map/weight_grad/pallas_call | solution.py:411
  344.4 4.1 collective-permute-done.8
  348.5 2.4 collective-permute-start.9
  352.6 2.9 collective-permute-done.9
  357.6 4.4 collective-permute-done.10
  362.1 5.6 %collective-permute-done.36 = bf16[768,768]{1,0:T(8,128)(2,1)S(1)} collective-permute-done((bf16[768,768]{1,0:T(8,128)(2,1)}, bf16[768,768]{1,0:T(8,128)(2,1)S(1)}, u32[]{:S(2)}, u32[]{:S(2)}) %collective-permute-start.36) | collective-permute-done | bytes 1179680 | tf_op jit(solution)/shard_map/ppermute | solution.py:548
  372.2 12.1 %collective-permute-done.37 = bf16[384,768]{1,0:T(8,128)(2,1)S(1)} collective-permute-done((bf16[384,768]{1,0:T(8,128)(2,1)S(1)}, bf16[384,768]{1,0:T(8,128)(2,1)S(1)}, u32[]{:S(2)}, u32[]{:S(2)}) %collective-permute-start.37) | collective-permute-done | bytes 589856 | tf_op jit(solution)/shard_map/ppermute | solution.py:553
  387.2 7.3 %collective-permute-done.38 = bf16[192,768]{1,0:T(8,128)(2,1)S(1)} collective-permute-done((bf16[192,768]{1,0:T(8,128)(2,1)S(1)}, bf16[192,768]{1,0:T(8,128)(2,1)S(1)}, u32[]{:S(2)}, u32[]{:S(2)}) %collective-permute-start.38) | collective-permute-done | bytes 294944 | tf_op jit(solution)/shard_map/ppermute | solution.py:553
  396.3 2.9 collective-permute-start.50
  399.2 6.3 %collective-permute-done.39 = bf16[96,768]{1,0:T(8,128)(2,1)S(1)} collective-permute-done((bf16[96,768]{1,0:T(8,128)(2,1)S(1)}, bf16[96,768]{1,0:T(8,128)(2,1)S(1)}, u32[]{:S(2)}, u32[]{:S(2)}) %collective-permute-start.39) | collective-permute-done | bytes 147488 | tf_op jit(solution)/shard_map/ppermute | solution.py:553
  405.7 4.6 %collective-permute-done.50 = bf16[192,384]{1,0:T(8,128)(2,1)S(1)} collective-permute-done((bf16[192,384]{1,0:T(8,128)(2,1)S(1)}, bf16[192,384]{1,0:T(8,128)(2,1)S(1)}, u32[]{:S(2)}, u32[]{:S(2)}) %collective-permute-start.50) | collective-permute-done | bytes 147488 | tf_op jit(solution)/shard_map/ppermute | solution.py:553
  410.8 3.2 collective-permute-done.40
  414.2 6.2 %collective-permute-done.51 = bf16[384,384]{1,0:T(8,128)(2,1)S(1)} collective-permute-done((bf16[384,384]{1,0:T(8,128)(2,1)S(1)}, bf16[384,384]{1,0:T(8,128)(2,1)S(1)}, u32[]{:S(2)}, u32[]{:S(2)}) %collective-permute-start.51) | collective-permute-done | bytes 294944 | tf_op jit(solution)/shard_map/ppermute | solution.py:553
  420.6 2.9 collective-permute-start.52
  425.6 3.0 collective-permute-start.42
  428.6 9.2 %collective-permute-done.52 = bf16[768,384]{1,0:T(8,128)(2,1)S(1)} collective-permute-done((bf16[768,384]{1,0:T(8,128)(2,1)S(1)}, bf16[768,384]{1,0:T(8,128)(2,1)S(1)}, u32[]{:S(2)}, u32[]{:S(2)}) %collective-permute-start.52) | collective-permute-done | bytes 589856 | tf_op jit(solution)/shard_map/ppermute | solution.py:553
  438.8 8.5 %collective-permute-done.42 = bf16[384,768]{1,0:T(8,128)(2,1)S(1)} collective-permute-done((bf16[384,768]{1,0:T(8,128)(2,1)S(1)}, bf16[384,768]{1,0:T(8,128)(2,1)S(1)}, u32[]{:S(2)}, u32[]{:S(2)}) %collective-permute-start.42) | collective-permute-done | bytes 589856 | tf_op jit(solution)/shard_map/ppermute | solution.py:553
  447.7 1.9 fusion.13
  450.0 2.5 maximum_convert_fusion.1
  453.0 2.8 maximum_convert_fusion
  (245 shorter events, 73.3 us)
Async XLA Ops:
  2.1 15.3 %collective-permute-start = (f32[804]{0:T(1024)S(1)}, f32[804]{0:T(1024)S(1)}, u32[]{:S(2)}, u32[]{:S(2)}) collective-permute-start(f32[804]{0:T(1024)S(1)} %pad_maximum_fusion.13), channel_id=1, source_target_pairs={{0,1},{1,0},{2,3},{3,2},{4,5},{5,4},{6,7},{7,6},{8,9},{9,8},{10,11... | collective-permute-start | bytes 9656 | tf_op jit(solution)/shard_map/ppermute | solution.py:548
  7.5 21.2 %collective-permute-start.1 = (bf16[3,384,384]{2,1,0:T(8,128)(2,1)S(1)}, bf16[3,384,384]{2,1,0:T(8,128)(2,1)S(1)}, u32[]{:S(2)}, u32[]{:S(2)}) collective-permute-start(bf16[3,384,384]{2,1,0:T(8,128)(2,1)S(1)} %pad_maximum_fusion.2), channel_id=1, source_target_pairs={{0,1},{1,0},{2,3},{3,2},{4,5},{5,4},{6,7},{7,6},{8,9},{9,8},{10,11... | collective-permute-start | bytes 2654216 | tf_op jit(solution)/shard_map/ppermute | solution.py:548
  28.6 23.7 %collective-permute-start.2 = (bf16[3,384,384]{2,1,0:T(8,128)(2,1)S(1)}, bf16[3,384,384]{2,1,0:T(8,128)(2,1)S(1)}, u32[]{:S(2)}, u32[]{:S(2)}) collective-permute-start(bf16[3,384,384]{2,1,0:T(8,128)(2,1)S(1)} %collective-permute-done.1.near), channel_id=1, source_target_pairs={{0,2},{2,0},{4,6},{6,4},{8,10},{10,8},{12,14},{14,12},{16,18},{18,... | collective-permute-start | bytes 2654216 | tf_op jit(solution)/shard_map/ppermute | solution.py:553
  148.6 150.3 %collective-permute-start.45 = (bf16[1536,384]{1,0:T(8,128)(2,1)}, bf16[1536,384]{1,0:T(8,128)(2,1)S(1)}, u32[]{:S(2)}, u32[]{:S(2)}) collective-permute-start(bf16[1536,384]{1,0:T(8,128)(2,1)} %weight_grad.22), channel_id=1, source_target_pairs={{0,2},{2,0},{4,6},{6,4},{8,10},{10,8},{12,14},{14,12},{16,18},{18,... | collective-permute-start | bytes 3538952 | tf_op jit(solution)/shard_map/ppermute | solution.py:553
  161.6 49.8 %collective-permute-start.29 = (f32[16,768]{1,0:T(8,128)S(1)}, f32[16,768]{1,0:T(8,128)S(1)}, u32[]{:S(2)}, u32[]{:S(2)}) collective-permute-start(f32[16,768]{1,0:T(8,128)S(1)} %copy-done.9), channel_id=1, source_target_pairs={{0,1},{1,0},{2,3},{3,2},{4,5},{5,4},{6,7},{7,6},{8,9},{9,8},{10,11... | collective-permute-start | bytes 147464 | tf_op jit(solution)/shard_map/ppermute | solution.py:548
  165.8 45.7 %collective-permute-start.20 = (bf16[384,384]{1,0:T(8,128)(2,1)}, bf16[384,384]{1,0:T(8,128)(2,1)S(1)}, u32[]{:S(2)}, u32[]{:S(2)}) collective-permute-start(bf16[384,384]{1,0:T(8,128)(2,1)} %weight_grad.14), channel_id=1, source_target_pairs={{0,2},{2,0},{4,6},{6,4},{8,10},{10,8},{12,14},{14,12},{16,18},{18,... | collective-permute-start | bytes 884744 | tf_op jit(solution)/shard_map/ppermute | solution.py:553
  184.3 20.4 %collective-permute-start.14 = (f32[8,384]{1,0:T(8,128)}, f32[8,384]{1,0:T(8,128)S(1)}, u32[]{:S(2)}, u32[]{:S(2)}) collective-permute-start(f32[8,384]{1,0:T(8,128)} %get-tuple-element.62), channel_id=1, source_target_pairs={{0,1},{1,0},{2,3},{3,2},{4,5},{5,4},{6,7},{7,6},{8,9},{9,8},{10,11... | collective-permute-start | bytes 36872 | tf_op jit(solution)/shard_map/ppermute | solution.py:548
  209.6 16.2 %collective-permute-start.19 = (bf16[384,384]{1,0:T(8,128)(2,1)}, bf16[384,384]{1,0:T(8,128)(2,1)S(1)}, u32[]{:S(2)}, u32[]{:S(2)}) collective-permute-start(bf16[384,384]{1,0:T(8,128)(2,1)} %weight_grad.12), channel_id=1, source_target_pairs={{0,2},{2,0},{4,6},{6,4},{8,10},{10,8},{12,14},{14,12},{16,18},{18,... | collective-permute-start | bytes 884744 | tf_op jit(solution)/shard_map/ppermute | solution.py:553
  209.9 14.1 %collective-permute-start.16 = (f32[8,384]{1,0:T(8,128)S(1)}, f32[8,384]{1,0:T(8,128)S(1)}, u32[]{:S(2)}, u32[]{:S(2)}) collective-permute-start(f32[8,384]{1,0:T(8,128)S(1)} %add.226), channel_id=1, source_target_pairs={{0,4},{2,6},{4,0},{6,2},{8,12},{10,14},{12,8},{14,10},{16,20},{18,... | collective-permute-start | bytes 36872 | tf_op jit(solution)/shard_map/ppermute | solution.py:553
  211.4 12.8 %collective-permute-start.30 = (f32[16,768]{1,0:T(8,128)S(1)}, f32[16,768]{1,0:T(8,128)S(1)}, u32[]{:S(2)}, u32[]{:S(2)}) collective-permute-start(f32[16,768]{1,0:T(8,128)S(1)} %add.234), channel_id=1, source_target_pairs={{0,2},{2,0},{4,6},{6,4},{8,10},{10,8},{12,14},{14,12},{16,18},{18,... | collective-permute-start | bytes 147464 | tf_op jit(solution)/shard_map/ppermute | solution.py:553
  216.2 14.4 %collective-permute-start.21 = (bf16[384,384]{1,0:T(8,128)(2,1)}, bf16[384,384]{1,0:T(8,128)(2,1)S(1)}, u32[]{:S(2)}, u32[]{:S(2)}) collective-permute-start(bf16[384,384]{1,0:T(8,128)(2,1)} %weight_grad.15), channel_id=1, source_target_pairs={{0,1},{1,0},{2,3},{3,2},{4,5},{5,4},{6,7},{7,6},{8,9},{9,8},{10,11... | collective-permute-start | bytes 884744 | tf_op jit(solution)/shard_map/ppermute | solution.py:548
  224.0 83.3 %collective-permute-start.35 = (bf16[768,768]{1,0:T(8,128)(2,1)}, bf16[768,768]{1,0:T(8,128)(2,1)}, u32[]{:S(2)}, u32[]{:S(2)}) collective-permute-start(bf16[768,768]{1,0:T(8,128)(2,1)} %weight_grad.18), channel_id=1, source_target_pairs={{0,2},{2,0},{4,6},{6,4},{8,10},{10,8},{12,14},{14,12},{16,18},{18,... | collective-permute-start | bytes 3538952 | tf_op jit(solution)/shard_map/ppermute | solution.py:553
  224.2 16.6 %collective-permute-start.17 = (f32[8,384]{1,0:T(8,128)S(1)}, f32[8,384]{1,0:T(8,128)S(1)}, u32[]{:S(2)}, u32[]{:S(2)}) collective-permute-start(f32[8,384]{1,0:T(8,128)S(1)} %add.227), channel_id=1, source_target_pairs={{0,8},{2,10},{4,12},{6,14},{8,0},{10,2},{12,4},{14,6},{16,24},{18,... | collective-permute-start | bytes 36872 | tf_op jit(solution)/shard_map/ppermute | solution.py:553
  225.8 17.6 %collective-permute-start.31 = (f32[16,768]{1,0:T(8,128)S(1)}, f32[16,768]{1,0:T(8,128)S(1)}, u32[]{:S(2)}, u32[]{:S(2)}) collective-permute-start(f32[16,768]{1,0:T(8,128)S(1)} %add.235), channel_id=1, source_target_pairs={{0,4},{2,6},{4,0},{6,2},{8,12},{10,14},{12,8},{14,10},{16,20},{18,... | collective-permute-start | bytes 147464 | tf_op jit(solution)/shard_map/ppermute | solution.py:553
  231.6 12.3 %collective-permute-start.22 = (bf16[192,384]{1,0:T(8,128)(2,1)S(1)}, bf16[192,384]{1,0:T(8,128)(2,1)S(1)}, u32[]{:S(2)}, u32[]{:S(2)}) collective-permute-start(bf16[192,384]{1,0:T(8,128)(2,1)S(1)} %constant_dynamic-slice_fusion.14), channel_id=1, source_target_pairs={{0,4},{2,6},{4,0},{6,2},{8,12},{10,14},{12,8},{14,10},{16,20},{18,... | collective-permute-start | bytes 442376 | tf_op jit(solution)/shard_map/ppermute | solution.py:553
  240.7 10.0 %collective-permute-start.18 = (f32[8,384]{1,0:T(8,128)S(1)}, f32[8,384]{1,0:T(8,128)S(1)}, u32[]{:S(2)}, u32[]{:S(2)}) collective-permute-start(f32[8,384]{1,0:T(8,128)S(1)} %add.228), channel_id=1, source_target_pairs={{0,16},{2,18},{4,20},{6,22},{8,24},{10,26},{12,28},{14,30},{16,0},... | collective-permute-start | bytes 36872 | tf_op jit(solution)/shard_map/ppermute | solution.py:553
  243.4 7.4 %collective-permute-start.32 = (f32[16,768]{1,0:T(8,128)S(1)}, f32[16,768]{1,0:T(8,128)S(1)}, u32[]{:S(2)}, u32[]{:S(2)}) collective-permute-start(f32[16,768]{1,0:T(8,128)S(1)} %add.236), channel_id=1, source_target_pairs={{0,8},{2,10},{4,12},{6,14},{8,0},{10,2},{12,4},{14,6},{16,24},{18,... | collective-permute-start | bytes 147464 | tf_op jit(solution)/shard_map/ppermute | solution.py:553
  244.0 7.2 %collective-permute-start.23 = (bf16[96,384]{1,0:T(8,128)(2,1)S(1)}, bf16[96,384]{1,0:T(8,128)(2,1)S(1)}, u32[]{:S(2)}, u32[]{:S(2)}) collective-permute-start(bf16[96,384]{1,0:T(8,128)(2,1)S(1)} %constant_dynamic-slice_fusion.13), channel_id=1, source_target_pairs={{0,8},{2,10},{4,12},{6,14},{8,0},{10,2},{12,4},{14,6},{16,24},{18,... | collective-permute-start | bytes 221192 | tf_op jit(solution)/shard_map/ppermute | solution.py:553
  250.7 14.3 %collective-permute-start.5 = (bf16[384,1152]{1,0:T(8,128)(2,1)S(1)}, bf16[384,1152]{1,0:T(8,128)(2,1)S(1)}, u32[]{:S(2)}, u32[]{:S(2)}) collective-permute-start(bf16[384,1152]{1,0:T(8,128)(2,1)S(1)} %copy-done.20), channel_id=1, source_target_pairs={{0,2},{2,0},{4,6},{6,4},{8,10},{10,8},{12,14},{14,12},{16,18},{18,... | collective-permute-start | bytes 2654216 | tf_op jit(solution)/shard_map/ppermute | solution.py:553
  251.3 7.2 %collective-permute-start.24 = (bf16[48,384]{1,0:T(8,128)(2,1)S(1)}, bf16[48,384]{1,0:T(8,128)(2,1)S(1)}, u32[]{:S(2)}, u32[]{:S(2)}) collective-permute-start(bf16[48,384]{1,0:T(8,128)(2,1)S(1)} %constant_dynamic-slice_fusion.12), channel_id=1, source_target_pairs={{0,16},{2,18},{4,20},{6,22},{8,24},{10,26},{12,28},{14,30},{16,0},... | collective-permute-start | bytes 110600 | tf_op jit(solution)/shard_map/ppermute | solution.py:553
  257.7 56.2 %collective-permute-start.4 = (bf16[384,1152]{1,0:T(8,128)(2,1)}, bf16[384,1152]{1,0:T(8,128)(2,1)}, u32[]{:S(2)}, u32[]{:S(2)}) collective-permute-start(bf16[384,1152]{1,0:T(8,128)(2,1)} %qkv_weight.4), channel_id=1, source_target_pairs={{0,2},{2,0},{4,6},{6,4},{8,10},{10,8},{12,14},{14,12},{16,18},{18,... | collective-permute-start | bytes 2654216 | tf_op jit(solution)/shard_map/ppermute | solution.py:553
  263.4 20.8 %collective-permute-start.3 = (bf16[512,768]{1,0:T(8,128)(2,1)}, bf16[512,768]{1,0:T(8,128)(2,1)}, u32[]{:S(2)}, u32[]{:S(2)}) collective-permute-start(bf16[512,768]{1,0:T(8,128)(2,1)} %foreign_grad.1), channel_id=1, source_target_pairs={{0,1},{1,0},{2,3},{3,2},{4,5},{5,4},{6,7},{7,6},{8,9},{9,8},{10,11... | collective-permute-start | bytes 2359304 | tf_op jit(solution)/shard_map/ppermute | solution.py:548
  265.0 8.7 %collective-permute-start.26 = (bf16[96,384]{1,0:T(8,128)(2,1)S(1)}, bf16[96,384]{1,0:T(8,128)(2,1)S(1)}, u32[]{:S(2)}, u32[]{:S(2)}) collective-permute-start(bf16[96,384]{1,0:T(8,128)(2,1)S(1)} %pad_maximum_fusion.12), channel_id=1, source_target_pairs={{0,8},{2,10},{4,12},{6,14},{8,0},{10,2},{12,4},{14,6},{16,24},{18,... | collective-permute-start | bytes 221192 | tf_op jit(solution)/shard_map/ppermute | solution.py:553
  273.7 41.6 %collective-permute-start.6 = (bf16[384,1152]{1,0:T(8,128)(2,1)}, bf16[384,1152]{1,0:T(8,128)(2,1)}, u32[]{:S(2)}, u32[]{:S(2)}) collective-permute-start(bf16[384,1152]{1,0:T(8,128)(2,1)} %qkv_weight.6), channel_id=1, source_target_pairs={{0,1},{1,0},{2,3},{3,2},{4,5},{5,4},{6,7},{7,6},{8,9},{9,8},{10,11... | collective-permute-start | bytes 2654216 | tf_op jit(solution)/shard_map/ppermute | solution.py:548
  284.2 14.6 %collective-permute-start.27 = (bf16[192,384]{1,0:T(8,128)(2,1)S(1)}, bf16[192,384]{1,0:T(8,128)(2,1)S(1)}, u32[]{:S(2)}, u32[]{:S(2)}) collective-permute-start(bf16[192,384]{1,0:T(8,128)(2,1)S(1)} %pad_maximum_fusion.11), channel_id=1, source_target_pairs={{0,4},{2,6},{4,0},{6,2},{8,12},{10,14},{12,8},{14,10},{16,20},{18,... | collective-permute-start | bytes 442376 | tf_op jit(solution)/shard_map/ppermute | solution.py:553
  298.8 27.1 %collective-permute-start.44 = (bf16[1536,384]{1,0:T(8,128)(2,1)S(1)}, bf16[1536,384]{1,0:T(8,128)(2,1)}, u32[]{:S(2)}, u32[]{:S(2)}) collective-permute-start(bf16[1536,384]{1,0:T(8,128)(2,1)S(1)} %copy-done.4), channel_id=1, source_target_pairs={{0,2},{2,0},{4,6},{6,4},{8,10},{10,8},{12,14},{14,12},{16,18},{18,... | collective-permute-start | bytes 3538952 | tf_op jit(solution)/shard_map/ppermute | solution.py:553
  300.0 33.7 %collective-permute-start.34 = (bf16[768,768]{1,0:T(8,128)(2,1)S(1)}, bf16[768,768]{1,0:T(8,128)(2,1)}, u32[]{:S(2)}, u32[]{:S(2)}) collective-permute-start(bf16[768,768]{1,0:T(8,128)(2,1)S(1)} %copy-done.3), channel_id=1, source_target_pairs={{0,2},{2,0},{4,6},{6,4},{8,10},{10,8},{12,14},{14,12},{16,18},{18,... | collective-permute-start | bytes 3538952 | tf_op jit(solution)/shard_map/ppermute | solution.py:553
  307.3 34.8 %collective-permute-start.28 = (bf16[384,384]{1,0:T(8,128)(2,1)S(1)}, bf16[384,384]{1,0:T(8,128)(2,1)}, u32[]{:S(2)}, u32[]{:S(2)}) collective-permute-start(bf16[384,384]{1,0:T(8,128)(2,1)S(1)} %pad_maximum_fusion.7), channel_id=1, source_target_pairs={{0,2},{2,0},{4,6},{6,4},{8,10},{10,8},{12,14},{14,12},{16,18},{18,... | collective-permute-start | bytes 884744 | tf_op jit(solution)/shard_map/ppermute | solution.py:553
  313.9 37.1 %collective-permute-start.46 = (bf16[1536,384]{1,0:T(8,128)(2,1)}, bf16[1536,384]{1,0:T(8,128)(2,1)}, u32[]{:S(2)}, u32[]{:S(2)}) collective-permute-start(bf16[1536,384]{1,0:T(8,128)(2,1)} %weight_grad.23), channel_id=1, source_target_pairs={{0,1},{1,0},{2,3},{3,2},{4,5},{5,4},{6,7},{7,6},{8,9},{9,8},{10,11... | collective-permute-start | bytes 3538952 | tf_op jit(solution)/shard_map/ppermute | solution.py:548
  315.3 52.3 %collective-permute-start.36 = (bf16[768,768]{1,0:T(8,128)(2,1)}, bf16[768,768]{1,0:T(8,128)(2,1)S(1)}, u32[]{:S(2)}, u32[]{:S(2)}) collective-permute-start(bf16[768,768]{1,0:T(8,128)(2,1)} %weight_grad.19), channel_id=1, source_target_pairs={{0,1},{1,0},{2,3},{3,2},{4,5},{5,4},{6,7},{7,6},{8,9},{9,8},{10,11... | collective-permute-start | bytes 3538952 | tf_op jit(solution)/shard_map/ppermute | solution.py:548
  325.8 14.4 %collective-permute-start.7 = (bf16[192,1152]{1,0:T(8,128)(2,1)}, bf16[192,1152]{1,0:T(8,128)(2,1)}, u32[]{:S(2)}, u32[]{:S(2)}) collective-permute-start(bf16[192,1152]{1,0:T(8,128)(2,1)} %constant_dynamic-slice_fusion.17), channel_id=1, source_target_pairs={{0,4},{2,6},{4,0},{6,2},{8,12},{10,14},{12,8},{14,10},{16,20},{18,... | collective-permute-start | bytes 1327112 | tf_op jit(solution)/shard_map/ppermute | solution.py:553
  341.4 7.0 %collective-permute-start.8 = (bf16[96,1152]{1,0:T(8,128)(2,1)S(1)}, bf16[96,1152]{1,0:T(8,128)(2,1)S(1)}, u32[]{:S(2)}, u32[]{:S(2)}) collective-permute-start(bf16[96,1152]{1,0:T(8,128)(2,1)S(1)} %constant_dynamic-slice_fusion.16), channel_id=1, source_target_pairs={{0,8},{2,10},{4,12},{6,14},{8,0},{10,2},{12,4},{14,6},{16,24},{18,... | collective-permute-start | bytes 663560 | tf_op jit(solution)/shard_map/ppermute | solution.py:553
  356.8 13.5 %collective-permute-start.47 = (bf16[768,384]{1,0:T(8,128)(2,1)S(1)}, bf16[768,384]{1,0:T(8,128)(2,1)S(1)}, u32[]{:S(2)}, u32[]{:S(2)}) collective-permute-start(bf16[768,384]{1,0:T(8,128)(2,1)S(1)} %constant_dynamic-slice_fusion.5), channel_id=1, source_target_pairs={{0,4},{2,6},{4,0},{6,2},{8,12},{10,14},{12,8},{14,10},{16,20},{18,... | collective-permute-start | bytes 1769480 | tf_op jit(solution)/shard_map/ppermute | solution.py:553
  362.0 7.5 %collective-permute-start.11 = (bf16[96,1152]{1,0:T(8,128)(2,1)S(1)}, bf16[96,1152]{1,0:T(8,128)(2,1)S(1)}, u32[]{:S(2)}, u32[]{:S(2)}) collective-permute-start(bf16[96,1152]{1,0:T(8,128)(2,1)S(1)} %pad_maximum_fusion.10), channel_id=1, source_target_pairs={{0,8},{2,10},{4,12},{6,14},{8,0},{10,2},{12,4},{14,6},{16,24},{18,... | collective-permute-start | bytes 663560 | tf_op jit(solution)/shard_map/ppermute | solution.py:553
  368.0 16.3 %collective-permute-start.37 = (bf16[384,768]{1,0:T(8,128)(2,1)S(1)}, bf16[384,768]{1,0:T(8,128)(2,1)S(1)}, u32[]{:S(2)}, u32[]{:S(2)}) collective-permute-start(bf16[384,768]{1,0:T(8,128)(2,1)S(1)} %constant_dynamic-slice_fusion.8), channel_id=1, source_target_pairs={{0,4},{2,6},{4,0},{6,2},{8,12},{10,14},{12,8},{14,10},{16,20},{18,... | collective-permute-start | bytes 1769480 | tf_op jit(solution)/shard_map/ppermute | solution.py:553
  369.6 26.5 %collective-permute-start.12 = (bf16[192,1152]{1,0:T(8,128)(2,1)S(1)}, bf16[192,1152]{1,0:T(8,128)(2,1)S(1)}, u32[]{:S(2)}, u32[]{:S(2)}) collective-permute-start(bf16[192,1152]{1,0:T(8,128)(2,1)S(1)} %pad_maximum_fusion.6), channel_id=1, source_target_pairs={{0,4},{2,6},{4,0},{6,2},{8,12},{10,14},{12,8},{14,10},{16,20},{18,... | collective-permute-start | bytes 1327112 | tf_op jit(solution)/shard_map/ppermute | solution.py:553
  370.5 14.8 %collective-permute-start.48 = (bf16[384,384]{1,0:T(8,128)(2,1)S(1)}, bf16[384,384]{1,0:T(8,128)(2,1)S(1)}, u32[]{:S(2)}, u32[]{:S(2)}) collective-permute-start(bf16[384,384]{1,0:T(8,128)(2,1)S(1)} %constant_dynamic-slice_fusion.4), channel_id=1, source_target_pairs={{0,8},{2,10},{4,12},{6,14},{8,0},{10,2},{12,4},{14,6},{16,24},{18,... | collective-permute-start | bytes 884744 | tf_op jit(solution)/shard_map/ppermute | solution.py:553
  384.5 10.0 %collective-permute-start.38 = (bf16[192,768]{1,0:T(8,128)(2,1)S(1)}, bf16[192,768]{1,0:T(8,128)(2,1)S(1)}, u32[]{:S(2)}, u32[]{:S(2)}) collective-permute-start(bf16[192,768]{1,0:T(8,128)(2,1)S(1)} %constant_dynamic-slice_fusion.7), channel_id=1, source_target_pairs={{0,8},{2,10},{4,12},{6,14},{8,0},{10,2},{12,4},{14,6},{16,24},{18,... | collective-permute-start | bytes 884744 | tf_op jit(solution)/shard_map/ppermute | solution.py:553
  385.4 10.8 %collective-permute-start.49 = (bf16[192,384]{1,0:T(8,128)(2,1)S(1)}, bf16[192,384]{1,0:T(8,128)(2,1)S(1)}, u32[]{:S(2)}, u32[]{:S(2)}) collective-permute-start(bf16[192,384]{1,0:T(8,128)(2,1)S(1)} %constant_dynamic-slice_fusion.3), channel_id=1, source_target_pairs={{0,16},{2,18},{4,20},{6,22},{8,24},{10,26},{12,28},{14,30},{16,0},... | collective-permute-start | bytes 442376 | tf_op jit(solution)/shard_map/ppermute | solution.py:553
  394.6 10.9 %collective-permute-start.39 = (bf16[96,768]{1,0:T(8,128)(2,1)S(1)}, bf16[96,768]{1,0:T(8,128)(2,1)S(1)}, u32[]{:S(2)}, u32[]{:S(2)}) collective-permute-start(bf16[96,768]{1,0:T(8,128)(2,1)S(1)} %constant_dynamic-slice_fusion.6), channel_id=1, source_target_pairs={{0,16},{2,18},{4,20},{6,22},{8,24},{10,26},{12,28},{14,30},{16,0},... | collective-permute-start | bytes 442376 | tf_op jit(solution)/shard_map/ppermute | solution.py:553
  396.3 14.0 %collective-permute-start.50 = (bf16[192,384]{1,0:T(8,128)(2,1)S(1)}, bf16[192,384]{1,0:T(8,128)(2,1)S(1)}, u32[]{:S(2)}, u32[]{:S(2)}) collective-permute-start(bf16[192,384]{1,0:T(8,128)(2,1)S(1)} %add_convert_fusion.9), channel_id=1, source_target_pairs={{0,16},{2,18},{4,20},{6,22},{8,24},{10,26},{12,28},{14,30},{16,0},... | collective-permute-start | bytes 442376 | tf_op jit(solution)/shard_map/ppermute | solution.py:553
  405.6 8.5 %collective-permute-start.40 = (bf16[96,768]{1,0:T(8,128)(2,1)S(1)}, bf16[96,768]{1,0:T(8,128)(2,1)S(1)}, u32[]{:S(2)}, u32[]{:S(2)}) collective-permute-start(bf16[96,768]{1,0:T(8,128)(2,1)S(1)} %add_convert_fusion.10), channel_id=1, source_target_pairs={{0,16},{2,18},{4,20},{6,22},{8,24},{10,26},{12,28},{14,30},{16,0},... | collective-permute-start | bytes 442376 | tf_op jit(solution)/shard_map/ppermute | solution.py:553
  410.4 10.1 %collective-permute-start.51 = (bf16[384,384]{1,0:T(8,128)(2,1)S(1)}, bf16[384,384]{1,0:T(8,128)(2,1)S(1)}, u32[]{:S(2)}, u32[]{:S(2)}) collective-permute-start(bf16[384,384]{1,0:T(8,128)(2,1)S(1)} %pad_maximum_fusion.9), channel_id=1, source_target_pairs={{0,8},{2,10},{4,12},{6,14},{8,0},{10,2},{12,4},{14,6},{16,24},{18,... | collective-permute-start | bytes 884744 | tf_op jit(solution)/shard_map/ppermute | solution.py:553
  414.1 11.3 %collective-permute-start.41 = (bf16[192,768]{1,0:T(8,128)(2,1)S(1)}, bf16[192,768]{1,0:T(8,128)(2,1)S(1)}, u32[]{:S(2)}, u32[]{:S(2)}) collective-permute-start(bf16[192,768]{1,0:T(8,128)(2,1)S(1)} %pad_maximum_fusion.8), channel_id=1, source_target_pairs={{0,8},{2,10},{4,12},{6,14},{8,0},{10,2},{12,4},{14,6},{16,24},{18,... | collective-permute-start | bytes 884744 | tf_op jit(solution)/shard_map/ppermute | solution.py:553
  420.6 17.2 %collective-permute-start.52 = (bf16[768,384]{1,0:T(8,128)(2,1)S(1)}, bf16[768,384]{1,0:T(8,128)(2,1)S(1)}, u32[]{:S(2)}, u32[]{:S(2)}) collective-permute-start(bf16[768,384]{1,0:T(8,128)(2,1)S(1)} %pad_maximum_fusion.5), channel_id=1, source_target_pairs={{0,4},{2,6},{4,0},{6,2},{8,12},{10,14},{12,8},{14,10},{16,20},{18,... | collective-permute-start | bytes 1769480 | tf_op jit(solution)/shard_map/ppermute | solution.py:553
  423.6 14.6 %collective-permute-start.13 = (bf16[384,1152]{1,0:T(8,128)(2,1)S(1)}, bf16[384,1152]{1,0:T(8,128)(2,1)S(1)}, u32[]{:S(2)}, u32[]{:S(2)}) collective-permute-start(bf16[384,1152]{1,0:T(8,128)(2,1)S(1)} %pad_maximum_fusion.3), channel_id=1, source_target_pairs={{0,2},{2,0},{4,6},{6,4},{8,10},{10,8},{12,14},{14,12},{16,18},{18,... | collective-permute-start | bytes 2654216 | tf_op jit(solution)/shard_map/ppermute | solution.py:553
  425.6 21.7 %collective-permute-start.42 = (bf16[384,768]{1,0:T(8,128)(2,1)S(1)}, bf16[384,768]{1,0:T(8,128)(2,1)S(1)}, u32[]{:S(2)}, u32[]{:S(2)}) collective-permute-start(bf16[384,768]{1,0:T(8,128)(2,1)S(1)} %pad_maximum_fusion.4), channel_id=1, source_target_pairs={{0,4},{2,6},{4,0},{6,2},{8,12},{10,14},{12,8},{14,10},{16,20},{18,... | collective-permute-start | bytes 1769480 | tf_op jit(solution)/shard_map/ppermute | solution.py:553
  438.1 11.4 %collective-permute-start.53 = (bf16[1536,384]{1,0:T(8,128)(2,1)S(1)}, bf16[1536,384]{1,0:T(8,128)(2,1)S(1)}, u32[]{:S(2)}, u32[]{:S(2)}) collective-permute-start(bf16[1536,384]{1,0:T(8,128)(2,1)S(1)} %pad_maximum_fusion.1), channel_id=1, source_target_pairs={{0,2},{2,0},{4,6},{6,4},{8,10},{10,8},{12,14},{14,12},{16,18},{18,... | collective-permute-start | bytes 3538952 | tf_op jit(solution)/shard_map/ppermute | solution.py:553
  (28 other events, 175.6 us)

commit v2 on v1

v2 whole, which is shorter than its diff:
```python
import functools
import math

import jax
import jax.numpy as jnp
from jax import lax
from jax.experimental import pallas as pl
from jax.experimental.pallas import tpu as pltpu
from jax.sharding import PartitionSpec as P

HEAD_DIM = 64
BLOCK = 512
PAIR = 2 * HEAD_DIM
EPS = 1e-5
SCALE = 1.0 / math.sqrt(HEAD_DIM)
VMEM_LIMIT = 60 * 1024 * 1024
bf16, f32 = jnp.bfloat16, jnp.float32
NT = (((1,), (1,)), ((), ()))
TN = (((0,), (0,)), ((), ()))
QUICK = pl.CostEstimate(flops=1000, bytes_accessed=1000, transcendentals=0)


def dot(left, right, dims=None):
    if dims is None:
        return jnp.dot(left, right, preferred_element_type=f32)
    return lax.dot_general(left, right, dims, preferred_element_type=f32)


def params():
    return pltpu.CompilerParams(vmem_limit_bytes=VMEM_LIMIT)


def whole(shape):
    return pl.BlockSpec(shape, lambda *_: (0,) * len(shape), pipeline_mode=pl.Buffered(1))


def colsum(values):
    return jnp.sum(values, axis=0, keepdims=True)


HEAD, CORE, NEXT = range(3)


def block_row(s, info, own):
    return jnp.where(s < own, info[HEAD] * own + s, jnp.where(info[HEAD] == 0, own, own - 1))


def key_place(own, info, length, perm, i, h):
    n = length[0] // BLOCK
    p = info[HEAD] * own + i
    c = p // n * n + perm[p, h] % n - info[HEAD] * own
    return jnp.where((c >= 0) & (c < own), c, own)


def attend_steps(own, info, length, perm, x_ref, w_ref, b_ref, att_ref, qaug_ref, kv_ref, q_scr):
    step = pl.program_id(0)
    half = q_scr.shape[2]
    heads = half // HEAD_DIM

    @pl.when(step <= own)
    def _():
        x = x_ref[...]
        kv = dot(x, w_ref[:, half:])
        kv_ref[step, :, :half] = kv[:, :half].astype(bf16)
        kv_ref[step, :, half:] = (kv[:, half:] + b_ref[1:2, :]).astype(bf16)

        @pl.when(step < own)
        def _():
            q = (dot(x, w_ref[:, :half]) + b_ref[0:1, :]).astype(bf16)
            q_scr[step] = (q.astype(f32) * SCALE).astype(bf16)

    @pl.when(step > own)
    def _():
        i = step - own - 1
        lane = lax.broadcasted_iota(jnp.int32, (BLOCK, PAIR), 1)
        low = lane < HEAD_DIM
        for pair in range(heads // 2):
            cols = slice(pair * PAIR, pair * PAIR + PAIR)
            vcols = slice(half + pair * PAIR, half + pair * PAIR + PAIR)
            q = q_scr[i, :, cols]
            outs = []
            for a in range(2):
                c = key_place(own, info, length, perm, i, 2 * pair + a)
                mine = low if a == 0 else jnp.logical_not(low)
                base = HEAD_DIM if a == 0 else 0
                k = kv_ref[c, :, cols]
                v = kv_ref[c, :, vcols]
                s = dot(jnp.where(mine, q, jnp.zeros_like(q)), k, NT)
                m = jnp.max(s, axis=1, keepdims=True)
                p = jnp.exp(s - m).astype(bf16)
                o = dot(p, jnp.where(mine, v, jnp.ones_like(v)))
                total = m + jnp.log(o)
                hi = total.astype(bf16).astype(f32)
                rest = total - hi
                mid = rest.astype(bf16).astype(f32)
                aug = jnp.where(
                    lane == base,
                    hi,
                    jnp.where(lane == base + 1, mid, jnp.where(lane == base + 2, rest - mid, 0.0)),
                )
                qaug_ref[i, 2 * pair + a] = jnp.where(mine, q, aug.astype(bf16))
                outs.append(o * pl.reciprocal(pltpu.roll(o, HEAD_DIM, 1), approx=True))
            att_ref[:, cols] = jnp.where(low, outs[0], outs[1]).astype(bf16)


def attend_own_kernel(own, info, length, perm, x, w, b, att, qaug, kv, q_scr):
    attend_steps(own, info, length, perm, x, w, b, att, qaug, kv, q_scr)


def attend_other_kernel(own, info, length, perm, x, near, far, b, _, att, qaug, kv, w, q_scr):
    rows = near.shape[0]

    @pl.when(pl.program_id(0) == 0)
    def _():
        core = info[CORE]
        w[pl.ds(pl.multiple_of(core * rows, rows), rows), :] = near[...]
        w[pl.ds(pl.multiple_of((1 - core) * rows, rows), rows), :] = far[...]

    attend_steps(own, info, length, perm, x, w, b, att, qaug, kv, q_scr)


def attend(scalars, side, x, weights, biases, own, att=None):
    D = x.shape[1]
    half = D // 2
    heads = half // HEAD_DIM
    in_specs = [
        pl.BlockSpec((BLOCK, D), lambda s, n, *_: (block_row(jnp.minimum(s, own), n, own), 0)),
        *[whole(w.shape) for w in weights],
        whole(biases.shape),
    ]
    column = lambda n: n[HEAD] if side == 0 else 1 - n[HEAD]
    out_specs = [
        pl.BlockSpec((BLOCK, half), lambda s, n, *_: (jnp.maximum(s - own - 1, 0), column(n))),
        whole((own, heads, BLOCK, PAIR)),
        whole((own + 1, BLOCK, 2 * half)),
    ]
    out_shape = [
        jax.ShapeDtypeStruct((own * BLOCK, D), bf16),
        jax.ShapeDtypeStruct((own, heads, BLOCK, PAIR), bf16),
        jax.ShapeDtypeStruct((own + 1, BLOCK, 2 * half), bf16),
    ]
    operands = [*scalars, x, *weights, biases]
    aliases = {}
    if att is None:
        body = attend_own_kernel
    else:
        body = attend_other_kernel
        in_specs.append(pl.BlockSpec(memory_space=pl.ANY))
        operands.append(att)
        aliases = {len(operands) - 1: 0}
        out_specs.append(whole((D, 3 * half)))
        out_shape.append(jax.ShapeDtypeStruct((D, 3 * half), bf16))
    return pl.pallas_call(
        functools.partial(body, own),
        grid_spec=pltpu.PrefetchScalarGridSpec(
            num_scalar_prefetch=3,
            grid=(2 * own + 1,),
            in_specs=in_specs,
            out_specs=out_specs,
            scratch_shapes=[pltpu.VMEM((own, BLOCK, half), bf16)],
        ),
        out_shape=out_shape,
        input_output_aliases=aliases,
        compiler_params=params(),
        cost_estimate=QUICK,
        name="attend_forward",
    )(*operands)


def attend_back_kernel(
    own,
    info,
    length,
    perm,
    qaug_ref,
    kv_ref,
    att_ref,
    do_ref,
    x_ref,
    d_ref,
    near_ref,
    left_ref,
    right_ref,
    x_scr,
):
    step = pl.program_id(0)
    heads = qaug_ref.shape[1]
    half = heads * HEAD_DIM

    @pl.when(step == 0)
    def _():
        d_ref[...] = jnp.zeros_like(d_ref)

    x_scr[pl.ds(pl.multiple_of(step * BLOCK, BLOCK), BLOCK), :] = x_ref[...]

    @pl.when(step < own)
    def _():
        lane = lax.broadcasted_iota(jnp.int32, (BLOCK, PAIR), 1)
        low = lane < HEAD_DIM
        here = pl.ds(pl.multiple_of(step * BLOCK, BLOCK), BLOCK)
        for pair in range(heads // 2):
            cols = slice(pair * PAIR, pair * PAIR + PAIR)
            kcols = slice(half + pair * PAIR, half + pair * PAIR + PAIR)
            vcols = slice(2 * half + pair * PAIR, 2 * half + pair * PAIR + PAIR)
            do = do_ref[:, cols]
            prod = do.astype(f32) * att_ref[:, cols].astype(f32)
            dqs = []
            for a in range(2):
                c = key_place(own, info, length, perm, step, 2 * pair + a)
                mine = low if a == 0 else jnp.logical_not(low)
                base = HEAD_DIM if a == 0 else 0
                delta = jnp.sum(jnp.where(mine, prod, 0.0), axis=1, keepdims=True)
                hi = delta.astype(bf16).astype(f32)
                aug = jnp.where(lane == base, hi, jnp.where(lane == base + 1, delta - hi, 0.0))
                doaug = jnp.where(mine, do, aug.astype(bf16))
                k = kv_ref[c, :, cols]
                v = kv_ref[c, :, kcols]
                extra = jnp.where((lane >= base) & (lane < base + 3), -1.0, 0.0).astype(bf16)
                q = qaug_ref[0, 2 * pair + a]
                p = jnp.exp(dot(jnp.where(mine, k, extra), q, NT))
                ds = (p * dot(jnp.where(mine, v, extra), doaug, NT)).astype(bf16)
                dv = dot(p.astype(bf16), do).astype(bf16)
                dk = dot(ds, q).astype(bf16)
                dqs.append(dot(ds, k, TN) * SCALE)
                there = pl.ds(pl.multiple_of(c * BLOCK, BLOCK), BLOCK)
                d_ref[there, kcols] = jnp.where(mine, dk, d_ref[there, kcols])
                d_ref[there, vcols] = jnp.where(mine, dv, d_ref[there, vcols])
            d_ref[here, cols] = jnp.where(low, dqs[0], dqs[1]).astype(bf16)

    @pl.when(step == own)
    def _():
        core = info[CORE]
        d = d_ref[...]
        more = near_ref.shape[0] - half
        row = lax.broadcasted_iota(jnp.int32, (more, d.shape[1]), 0)
        sums = jnp.where(row == 0, colsum(d.astype(f32)), 0.0).astype(bf16)
        width = left_ref.shape[1]
        near_ref[half:, :] = sums
        left_ref[half:, :] = sums[:, :width]
        right_ref[half:, :] = sums[:, width:]
        x = x_scr[:, pl.ds(pl.multiple_of((1 - core) * half, half), half)]
        far = dot(x, d, TN).astype(bf16)
        left_ref[:half, :] = far[:, :width]
        right_ref[:half, :] = far[:, width:]
        x = x_scr[:, pl.ds(pl.multiple_of(core * half, half), half)]
        near_ref[:half, :] = dot(x, d, TN).astype(bf16)


def attend_back(scalars, side, qaug, kv, att, do, x, own):
    heads = qaug.shape[1]
    half = heads * HEAD_DIM
    D = x.shape[1]
    column = lambda n: n[HEAD] if side == 0 else 1 - n[HEAD]
    last = own - 1
    rows = pl.BlockSpec((BLOCK, half), lambda s, n, *_: (jnp.minimum(s, last), column(n)))
    d_shape = ((own + 1) * BLOCK, 3 * half)
    w_shape = (D // 2 + 16, 3 * half)
    w_parts = [(D // 2 + 16, width) for width in (2 * half - PAIR, half + PAIR)]
    return pl.pallas_call(
        functools.partial(attend_back_kernel, own),
        grid_spec=pltpu.PrefetchScalarGridSpec(
            num_scalar_prefetch=3,
            grid=(own + 1,),
            in_specs=[
                pl.BlockSpec(
                    (1, heads, BLOCK, PAIR), lambda s, *_: (jnp.minimum(s, last), 0, 0, 0)
                ),
                whole(kv.shape),
                rows,
                rows,
                pl.BlockSpec((BLOCK, D), lambda s, n, *_: (block_row(s, n, own), 0)),
            ],
            out_specs=[whole(d_shape), whole(w_shape), *[whole(w) for w in w_parts]],
            scratch_shapes=[pltpu.VMEM(((own + 1) * BLOCK, D), bf16)],
        ),
        out_shape=[
            jax.ShapeDtypeStruct(d_shape, bf16),
            jax.ShapeDtypeStruct(w_shape, bf16),
            *[jax.ShapeDtypeStruct(w, bf16) for w in w_parts],
        ],
        compiler_params=params(),
        cost_estimate=QUICK,
        name="attend_backward",
    )(*scalars, qaug, kv, att, do, x)


def norm_terms(z):
    mean = jnp.mean(z, axis=1, keepdims=True)
    centred = z - mean
    variance = jnp.mean(centred * centred, axis=1, keepdims=True)
    inverse = lax.rsqrt(variance + EPS)
    return centred * inverse, inverse


def norm_back(incoming, normed, inverse, gain):
    scaled = incoming * gain
    first = jnp.mean(scaled, axis=1, keepdims=True)
    second = jnp.mean(scaled * normed, axis=1, keepdims=True)
    return inverse * (scaled - first - normed * second)


def gelu_parts(v):
    cdf = 0.5 + 0.5 * lax.erf(v * math.sqrt(0.5))
    return v * cdf, cdf + v * (math.sqrt(0.5 / math.pi) * jnp.exp(v * (v * -0.5)))


def start_copies(pairs, sems):
    copies = [pltpu.make_async_copy(s, d, sems.at[n]) for n, (s, d) in enumerate(pairs)]

    @pl.when(pl.program_id(0) == 0)
    def _():
        for copy in copies:
            copy.start()

    return copies


def wait_copies(copies):
    @pl.when(pl.program_id(0) == 0)
    def _():
        for copy in copies:
            copy.wait()


def add_up(acc, rows, cols, value):
    first = pl.program_id(0) == 0
    acc[rows, cols] = jnp.where(first, value, value + acc[rows, cols])


OUT_ROWS = 32


def place_piece(info, c, y, x, near_ref, far_ref, rows, cols, piece):
    number = (info[HEAD] ^ y) * 2 + (info[NEXT] ^ x)

    @pl.when(info[CORE] == c)
    def _():
        near_ref[number, rows, cols] = piece

    @pl.when(info[CORE] != c)
    def _():
        far_ref[number, rows, cols] = piece


def middle_up_kernel(
    info,
    att_ref,
    x_ref,
    cot_ref,
    c_ref,
    wo_hbm,
    wu_hbm,
    wd_hbm,
    out_ref,
    slope_ref,
    n1_ref,
    inv_ref,
    gsec_ref,
    near_ref,
    far_ref,
    vec_ref,
    wo_ref,
    wu_ref,
    wd_ref,
    act_scr,
    acc,
    sems,
):
    i = pl.program_id(0)
    D, ff = wu_ref.shape
    copies = start_copies([(wo_hbm, wo_ref), (wu_hbm, wu_ref), (wd_hbm, wd_ref)], sems)
    bo, g1, s1, bd, g2, s2 = (c_ref[r : r + 1, :] for r in range(6))
    wait_copies(copies[:1])
    branch = dot(att_ref[...], wo_ref[...]) + bo
    n1, inv1 = norm_terms(x_ref[...].astype(f32) + branch)
    n1_ref[...] = n1
    inv_ref[...] = jnp.broadcast_to(inv1, inv_ref.shape)
    y1 = n1 * g1 + s1
    upin = y1.astype(bf16)
    wait_copies(copies[1:])
    ffn = bd
    for f in range(ff // D):
        cols = slice(f * D, f * D + D)
        value, slope = gelu_parts(dot(upin, wu_ref[:, cols]) + c_ref[8 + f : 9 + f, :])
        act = value.astype(bf16)
        act_scr[:, cols] = act
        slope_ref[:, cols] = slope.astype(bf16)
        ffn = ffn + dot(act, wd_ref[cols, :])
    n2, inv2 = norm_terms(y1 + ffn)
    out_ref[...] = (n2 * g2 + s2).astype(bf16)
    e = cot_ref[...].astype(f32)
    gsec = norm_back(e, n2, inv2, g2)
    gsec_ref[...] = gsec
    gffn = gsec.astype(bf16)
    for f in range(ff // D):
        cols = slice(f * D, f * D + D)
        add_up(acc, cols, slice(None), dot(act_scr[:, cols], gffn, TN))

    @pl.when(i == 0)
    def _():
        vec_ref[...] = jnp.zeros_like(vec_ref)

    for row, values in ((3, gffn.astype(f32)), (4, e * n2), (5, e)):
        vec_ref[row : row + 1, :] += colsum(values)

    @pl.when(i == pl.num_programs(0) - 1)
    def _():
        half = D // 2
        for number in range(4):
            near_ref[number, D:, :] = jnp.zeros((16, half), bf16)
            far_ref[number, D:, :] = jnp.zeros((16, half), bf16)
        for f in range(ff // D):
            for y in range(2):
                piece = acc[f * D : f * D + D, y * half : y * half + half].astype(bf16)
                place_piece(
                    info, f // 2, y, f % 2, near_ref, far_ref, slice(0, D), slice(None), piece
                )


def middle_up(info, att, x, cot, wo, wu, wd, consts, tile=BLOCK):
    R, D = att.shape
    FF = wu.shape[1]
    tiles = R // tile
    row = lambda width: pl.BlockSpec((tile, width), lambda s, n: (s, 0))
    anywhere = pl.BlockSpec(memory_space=pl.ANY)
    sd = jax.ShapeDtypeStruct
    pieces = (4, FF // 4 + 16, D // 2)
    return pl.pallas_call(
        middle_up_kernel,
        grid_spec=pltpu.PrefetchScalarGridSpec(
            num_scalar_prefetch=1,
            grid=(tiles,),
            in_specs=[
                row(D),
                pl.BlockSpec((tile, D), lambda s, n: (s + n[HEAD] * tiles, 0)),
                row(D),
                whole(consts.shape),
                anywhere,
                anywhere,
                anywhere,
            ],
            out_specs=[row(D), row(FF), row(D), row(128), row(D)]
            + [whole(pieces), whole(pieces), whole(consts.shape)],
            scratch_shapes=[
                pltpu.VMEM(wo.shape, bf16),
                pltpu.VMEM(wu.shape, bf16),
                pltpu.VMEM(wd.shape, bf16),
                pltpu.VMEM((tile, FF), bf16),
                pltpu.VMEM((FF, D), f32),
                pltpu.SemaphoreType.DMA((3,)),
            ],
        ),
        out_shape=[
            sd((R, D), bf16),
            sd((R, FF), bf16),
            sd((R, D), f32),
            sd((R, 128), f32),
            sd((R, D), f32),
            sd(pieces, bf16),
            sd(pieces, bf16),
            sd(consts.shape, f32),
        ],
        compiler_params=params(),
        cost_estimate=QUICK,
        name="middle_up",
    )(info, att, x, cot, consts, wo, wu, wd)


def middle_down_kernel(
    info,
    att_ref,
    slope_ref,
    n1_ref,
    inv_ref,
    gsec_ref,
    vec_in_ref,
    c_ref,
    wo_hbm,
    wu_hbm,
    wd_hbm,
    gatt_ref,
    gfirst_ref,
    near_ref,
    far_ref,
    wo_ref,
    wu_ref,
    wd_ref,
    vec_ref,
    gp_scr,
    acc,
    acc_out,
    sems,
):
    i = pl.program_id(0)
    D, ff = wu_ref.shape
    copies = start_copies([(wd_hbm, wd_ref), (wu_hbm, wu_ref), (wo_hbm, wo_ref)], sems)

    @pl.when(i == 0)
    def _():
        vec_ref[...] = vec_in_ref[...]

    wait_copies(copies[:1])
    g1, s1 = c_ref[1:2, :], c_ref[2:3, :]
    n1 = n1_ref[...]
    upin = (n1 * g1 + s1).astype(bf16)
    gsec = gsec_ref[...]
    gffn = gsec.astype(bf16)
    for f in range(ff // D):
        cols = slice(f * D, f * D + D)
        gp = (dot(gffn, wd_ref[cols, :], NT) * slope_ref[:, cols].astype(f32)).astype(bf16)
        gp_scr[:, cols] = gp
        vec_ref[8 + f : 9 + f, :] += colsum(gp.astype(f32))
    wait_copies(copies[1:])
    gnormed = gsec
    for f in range(ff // D):
        cols = slice(f * D, f * D + D)
        gp = gp_scr[:, cols]
        gnormed = gnormed + dot(gp, wu_ref[:, cols], NT)
        add_up(acc, slice(None), cols, dot(upin, gp, TN))
    gfirst = norm_back(gnormed, n1, inv_ref[:, :1], g1)
    gfirst_ref[...] = gfirst
    gbr = gfirst.astype(bf16)
    gatt_ref[...] = dot(gbr, wo_ref[...], NT).astype(bf16)
    add_up(acc_out, slice(None), slice(None), dot(gbr, att_ref[...], TN))
    for row, values in enumerate((gbr.astype(f32), gnormed * n1, gnormed)):
        vec_ref[row : row + 1, :] += colsum(values)

    @pl.when(i == pl.num_programs(0) - 1)
    def _():
        half, few = D // 2, D // 32
        for f in range(ff // D):
            for x in range(2):
                piece = acc[x * half : x * half + half, f * D : f * D + D].astype(bf16)
                place_piece(
                    info, f % 2, f // 2, x, near_ref, far_ref, slice(0, half), slice(None), piece
                )
        sums = vec_ref[...].astype(bf16)
        for number in range(4):
            near_ref[number, half + 4 * OUT_ROWS :, :] = sums
            far_ref[number, half + 4 * OUT_ROWS :, :] = sums
        for c in range(2):
            for y in range(2):
                for x in range(2):
                    for q in range(4):
                        top = (8 * y + 4 * x + q) * 2 * few
                        both = acc_out[top : top + 2 * few, c * half : c * half + half]
                        both = jnp.concatenate([both[:few], both[few:]], axis=1)
                        pad = jnp.zeros((OUT_ROWS - few, D), f32)
                        both = jnp.concatenate([both, pad], axis=0).astype(bf16)
                        rows = slice(half + q * OUT_ROWS, half + q * OUT_ROWS + OUT_ROWS)
                        place_piece(info, c, y, x, near_ref, far_ref, rows, slice(None), both)


def middle_down(info, att, saved, vectors, wo, wu, wd, consts, tile=BLOCK):
    R, D = att.shape
    FF = wu.shape[1]
    row = lambda width: pl.BlockSpec((tile, width), lambda s, n: (s, 0))
    anywhere = pl.BlockSpec(memory_space=pl.ANY)
    sd = jax.ShapeDtypeStruct
    pieces = (4, D // 2 + 4 * OUT_ROWS + consts.shape[0], FF // 4)
    return pl.pallas_call(
        middle_down_kernel,
        grid_spec=pltpu.PrefetchScalarGridSpec(
            num_scalar_prefetch=1,
            grid=(R // tile,),
            in_specs=[row(D), row(FF), row(D), row(128), row(D)]
            + [whole(consts.shape)] * 2
            + [anywhere] * 3,
            out_specs=[row(D), row(D), whole(pieces), whole(pieces)],
            scratch_shapes=[
                pltpu.VMEM(wo.shape, bf16),
                pltpu.VMEM(wu.shape, bf16),
                pltpu.VMEM(wd.shape, bf16),
                pltpu.VMEM(consts.shape, f32),
                pltpu.VMEM((tile, FF), bf16),
                pltpu.VMEM((D, FF), f32),
                pltpu.VMEM((D, D), f32),
                pltpu.SemaphoreType.DMA((3,)),
            ],
        ),
        out_shape=[
            sd((R, D), bf16),
            sd((R, D), f32),
            sd(pieces, bf16),
            sd(pieces, bf16),
        ],
        compiler_params=params(),
        cost_estimate=QUICK,
        name="middle_down",
    )(info, att, *saved, vectors, consts, wo, wu, wd)


def input_kernel(own, info, da, db, wa, wb, first, out_ref, next_ref):
    total = dot(da[...], wa[...], NT) + dot(db[...], wb[...], NT)

    @pl.when(pl.program_id(0) == 0)
    def _():
        next_ref[...] = total.astype(bf16)

    @pl.when(pl.program_id(0) > 0)
    def _():
        out_ref[...] = total + first[...]


def input_call(info, da, db, wa, wb, first, own):
    D, width = wa.shape
    row = pl.BlockSpec((BLOCK, width), lambda s, n: (jnp.where(s == 0, own, s - 1), 0))
    wide = pl.BlockSpec((BLOCK, D), lambda s, n: (jnp.maximum(s - 1, 0), 0))
    return pl.pallas_call(
        functools.partial(input_kernel, own),
        grid_spec=pltpu.PrefetchScalarGridSpec(
            num_scalar_prefetch=1,
            grid=(own + 1,),
            in_specs=[row, row, whole((D, width)), whole((D, width)), wide],
            out_specs=[wide, whole((BLOCK, D))],
        ),
        out_shape=[
            jax.ShapeDtypeStruct(first.shape, f32),
            jax.ShapeDtypeStruct((BLOCK, D), bf16),
        ],
        compiler_params=params(),
        cost_estimate=QUICK,
        name="input_grad",
    )(info, da, db, wa, wb, first)


def edge_kernel(info, recv, rest, out_ref):
    out_ref[...] = rest[...] + recv[...].astype(f32)


def edge_call(info, recv, rest, own):
    D = rest.shape[1]
    edge = pl.BlockSpec((BLOCK // 4, D), lambda s, n: (s + 4 * jnp.where(n[HEAD] == 0, own - 1, 0), 0))
    return pl.pallas_call(
        edge_kernel,
        grid_spec=pltpu.PrefetchScalarGridSpec(
            num_scalar_prefetch=1,
            grid=(4,),
            in_specs=[pl.BlockSpec((BLOCK // 4, D), lambda s, n: (s, 0)), edge],
            out_specs=edge,
        ),
        out_shape=jax.ShapeDtypeStruct(rest.shape, f32),
        input_output_aliases={2: 0},
        compiler_params=params(),
        cost_estimate=QUICK,
        name="edge_block",
    )(info, recv, rest)


def finish_up_kernel(info, vec_in_ref, parts, *refs):
    up_ref, out_ref, sums_ref, *vec_refs, scr = refs
    width = parts.shape[2]
    half, few = width // 2, width // 32
    count = parts.shape[0] // 4
    rows, size = half // count, parts.shape[1]
    for c in range(2):
        for x in range(2):
            for q in range(count):
                piece = parts[(2 * c + x) * count + q].astype(f32)
                up_ref[
                    x * half + q * rows : x * half + q * rows + rows, c * width : c * width + width
                ] = piece[:rows]
                for n in range(2):
                    top = x * (half // 2) + (2 * q + n) * few
                    scr[top : top + few, c * half : c * half + half] = piece[
                        rows : rows + few, n * half : n * half + half
                    ]
    out_ref[...] = scr[...].T
    vectors = vec_in_ref[...].astype(f32)
    mine = jnp.where(info[HEAD] == 0, vectors[:, :half], vectors[:, half:])
    for row, ref in enumerate(vec_refs):
        ref[...] = mine[row]
    chunks = sums_ref.shape[0] // width
    for n in range(chunks):
        both = jnp.where(info[HEAD] == 0, vectors[8 + n], vectors[8 + chunks + n])
        sums_ref[n * width : n * width + width] = both


def finish_up(info, vectors, parts):
    width = parts.shape[2]
    outs = [
        ((width, 2 * width), f32),
        ((width, width // 2), f32),
        ((2 * width,), f32),
        *[((width // 2,), f32)] * 6,
    ]
    scratch = [pltpu.VMEM((width // 2, width), f32)]
    return small_call(finish_up_kernel, "finish_up", outs, [info], [vectors, parts], scratch)


def small_call(kernel, name, outs, scalars, arrays, scratch=()):
    vmem = pl.BlockSpec(memory_space=pltpu.VMEM)
    smem = pl.BlockSpec(memory_space=pltpu.SMEM)
    return pl.pallas_call(
        kernel,
        in_specs=[smem] * len(scalars) + [vmem] * len(arrays),
        out_shape=[jax.ShapeDtypeStruct(shape, kind) for shape, kind in outs],
        scratch_shapes=list(scratch),
        compiler_params=params(),
        cost_estimate=QUICK,
        name=name,
    )(*scalars, *arrays)


def quarters_kernel(sections, at, place, *refs):
    terms, outs = refs[:-4], refs[-4:]
    for n, out in enumerate(outs):
        done = 0
        parts = [(start + (place[at] ^ n) * (rows // 4), rows // 4) for start, rows in sections]
        for top, rows in parts + [(sum(sections[-1]), 16)]:
            if not isinstance(top, int):
                top = pl.multiple_of(top, 16)
            values = [term[pl.ds(top, rows), :].astype(f32) for term in terms]
            if values[-1].shape[1] < out.shape[1]:
                values[-2:] = [jnp.concatenate(values[-2:], axis=1)]
            out[done : done + rows, :] = sum(values).astype(out.dtype)
            done += rows


def quarters(sections, at, place, terms):
    rows, width = sum(rows // 4 for _, rows in sections) + 16, terms[0].shape[1]
    outs = [((rows, width), f32)] + [((rows, width), bf16)] * 3
    kernel = functools.partial(quarters_kernel, sections, at)
    return small_call(kernel, "quarters", outs, [place], terms)


def join_cores_kernel(near, left, right, out):
    far = jnp.concatenate([left[...].astype(f32), right[...].astype(f32)], axis=1)
    out[...] = (near[...].astype(f32) + far).astype(bf16)


def join_cores(near, left, right):
    outs = [(near.shape, bf16)]
    return small_call(join_cores_kernel, "join_cores", outs, [], [near, left, right])[0]


def settle_up_kernel(*refs):
    terms, (part, vectors) = refs[:-2], refs[-2:]
    rows = part.shape[0]
    part[...] = sum(term[:rows, :].astype(f32) for term in terms).astype(bf16)
    vectors[...] = sum(term[rows:, :].astype(f32) for term in terms)


def settle_up(terms):
    rows, width = terms[0].shape
    outs = [((rows - 16, width), bf16), ((16, width), f32)]
    return small_call(settle_up_kernel, "settle_up", outs, [], terms)


def halves_kernel(place, *refs):
    terms, (kept, sent, scr) = refs[:4], refs[4:]
    few = kept.shape[0] - 16
    scr[...] = sum(term[...].astype(f32) for term in terms)
    for out, which in ((kept, place[1]), (sent, 1 - place[1])):
        out[:few, :] = scr[pl.ds(pl.multiple_of(which * few, 16), few), :].astype(out.dtype)
        out[few:, :] = scr[2 * few :, :].astype(out.dtype)


def halves(place, terms):
    rows, width = terms[0].shape
    shape = ((rows - 16) // 2 + 16, width)
    scratch = [pltpu.VMEM((rows, width), f32)]
    return small_call(
        halves_kernel, "halves", [(shape, f32), (shape, bf16)], [place], terms, scratch
    )


def settle_kernel(kept, got, part, q_sum, v_sum):
    few, width = part.shape
    half = width // 3
    total = kept[...] + got[...].astype(f32)
    part[...] = total[:few].astype(bf16)
    q_sum[...] = total[few, :half]
    v_sum[...] = total[few, 2 * half :]


def settle(kept, got):
    rows, width = kept.shape
    outs = [((rows - 16, width), bf16), ((width // 3,), f32), ((width // 3,), f32)]
    return small_call(settle_kernel, "settle", outs, [], [kept, got])


def finish_qkv_kernel(info, place, *refs):
    pieces, outs = refs[:8], refs[8:]
    rows = pieces[0].shape[0]
    half = outs[0].shape[1]
    for n, ref in enumerate(pieces):
        core = info[CORE] ^ (n // 4)
        top = pl.multiple_of((4 * core + (place[0] ^ (n % 4))) * rows, 8)
        piece = ref[...].astype(f32)
        for m, out in enumerate(outs):
            out[pl.ds(top, rows), :] = piece[:, m * half : m * half + half]


def finish_qkv(info, place, pieces):
    rows, width = pieces[0].shape
    outs = [((8 * rows, width // 3), f32)] * 3
    return small_call(finish_qkv_kernel, "finish_qkv", outs, [info, place], pieces)


def flip_head(value):
    return lax.ppermute(value, "head", [(0, 1), (1, 0)])


def flip_dp(value, bit):
    size = lax.axis_size("dp")
    return lax.ppermute(value, "dp", [(i, i ^ (1 << bit)) for i in range(size)])


def flip_both(value, bit):
    size = lax.axis_size("dp")
    pairs = [(2 * i + h, 2 * (i ^ (1 << bit)) + 1 - h) for i in range(size) for h in range(2)]
    return lax.ppermute(value, ("dp", "head"), pairs)


def bit_of(bit):
    return (lax.axis_index("dp") >> bit) & 1


def dp_bits(first):
    return list(range(first, (lax.axis_size("dp") - 1).bit_length()))


def flip_quarter(value, number, bit):
    size = lax.axis_size("dp")
    return lax.ppermute(value, "dp", [(i, i ^ (number << bit)) for i in range(size)])


def total_of(terms):
    total = 0.0
    for term in terms:
        total = total + term.astype(f32)
    return total.astype(bf16)


def rows_of(terms, place, rows):
    return total_of([lax.dynamic_slice_in_dim(term, place * rows, rows, 0) for term in terms])


def gather_pieces(part):
    size = lax.axis_size("dp")
    one = [c + 2 * x + 4 * q for c in range(2) for x in range(2) for q in range(4)]
    groups = [[16 * k + i for i in one] for k in range(size // 16)]
    return lax.all_gather(part, "dp", axis_index_groups=groups)


def finish_quarters(kept, got):
    part, sums = settle_up([kept, *got])
    for bit in dp_bits(4):
        size = part.shape[0] // 2
        part_got = flip_dp(rows_of([part], 1 - bit_of(bit), size), bit)
        part = total_of([rows_of([part], bit_of(bit), size), part_got])
        sums = sums + flip_dp(sums, bit)
    for bit in dp_bits(4)[::-1]:
        part = join(part, flip_dp(part, bit), bit_of(bit), 0)
    return part, sums


def order(*values):
    return lax.optimization_barrier(values)


def join(mine, theirs, own, axis):
    first = jnp.where(own == 0, mine, theirs)
    second = jnp.where(own == 0, theirs, mine)
    return jnp.concatenate([first, second], axis=axis)


def body(
    hidden_in,
    w_query,
    b_query,
    w_key,
    w_value,
    b_value,
    w_out,
    b_out,
    gain_one,
    shift_one,
    w_up,
    b_up,
    w_down,
    b_down,
    gain_two,
    shift_two,
    seq_length,
    block_perm,
    cotangent,
):
    D, half = w_query.shape
    FF = w_up.shape[1]
    own = hidden_in.shape[0] // BLOCK // 2
    head = lax.axis_index("head")
    core = bit_of(0)
    mine = (w_query, w_key, w_value)

    rows = D // 2
    near = flip_head(
        jnp.concatenate([lax.dynamic_slice_in_dim(w, core * rows, rows, 0) for w in mine], 1)
    )
    w_a = jnp.concatenate(mine, 1)
    bias_a = jnp.stack([b_query, b_value])
    bias_b = flip_head(bias_a)
    perm_b = flip_head(block_perm)
    place = lax.broadcasted_iota(jnp.int32, (3,), 0)
    info = jnp.where(place == HEAD, head, jnp.where(place == CORE, core, bit_of(1))).astype(
        jnp.int32
    )
    scalars_a = (info, seq_length, block_perm)
    scalars_b = (info, seq_length, perm_b)
    zeros = jnp.zeros((D,), f32)
    consts = jnp.concatenate(
        [
            jnp.stack([b_out, gain_one, shift_one, b_down, gain_two, shift_two, zeros, zeros]),
            b_up.reshape(FF // D, D),
            jnp.zeros((8 - FF // D, D), f32),
        ]
    )

    att, q_a, kv_a = attend(scalars_a, 0, hidden_in, (w_a,), bias_a, own)
    near, att = order(near, att)
    far = flip_dp(near, 0)
    att, q_b, kv_b, w_b = attend(scalars_b, 1, hidden_in, (near, far), bias_b, own, att)

    dp = lax.axis_index("dp")
    slot = lax.broadcasted_iota(jnp.int32, (3,), 0)
    place = jnp.where(slot == 0, (dp >> 1) & 3, jnp.where(slot == 1, (dp >> 3) & 1, (dp >> 2) & 3))
    place = place.astype(jnp.int32)

    block_out, *saved, down_near, down_far, vectors = middle_up(
        info, att, hidden_in, cotangent, w_out, w_up, w_down, consts
    )
    down_far = flip_dp(down_far, 0)

    def leave(mine, sent):
        return [total_of([mine[n], sent[n]]) for n in (1, 2, 3)]

    def across(beside, over, corner):
        return [flip_both(corner, 1), flip_head(over), flip_dp(beside, 1)]

    att, *leaving = order(att, *leave(down_near, down_far))
    down = across(*leaving)
    gatt, gfirst, up_near, up_far = middle_down(
        info, att, saved, vectors, w_out, w_up, w_down, consts
    )
    gatt, up_far, *down = order(gatt, up_far, *down)
    up_far = flip_dp(up_far, 0)
    down_kept, *down = quarters(((0, FF // 4),), 2, place, [*down, down_near[0], down_far[0]])
    up_far, *down = order(up_far, *down)
    gatt, *both = order(gatt, *leave(up_near, up_far), *down)
    up = across(*both[:3])
    down = [flip_quarter(value, n + 1, 2) for n, value in enumerate(both[3:])]
    d_b, near_b, *far_b = attend_back(scalars_b, 1, q_b, kv_b, att, gatt, hidden_in, own)
    d_b, *more = order(d_b, *down, *up, *far_b)
    down, up = more[:3], more[3:6]
    far_b = [flip_dp(far, 0) for far in more[6:]]
    down = gather_pieces(finish_quarters(down_kept, down)[0])
    sections = ((0, D // 2), (D // 2, 4 * OUT_ROWS))
    up_kept, *up = quarters(sections, 2, place, [*up, up_near[0], up_far[0]])
    gatt, near_b, *up = order(gatt, join_cores(near_b, *far_b), *up)
    from_other = flip_head(near_b)
    up = [flip_quarter(value, n + 1, 2) for n, value in enumerate(up)]
    d_a, near_a, *far_a = attend_back(scalars_a, 0, q_a, kv_a, att, gatt, hidden_in, own)

    from_other, d_a, *more = order(from_other, d_a, *up, *far_a)
    up, far_a = more[:3], [flip_dp(far, 0) for far in more[3:]]
    up, vectors = finish_quarters(up_kept, up)
    up = gather_pieces(up)

    kept, *out = quarters(((0, rows),), 0, place, [near_a, from_other, *far_a])
    d_a, *out = order(d_a, *out)
    got = [flip_quarter(value, n + 1, 1) for n, value in enumerate(out)]
    input_grad, next_block = input_call(info, d_a, d_b, w_a, w_b, gfirst, own)
    input_grad, *got = order(input_grad, *got)
    kept, sent = halves(place, [kept, *got])
    next_block, sent = order(next_block, sent)
    recv = flip_head(next_block)
    part, sum_q, sum_v = settle(kept, flip_dp(sent, 3))
    for bit in dp_bits(4):
        size = part.shape[0] // 2
        part_got = flip_dp(rows_of([part], 1 - bit_of(bit), size), bit)
        part = total_of([rows_of([part], bit_of(bit), size), part_got])
        sum_q, sum_v = sum_q + flip_dp(sum_q, bit), sum_v + flip_dp(sum_v, bit)
    for bit in dp_bits(3)[::-1]:
        part = join(part, flip_dp(part, bit), bit_of(bit), 0)
    part, down = order(part, down)
    got = [flip_quarter(part, n, 1) for n in (1, 2, 3)]
    pieces = [part, *got]
    grad_down = down.reshape(FF, half).astype(f32)
    input_grad = edge_call(info, recv, input_grad, own)
    grad_down, input_grad, *pieces = order(grad_down, input_grad, *pieces)
    pieces += [flip_dp(piece, 0) for piece in pieces]
    grad_up, grad_out, sum_up, *sums = finish_up(info, vectors, up)
    grad_q, grad_k, grad_v = finish_qkv(info, place, pieces)
    return (
        block_out,
        input_grad,
        grad_q,
        sum_q,
        grad_k,
        grad_v,
        sum_v,
        grad_out,
        sums[0],
        sums[1],
        sums[2],
        grad_up,
        sum_up,
        grad_down,
        sums[3],
        sums[4],
        sums[5],
    )


def solution(mesh):
    rows = P(("dp", "head"), None)
    cols = P(None, "head")
    piece = P("head")
    return jax.shard_map(
        body,
        mesh=mesh,
        in_specs=(
            P("dp", None),
            cols,
            piece,
            cols,
            cols,
            piece,
            *[P()] * 10,
            P("dp"),
            P("dp", "head"),
            rows,
        ),
        out_specs=(
            rows,
            rows,
            cols,
            piece,
            cols,
            cols,
            piece,
            cols,
            piece,
            piece,
            piece,
            cols,
            piece,
            cols,
            piece,
            piece,
            piece,
        ),
        check_vma=False,
    )
```

time: 465 us -> 374 us (0.80)
  waiting for transfers between devices: 101 us -> 52.7 us
  Pallas kernels: 256 us -> 223 us
  between operations: 2.31 us -> 15.8 us
  starting transfers between devices: 50 us -> 41.2 us
  other arithmetic: 22.4 us -> 14 us
  local copies, waits for them, and re-layouts: 24.9 us -> 20.1 us
    ppermute x45 -> x15, waiting for transfers between devices: 74.7 us -> 29.9 us  [flip_dp(): return lax.ppermute(value, 'dp', [(i, i ^ 1 << bit) for i in range(size)])]
    ppermute x45 -> x15, starting transfers between devices: 40.3 us -> 6.71 us  [flip_dp(): return lax.ppermute(value, 'dp', [(i, i ^ 1 << bit) for i in range(size)])]
    pallas_call x23 -> x18, Pallas kernels: 256 us -> 223 us  [the longest x2 49.2 us: attend_back(): pl.pallas_call(functools.partial(attend_back_kernel, own), grid_spec=pltp...]
    ppermute x0 -> x14, starting transfers between devices: none -> 26.9 us  [the longest x12 21 us: flip_quarter(): lax.ppermute(value, 'dp', [(i, i ^ number << bit) for i in range(size)])]
    ppermute x9 -> x7, waiting for transfers between devices: 25.8 us -> 11.6 us  [flip_head(): return lax.ppermute(value, 'head', [(0, 1), (1, 0)])]
    ppermute x0 -> x14, waiting for transfers between devices: none -> 11.1 us  [the longest x12 11.1 us: flip_quarter(): lax.ppermute(value, 'dp', [(i, i ^ number << bit) for i in range(size)])]
    squeeze x0 -> x4, local copies, waits for them, and re-layouts: none -> 7.06 us  [the longest x2 3.02 us: body(): up_kept, *up = quarters(sections, 2, place, [*up, up_near[0], up_far[0]])]
    reshape x14 -> x1, local copies, waits for them, and re-layouts: 5.99 us -> 0.01 us  [body(): b_up.reshape(FF // D, D)]
  transfers between devices with their start and end apart: 54 -> 38, of which waited for: 18 -> 15; matrix products, arithmetic and copies ran while one was open for 8% -> 4% of each run, Pallas kernels for 35% -> 41%
where the time goes in v2:
time: 374 us; the launch traced here: 367 us
  Pallas kernels  223 us (60%)
  waiting for transfers between devices  52.7 us (14%)
  starting transfers between devices  41.2 us (11%)
  local copies, waits for them, and re-layouts  20.1 us (5%)
  between operations  15.8 us (4%)
  other arithmetic  14 us (4%)
    pallas_call x2, Pallas kernels, attend_back(): pl.pallas_call(functools.partial(attend_back_kernel, own), grid_spec=pltp...  49.2 us
    pallas_call x1, Pallas kernels, middle_up(): pl.pallas_call(middle_up_kernel, grid_spec=pltpu.PrefetchScalarGridSpec(n...  45.6 us
    pallas_call x1, Pallas kernels, middle_down(): pl.pallas_call(middle_down_kernel, grid_spec=pltpu.PrefetchScalarGridSpec...  42 us
    pallas_call x2, Pallas kernels, attend(): pl.pallas_call(functools.partial(body, own), grid_spec=pltpu.PrefetchScal...  38.2 us
    ppermute x15, waiting for transfers between devices, flip_dp(): return lax.ppermute(value, 'dp', [(i, i ^ 1 << bit) for i in range(size)])  29.9 us
    pallas_call x10, Pallas kernels, small_call(): pl.pallas_call(kernel, in_specs=[smem] * len(scalars) + [vmem] * len(arra...  28.2 us
    ppermute x12, starting transfers between devices, flip_quarter(): lax.ppermute(value, 'dp', [(i, i ^ number << bit) for i in range(size)])  21 us
    pallas_call x1, Pallas kernels, input_call(): pl.pallas_call(functools.partial(input_kernel, own), grid_spec=pltpu.Pref...  15.5 us
  transfers between devices with their start and end apart: 38, of which 15 were waited for; matrix products, arithmetic and copies ran while one was open for 4% of the time, Pallas kernels for 41%

profile of v2, /device:TPU:0, one launch (start us, length us, event | category | flops | bytes accessed | tf_op | source)
XLA Modules:
  0.0 366.8 jit_solution(9446500205766276002)
XLA Ops:
  10.5 3.0 collective-permute-start.1
  15.6 1.2 copy-done
  16.9 18.8 %attend_forward.2 = (bf16[1536,768]{1,0:T(8,128)(2,1)}, bf16[3,6,512,128]{3,2,1,0:T(8,128)(2,1)}, bf16[4,512,768]{2,1,0:T(8,128)(2,1)}) custom-call(s32[3]{0:T(128)} %compare_select_fusion.3.info, s32[1]{0:T(128)S(6)} %copy.42.length, s32[6,6]{1,0:T(8,128)} %perm.3, bf16[3072,768]{1,0:T(8,128)(2,1)} %x_ref.5, bf16[768,1152]{1,0:T(8,128)(2,1)} %copy-done, ...), custom_call_target="tpu_custom_call" | custom-call | flops 1000 | bytes 1000 | tf_op jit(solution)/shard_map/attend_forward/pallas_call | solution.py:153
  35.9 2.0 collective-permute-start
  38.1 1.3 concatenate.18.c_ref
  41.1 19.4 %attend_forward.3 = (bf16[1536,768]{1,0:T(8,128)(2,1)}, bf16[3,6,512,128]{3,2,1,0:T(8,128)(2,1)}, bf16[4,512,768]{2,1,0:T(8,128)(2,1)}, bf16[768,1152]{1,0:T(8,128)(2,1)}) custom-call(s32[3]{0:T(128)} %compare_select_fusion.3.info, s32[1]{0:T(128)S(6)} %copy.42.length, s32[6,6]{1,0:T(8,128)} %copy-done.30, ...), custom_call_target="tpu_custom_call", output_to_operand_aliasing={{0}: (7, {})} | custom-call | flops 1000 | bytes 1000 | tf_op jit(solution)/shard_map/attend_forward/pallas_call | solution.py:153
  60.5 45.6 %middle_up.1 = (bf16[1536,768]{1,0:T(8,128)(2,1)}, bf16[1536,3072]{1,0:T(8,128)(2,1)}, f32[1536,768]{1,0:T(8,128)}, f32[1536,128]{1,0:T(8,128)}, f32[1536,768]{1...) custom-call(s32[3]{0:T(128)} %compare_select_fusion.3.info, ...), custom_call_target="tpu_custom_call" | custom-call | flops 1000 | bytes 1000 | tf_op jit(solution)/shard_map/middle_up/pallas_call | solution.py:428
  106.2 4.8 %collective-permute-done.4 = bf16[4,784,384]{2,1,0:T(8,128)(2,1)S(1)} collective-permute-done((bf16[4,784,384]{2,1,0:T(8,128)(2,1)}, bf16[4,784,384]{2,1,0:T(8,128)(2,1)S(1)}, u32[]{:S(2)}, u32[]{:S(2)}) %collective-permute-start.4) | collective-permute-done | bytes 2408480 | tf_op jit(solution)/shard_map/ppermute | solution.py:807
  111.0 2.8 fusion.5
  113.8 3.0 collective-permute-start.5
  117.4 42.0 %middle_down.1 = (bf16[1536,768]{1,0:T(8,128)(2,1)}, f32[1536,768]{1,0:T(8,128)}, bf16[4,528,768]{2,1,0:T(8,128)(2,1)}, bf16[4,528,768]{2,1,0:T(8,128)(2,1)}) custom-call(s32[3]{0:T(128)} %compare_select_fusion.3.info, bf16[1536,768]{1,0:T(8,128)(2,1)} %get-tuple-element.148.att_ref, bf16[1536,3072]{1,0:T(8,128)(2,1)} %get-tuple-element.149.slope_ref, ...), custom_call_target="tpu_custom_call" | custom-call | flops 1000 | bytes 1000 | tf_op jit(solution)/shard_map/middle_down/pallas_call | solution.py:561
  160.1 1.9 slice_bitcast_fusion.3.refs_3_
  162.0 2.1 slice_bitcast_fusion.2.refs_4_
  164.1 2.9 quarters.3
  167.1 3.4 fusion.2
  170.5 2.8 collective-permute-start.12
  174.0 1.9 collective-permute-start.9
  175.9 2.6 collective-permute-start.10
  178.5 3.9 %collective-permute-done.9.refs_1_ = bf16[208,384]{1,0:T(8,128)(2,1)S(1)} collective-permute-done((bf16[208,384]{1,0:T(8,128)(2,1)S(1)}, bf16[208,384]{1,0:T(8,128)(2,1)S(1)}, u32[]{:S(2)}, u32[]{:S(2)}) %collective-permute-start.9) | collective-permute-done | bytes 159776 | tf_op jit(solution)/shard_map/ppermute | solution.py:826
  182.4 3.2 collective-permute-start.11
  185.6 24.5 %attend_backward.2 = (bf16[2048,1152]{1,0:T(8,128)(2,1)}, bf16[400,1152]{1,0:T(8,128)(2,1)}, bf16[400,640]{1,0:T(8,128)(2,1)}, bf16[400,512]{1,0:T(8,128)(2,1)}) custom-call(s32[3]{0:T(128)} %compare_select_fusion.3.info, s32[1]{0:T(128)S(6)} %copy.42.length, s32[6,6]{1,0:T(8,128)} %copy-done.30, bf16[3,6,512,128]{3,2,1,0:T(8,128)(2,1)} %get-tuple-element.173.qaug_ref, ...), custom_call_target="tpu_custom_call" | custom-call | flops 1000 | bytes 1000 | tf_op jit(solution)/shard_map/attend_backward/pallas_call | solution.py:259
  210.7 1.9 settle_up.2
  214.2 2.1 slice_bitcast_fusion.refs_4_
  216.3 3.5 quarters.4
  220.6 2.6 join_cores.1
  223.2 1.6 collective-permute-start.17
  225.5 2.6 collective-permute-start.19
  229.2 24.7 %attend_backward.3 = (bf16[2048,1152]{1,0:T(8,128)(2,1)}, bf16[400,1152]{1,0:T(8,128)(2,1)}, bf16[400,640]{1,0:T(8,128)(2,1)}, bf16[400,512]{1,0:T(8,128)(2,1)}) custom-call(s32[3]{0:T(128)} %compare_select_fusion.3.info, s32[1]{0:T(128)S(6)} %copy.42.length, s32[6,6]{1,0:T(8,128)} %perm.3, bf16[3,6,512,128]{3,2,1,0:T(8,128)(2,1)} %get-tuple-element.144.qaug_ref, ...), custom_call_target="tpu_custom_call" | custom-call | flops 1000 | bytes 1000 | tf_op jit(solution)/shard_map/attend_backward/pallas_call | solution.py:259
  254.8 2.0 settle_up.3
  257.4 2.3 collective-permute-done.22.refs_3_
  260.7 3.0 quarters.5
  263.6 1.7 collective-permute-start.23
  265.3 2.8 collective-permute-start.24
  268.9 15.5 %input_grad.1 = (f32[1536,768]{1,0:T(8,128)}, bf16[512,768]{1,0:T(8,128)(2,1)}) custom-call(s32[3]{0:T(128)} %compare_select_fusion.3.info, bf16[2048,1152]{1,0:T(8,128)(2,1)} %get-tuple-element.210.da, bf16[2048,1152]{1,0:T(8,128)(2,1)} %get-tuple-element.211.db, bf16[768,1152]{1,0:T(8,128)(2,1)} %copy-done, bf16[768,1152]{1,0:T(8,128)(2,1)} %get-tuple-element.212.wb, ...), custom_call_target="tpu_custom_call" | custom-call | flops 1000 | bytes 1000 | tf_op jit(solution)/shard_map/input_grad/pallas_call | solution.py:609
  284.4 2.8 collective-permute-done.25.refs_3_
  287.9 2.3 halves.1
  290.2 3.9 %collective-permute-start.26 = (bf16[64,1152]{1,0:T(8,128)(2,1)}, bf16[64,1152]{1,0:T(8,128)(2,1)S(1)}, u32[]{:S(2)}, u32[]{:S(2)}) collective-permute-start(bf16[64,1152]{1,0:T(8,128)(2,1)} %get-tuple-element.224), channel_id=1, source_target_pairs={{0,16},{2,18},{4,20},{6,22},{8,24},{10,26},{12,28},{14,30},{16,0},... | collective-permute-start | bytes 442376 | tf_op jit(solution)/shard_map/ppermute | solution.py:807
  294.1 14.3 %collective-permute-done.26.got = bf16[64,1152]{1,0:T(8,128)(2,1)S(1)} collective-permute-done((bf16[64,1152]{1,0:T(8,128)(2,1)}, bf16[64,1152]{1,0:T(8,128)(2,1)S(1)}, u32[]{:S(2)}, u32[]{:S(2)}) %collective-permute-start.26) | collective-permute-done | bytes 147488 | tf_op jit(solution)/shard_map/ppermute | solution.py:807
  309.1 1.7 settle.1
  310.8 7.1 %collective-permute-done.27 = bf16[48,1152]{1,0:T(8,128)(2,1)S(1)} collective-permute-done((bf16[48,1152]{1,0:T(8,128)(2,1)}, bf16[48,1152]{1,0:T(8,128)(2,1)S(1)}, u32[]{:S(2)}, u32[]{:S(2)}) %collective-permute-start.27) | collective-permute-done | bytes 110624 | tf_op jit(solution)/shard_map/ppermute | solution.py:807
  318.8 11.4 %collective-permute-done.28.recv = bf16[512,768]{1,0:T(8,128)(2,1)S(1)} collective-permute-done((bf16[512,768]{1,0:T(8,128)(2,1)}, bf16[512,768]{1,0:T(8,128)(2,1)S(1)}, u32[]{:S(2)}, u32[]{:S(2)}) %collective-permute-start.28) | collective-permute-done | bytes 786464 | tf_op jit(solution)/shard_map/ppermute | solution.py:802
  331.1 4.4 %edge_block.1 = f32[1536,768]{1,0:T(8,128)} custom-call(s32[3]{0:T(128)} %compare_select_fusion.3.info, bf16[512,768]{1,0:T(8,128)(2,1)} %copy-done.9, f32[1536,768]{1,0:T(8,128)} %get-tuple-element.233.rest), custom_call_target="tpu_custom_call", output_to_operand_aliasing={{}: (2, {})} | custom-call | flops 1000 | bytes 1000 | tf_op jit(solution)/shard_map/edge_block/pallas_call | solution.py:634
  335.5 3.0 collective-permute-start.31
  339.2 4.2 %bitcast_convert_fusion = f32[3072,384]{1,0:T(8,128)} fusion(bf16[16,192,384]{2,1,0:T(8,128)(2,1)} %bitcast.26), kind=kLoop, calls=%fused_computation | loop fusion | flops 1179648 | bytes 7077888 | tf_op jit(solution)/shard_map/convert_element_type | solution.py:989
  343.3 1.6 collective-permute-done.31.refs_3_
  344.9 2.2 collective-permute-done.30.refs_2_
  351.2 3.5 finish_qkv.1
  354.8 4.8 %finish_up.1 = (f32[768,1536]{1,0:T(8,128)}, f32[768,384]{1,0:T(8,128)}, f32[1536]{0:T(1024)}, f32[384]{0:T(512)}, f32[384]{0:T(512)}, /*index=5*/f32[384]{0:T(512)}, f32[384]{0:T(512)}, f32[384]{0:T(512)}, f32[384]{0:T(512)}) custom-call(s32[3]{0:T(128)} %compare_select_fusion.3.info, f32[16,768]{1,0:T(8,128)} %get-tuple-element.249.vec_in_ref, ...), custom_call_target="tpu_custom_call" | custom-call | flops 1000 | bytes 1000 | tf_op jit(solution)/shard_map/finish_up/pallas_call | solution.py:694
  (174 shorter events, 24.6 us)
Async XLA Ops:
  7.2 328.3 %all-gather.5.cloned.1.call-start = ((), (), s32[]{:S(2)}) async-start(), calls=%async_computation | async-start | bytes 2506752 | tf_op jit(solution)/shard_map/all_gather | solution.py:844
  10.5 25.3 %collective-permute-start.1 = (bf16[384,1152]{1,0:T(8,128)(2,1)}, bf16[384,1152]{1,0:T(8,128)(2,1)}, u32[]{:S(2)}, u32[]{:S(2)}) collective-permute-start(bf16[384,1152]{1,0:T(8,128)(2,1)} %pad_maximum_fusion), channel_id=1, source_target_pairs={{0,1},{1,0},{2,3},{3,2},{4,5},{5,4},{6,7},{7,6},{8,9},{9,8},{10,11... | collective-permute-start | bytes 2654216 | tf_op jit(solution)/shard_map/ppermute | solution.py:802
  16.8 19.1 %copy-start.31 = (s32[6,6]{1,0:T(8,128)S(1)}, s32[6,6]{1,0:T(8,128)}, u32[]{:S(2)}) copy-start(s32[6,6]{1,0:T(8,128)} %perm.3) | copy-start | bytes 436
  16.8 21.1 %copy-start.34 = (f32[768]{0:T(1024)S(1)}, f32[768]{0:T(1024)}, u32[]{:S(2)}) copy-start(f32[768]{0:T(1024)} %param.26) | copy-start | bytes 9220
  16.8 21.1 %copy-start.35 = (f32[768]{0:T(1024)S(1)}, f32[768]{0:T(1024)}, u32[]{:S(2)}) copy-start(f32[768]{0:T(1024)} %param.27) | copy-start | bytes 9220
  16.8 21.1 %copy-start.36 = (f32[768]{0:T(1024)S(1)}, f32[768]{0:T(1024)}, u32[]{:S(2)}) copy-start(f32[768]{0:T(1024)} %param.28) | copy-start | bytes 9220
  16.8 21.1 %copy-start.37 = (f32[768]{0:T(1024)S(1)}, f32[768]{0:T(1024)}, u32[]{:S(2)}) copy-start(f32[768]{0:T(1024)} %param.32) | copy-start | bytes 9220
  16.9 21.1 %copy-start.38 = (f32[768]{0:T(1024)S(1)}, f32[768]{0:T(1024)}, u32[]{:S(2)}) copy-start(f32[768]{0:T(1024)} %param.33) | copy-start | bytes 9220
  16.9 21.2 %copy-start.39 = (f32[768]{0:T(1024)S(1)}, f32[768]{0:T(1024)}, u32[]{:S(2)}) copy-start(f32[768]{0:T(1024)} %param.34) | copy-start | bytes 9220
  16.9 21.2 %copy-start.33 = (f32[3072]{0:T(1024)S(1)}, f32[3072]{0:T(1024)}, u32[]{:S(2)}) copy-start(f32[3072]{0:T(1024)} %param.30) | copy-start | bytes 36868
  35.7 3.9 %collective-permute-start.2 = (bf16[384,1152]{1,0:T(8,128)(2,1)}, bf16[384,1152]{1,0:T(8,128)(2,1)S(1)}, u32[]{:S(2)}, u32[]{:S(2)}) collective-permute-start(bf16[384,1152]{1,0:T(8,128)(2,1)} %collective-permute-done.1.near), channel_id=1, source_target_pairs={{0,2},{2,0},{4,6},{6,4},{8,10},{10,8},{12,14},{14,12},{16,18},{18,... | collective-permute-start | bytes 2654216 | tf_op jit(solution)/shard_map/ppermute | solution.py:807
  35.8 3.8 %collective-permute-start.3 = (f32[2,384]{1,0:T(2,128)S(1)}, f32[2,384]{1,0:T(2,128)S(1)}, u32[]{:S(2)}, u32[]{:S(2)}) collective-permute-start(f32[2,384]{1,0:T(2,128)S(1)} %copy-done.32), channel_id=1, source_target_pairs={{0,1},{1,0},{2,3},{3,2},{4,5},{5,4},{6,7},{7,6},{8,9},{9,8},{10,11... | collective-permute-start | bytes 9224 | tf_op jit(solution)/shard_map/ppermute | solution.py:802
  35.9 3.7 %collective-permute-start = (s32[6,6]{1,0:T(8,128)S(1)}, s32[6,6]{1,0:T(8,128)S(1)}, u32[]{:S(2)}, u32[]{:S(2)}) collective-permute-start(s32[6,6]{1,0:T(8,128)S(1)} %copy-done.31), channel_id=1, source_target_pairs={{0,1},{1,0},{2,3},{3,2},{4,5},{5,4},{6,7},{7,6},{8,9},{9,8},{10,11... | collective-permute-start | bytes 440 | tf_op jit(solution)/shard_map/ppermute | solution.py:802
  106.1 4.9 %collective-permute-start.4 = (bf16[4,784,384]{2,1,0:T(8,128)(2,1)}, bf16[4,784,384]{2,1,0:T(8,128)(2,1)S(1)}, u32[]{:S(2)}, u32[]{:S(2)}) collective-permute-start(bf16[4,784,384]{2,1,0:T(8,128)(2,1)} %get-tuple-element.147), channel_id=1, source_target_pairs={{0,2},{2,0},{4,6},{6,4},{8,10},{10,8},{12,14},{14,12},{16,18},{18,... | collective-permute-start | bytes 7225352 | tf_op jit(solution)/shard_map/ppermute | solution.py:807
  113.8 45.7 %collective-permute-start.5 = (bf16[784,384]{1,0:T(8,128)(2,1)S(1)}, bf16[784,384]{1,0:T(8,128)(2,1)}, u32[]{:S(2)}, u32[]{:S(2)}) collective-permute-start(bf16[784,384]{1,0:T(8,128)(2,1)S(1)} %get-tuple-element.156), channel_id=1, source_target_pairs={{0,5},{1,4},{2,7},{3,6},{4,1},{5,0},{6,3},{7,2},{8,13},{9,12},{10,... | collective-permute-start | bytes 1806344 | tf_op jit(solution)/shard_map/ppermute | solution.py:813
  116.8 42.7 %collective-permute-start.6 = (bf16[784,384]{1,0:T(8,128)(2,1)S(1)}, bf16[784,384]{1,0:T(8,128)(2,1)}, u32[]{:S(2)}, u32[]{:S(2)}) collective-permute-start(bf16[784,384]{1,0:T(8,128)(2,1)S(1)} %get-tuple-element.157), channel_id=1, source_target_pairs={{0,1},{1,0},{2,3},{3,2},{4,5},{5,4},{6,7},{7,6},{8,9},{9,8},{10,11... | collective-permute-start | bytes 1806344 | tf_op jit(solution)/shard_map/ppermute | solution.py:802
  117.2 42.2 %collective-permute-start.7 = (bf16[784,384]{1,0:T(8,128)(2,1)S(1)}, bf16[784,384]{1,0:T(8,128)(2,1)}, u32[]{:S(2)}, u32[]{:S(2)}) collective-permute-start(bf16[784,384]{1,0:T(8,128)(2,1)S(1)} %get-tuple-element.158), channel_id=1, source_target_pairs={{0,4},{2,6},{4,0},{6,2},{8,12},{10,14},{12,8},{14,10},{16,20},{18,... | collective-permute-start | bytes 1806344 | tf_op jit(solution)/shard_map/ppermute | solution.py:807
  159.5 7.6 %collective-permute-start.8 = (bf16[4,528,768]{2,1,0:T(8,128)(2,1)}, bf16[4,528,768]{2,1,0:T(8,128)(2,1)}, u32[]{:S(2)}, u32[]{:S(2)}) collective-permute-start(bf16[4,528,768]{2,1,0:T(8,128)(2,1)} %get-tuple-element.161), channel_id=1, source_target_pairs={{0,2},{2,0},{4,6},{6,4},{8,10},{10,8},{12,14},{14,12},{16,18},{18,... | collective-permute-start | bytes 9732104 | tf_op jit(solution)/shard_map/ppermute | solution.py:807
  170.5 39.6 %collective-permute-start.12 = (bf16[528,768]{1,0:T(8,128)(2,1)}, bf16[528,768]{1,0:T(8,128)(2,1)}, u32[]{:S(2)}, u32[]{:S(2)}) collective-permute-start(bf16[528,768]{1,0:T(8,128)(2,1)} %get-tuple-element.180), channel_id=1, source_target_pairs={{0,5},{1,4},{2,7},{3,6},{4,1},{5,0},{6,3},{7,2},{8,13},{9,12},{10,... | collective-permute-start | bytes 2433032 | tf_op jit(solution)/shard_map/ppermute | solution.py:813
  173.3 36.7 %collective-permute-start.13 = (bf16[528,768]{1,0:T(8,128)(2,1)}, bf16[528,768]{1,0:T(8,128)(2,1)}, u32[]{:S(2)}, u32[]{:S(2)}) collective-permute-start(bf16[528,768]{1,0:T(8,128)(2,1)} %get-tuple-element.181), channel_id=1, source_target_pairs={{0,1},{1,0},{2,3},{3,2},{4,5},{5,4},{6,7},{7,6},{8,9},{9,8},{10,11... | collective-permute-start | bytes 2433032 | tf_op jit(solution)/shard_map/ppermute | solution.py:802
  173.8 36.3 %collective-permute-start.14 = (bf16[528,768]{1,0:T(8,128)(2,1)}, bf16[528,768]{1,0:T(8,128)(2,1)}, u32[]{:S(2)}, u32[]{:S(2)}) collective-permute-start(bf16[528,768]{1,0:T(8,128)(2,1)} %get-tuple-element.182), channel_id=1, source_target_pairs={{0,4},{2,6},{4,0},{6,2},{8,12},{10,14},{12,8},{14,10},{16,20},{18,... | collective-permute-start | bytes 2433032 | tf_op jit(solution)/shard_map/ppermute | solution.py:807
  174.0 8.4 %collective-permute-start.9 = (bf16[208,384]{1,0:T(8,128)(2,1)S(1)}, bf16[208,384]{1,0:T(8,128)(2,1)S(1)}, u32[]{:S(2)}, u32[]{:S(2)}) collective-permute-start(bf16[208,384]{1,0:T(8,128)(2,1)S(1)} %copy-done.47), channel_id=1, source_target_pairs={{0,8},{2,10},{4,12},{6,14},{8,0},{10,2},{12,4},{14,6},{16,24},{18,... | collective-permute-start | bytes 479240 | tf_op jit(solution)/shard_map/ppermute | solution.py:826
  175.9 34.1 %collective-permute-start.10 = (bf16[208,384]{1,0:T(8,128)(2,1)}, bf16[208,384]{1,0:T(8,128)(2,1)S(1)}, u32[]{:S(2)}, u32[]{:S(2)}) collective-permute-start(bf16[208,384]{1,0:T(8,128)(2,1)} %get-tuple-element.178), channel_id=1, source_target_pairs={{0,16},{2,18},{4,20},{6,22},{8,24},{10,26},{12,28},{14,30},{16,0},... | collective-permute-start | bytes 479240 | tf_op jit(solution)/shard_map/ppermute | solution.py:826
  182.4 27.7 %copy-start.26 = (bf16[208,384]{1,0:T(8,128)(2,1)}, bf16[208,384]{1,0:T(8,128)(2,1)S(1)}, u32[]{:S(2)}) copy-start(bf16[208,384]{1,0:T(8,128)(2,1)S(1)} %collective-permute-done.9.refs_1_) | copy-start | bytes 479236
  182.4 27.7 %collective-permute-start.11 = (bf16[208,384]{1,0:T(8,128)(2,1)S(1)}, bf16[208,384]{1,0:T(8,128)(2,1)S(1)}, u32[]{:S(2)}, u32[]{:S(2)}) collective-permute-start(bf16[208,384]{1,0:T(8,128)(2,1)S(1)} %copy-done.46), channel_id=1, source_target_pairs={{0,24},{2,26},{4,28},{6,30},{8,16},{10,18},{12,20},{14,22},{16,8},... | collective-permute-start | bytes 479240 | tf_op jit(solution)/shard_map/ppermute | solution.py:826
  212.7 142.1 %all-gather.7.cloned.1.call-start = ((), (), s32[]{:S(2)}) async-start(), calls=%async_computation.1 | async-start | bytes 3342336 | tf_op jit(solution)/shard_map/all_gather | solution.py:844
  212.7 7.1 %collective-permute-start.16 = (bf16[400,512]{1,0:T(8,128)(2,1)}, bf16[400,512]{1,0:T(8,128)(2,1)}, u32[]{:S(2)}, u32[]{:S(2)}) collective-permute-start(bf16[400,512]{1,0:T(8,128)(2,1)} %get-tuple-element.186), channel_id=1, source_target_pairs={{0,2},{2,0},{4,6},{6,4},{8,10},{10,8},{12,14},{14,12},{16,18},{18,... | collective-permute-start | bytes 1228808 | tf_op jit(solution)/shard_map/ppermute | solution.py:807
  212.8 7.0 %collective-permute-start.15 = (bf16[400,640]{1,0:T(8,128)(2,1)}, bf16[400,640]{1,0:T(8,128)(2,1)S(1)}, u32[]{:S(2)}, u32[]{:S(2)}) collective-permute-start(bf16[400,640]{1,0:T(8,128)(2,1)} %get-tuple-element.185), channel_id=1, source_target_pairs={{0,2},{2,0},{4,6},{6,4},{8,10},{10,8},{12,14},{14,12},{16,18},{18,... | collective-permute-start | bytes 1536008 | tf_op jit(solution)/shard_map/ppermute | solution.py:807
  223.2 30.8 %collective-permute-start.17 = (bf16[400,1152]{1,0:T(8,128)(2,1)}, bf16[400,1152]{1,0:T(8,128)(2,1)S(1)}, u32[]{:S(2)}, u32[]{:S(2)}) collective-permute-start(bf16[400,1152]{1,0:T(8,128)(2,1)} %join_cores.1), channel_id=1, source_target_pairs={{0,1},{1,0},{2,3},{3,2},{4,5},{5,4},{6,7},{7,6},{8,9},{9,8},{10,11... | collective-permute-start | bytes 2764808 | tf_op jit(solution)/shard_map/ppermute | solution.py:802
  224.8 29.1 %collective-permute-start.18 = (bf16[144,768]{1,0:T(8,128)(2,1)S(1)}, bf16[144,768]{1,0:T(8,128)(2,1)S(1)}, u32[]{:S(2)}, u32[]{:S(2)}) collective-permute-start(bf16[144,768]{1,0:T(8,128)(2,1)S(1)} %copy-done.45), channel_id=1, source_target_pairs={{0,8},{2,10},{4,12},{6,14},{8,0},{10,2},{12,4},{14,6},{16,24},{18,... | collective-permute-start | bytes 663560 | tf_op jit(solution)/shard_map/ppermute | solution.py:826
  225.5 28.4 %collective-permute-start.19 = (bf16[144,768]{1,0:T(8,128)(2,1)S(1)}, bf16[144,768]{1,0:T(8,128)(2,1)S(1)}, u32[]{:S(2)}, u32[]{:S(2)}) collective-permute-start(bf16[144,768]{1,0:T(8,128)(2,1)S(1)} %copy-done.44), channel_id=1, source_target_pairs={{0,16},{2,18},{4,20},{6,22},{8,24},{10,26},{12,28},{14,30},{16,0},... | collective-permute-start | bytes 663560 | tf_op jit(solution)/shard_map/ppermute | solution.py:826
  228.1 25.8 %collective-permute-start.20 = (bf16[144,768]{1,0:T(8,128)(2,1)S(1)}, bf16[144,768]{1,0:T(8,128)(2,1)S(1)}, u32[]{:S(2)}, u32[]{:S(2)}) collective-permute-start(bf16[144,768]{1,0:T(8,128)(2,1)S(1)} %copy-done.43), channel_id=1, source_target_pairs={{0,24},{2,26},{4,28},{6,30},{8,16},{10,18},{12,20},{14,22},{16,8},... | collective-permute-start | bytes 663560 | tf_op jit(solution)/shard_map/ppermute | solution.py:826
  256.8 2.9 collective-permute-start.21
  256.9 2.8 collective-permute-start.22
  263.6 20.8 %collective-permute-start.23 = (bf16[112,1152]{1,0:T(8,128)(2,1)}, bf16[112,1152]{1,0:T(8,128)(2,1)S(1)}, u32[]{:S(2)}, u32[]{:S(2)}) collective-permute-start(bf16[112,1152]{1,0:T(8,128)(2,1)} %get-tuple-element.215), channel_id=1, source_target_pairs={{0,4},{2,6},{4,0},{6,2},{8,12},{10,14},{12,8},{14,10},{16,20},{18,... | collective-permute-start | bytes 774152 | tf_op jit(solution)/shard_map/ppermute | solution.py:826
  265.3 19.1 %collective-permute-start.24 = (bf16[112,1152]{1,0:T(8,128)(2,1)}, bf16[112,1152]{1,0:T(8,128)(2,1)S(1)}, u32[]{:S(2)}, u32[]{:S(2)}) collective-permute-start(bf16[112,1152]{1,0:T(8,128)(2,1)} %get-tuple-element.216), channel_id=1, source_target_pairs={{0,8},{2,10},{4,12},{6,14},{8,0},{10,2},{12,4},{14,6},{16,24},{18,... | collective-permute-start | bytes 774152 | tf_op jit(solution)/shard_map/ppermute | solution.py:826
  268.1 19.1 %collective-permute-start.25 = (bf16[112,1152]{1,0:T(8,128)(2,1)}, bf16[112,1152]{1,0:T(8,128)(2,1)S(1)}, u32[]{:S(2)}, u32[]{:S(2)}) collective-permute-start(bf16[112,1152]{1,0:T(8,128)(2,1)} %get-tuple-element.217), channel_id=1, source_target_pairs={{0,12},{2,14},{4,8},{6,10},{8,4},{10,6},{12,0},{14,2},{16,28},{18,... | collective-permute-start | bytes 774152 | tf_op jit(solution)/shard_map/ppermute | solution.py:826
  290.2 18.3 %collective-permute-start.26 = (bf16[64,1152]{1,0:T(8,128)(2,1)}, bf16[64,1152]{1,0:T(8,128)(2,1)S(1)}, u32[]{:S(2)}, u32[]{:S(2)}) collective-permute-start(bf16[64,1152]{1,0:T(8,128)(2,1)} %get-tuple-element.224), channel_id=1, source_target_pairs={{0,16},{2,18},{4,20},{6,22},{8,24},{10,26},{12,28},{14,30},{16,0},... | collective-permute-start | bytes 442376 | tf_op jit(solution)/shard_map/ppermute | solution.py:807
  310.8 7.1 %collective-permute-start.27 = (bf16[48,1152]{1,0:T(8,128)(2,1)}, bf16[48,1152]{1,0:T(8,128)(2,1)S(1)}, u32[]{:S(2)}, u32[]{:S(2)}) collective-permute-start(bf16[48,1152]{1,0:T(8,128)(2,1)} %get-tuple-element.225), channel_id=1, source_target_pairs={{0,16},{2,18},{4,20},{6,22},{8,24},{10,26},{12,28},{14,30},{16,0},... | collective-permute-start | bytes 331784 | tf_op jit(solution)/shard_map/ppermute | solution.py:807
  310.8 19.4 %collective-permute-start.28 = (bf16[512,768]{1,0:T(8,128)(2,1)}, bf16[512,768]{1,0:T(8,128)(2,1)S(1)}, u32[]{:S(2)}, u32[]{:S(2)}) collective-permute-start(bf16[512,768]{1,0:T(8,128)(2,1)} %get-tuple-element.232), channel_id=1, source_target_pairs={{0,1},{1,0},{2,3},{3,2},{4,5},{5,4},{6,7},{7,6},{8,9},{9,8},{10,11... | collective-permute-start | bytes 2359304 | tf_op jit(solution)/shard_map/ppermute | solution.py:802
  318.8 28.9 %copy-start.8 = (bf16[96,1152]{1,0:T(8,128)(2,1)}, bf16[96,1152]{1,0:T(8,128)(2,1)S(1)}, u32[]{:S(2)}) copy-start(bf16[96,1152]{1,0:T(8,128)(2,1)S(1)} %pad_maximum_fusion.1.refs_0_) | copy-start | bytes 663556
  335.5 9.4 %collective-permute-start.31 = (bf16[96,1152]{1,0:T(8,128)(2,1)S(1)}, bf16[96,1152]{1,0:T(8,128)(2,1)S(1)}, u32[]{:S(2)}, u32[]{:S(2)}) collective-permute-start(bf16[96,1152]{1,0:T(8,128)(2,1)S(1)} %pad_maximum_fusion.1.refs_0_), channel_id=1, source_target_pairs={{0,12},{2,14},{4,8},{6,10},{8,4},{10,6},{12,0},{14,2},{16,28},{18,... | collective-permute-start | bytes 663560 | tf_op jit(solution)/shard_map/ppermute | solution.py:826
  338.5 8.5 %collective-permute-start.30 = (bf16[96,1152]{1,0:T(8,128)(2,1)S(1)}, bf16[96,1152]{1,0:T(8,128)(2,1)S(1)}, u32[]{:S(2)}, u32[]{:S(2)}) collective-permute-start(bf16[96,1152]{1,0:T(8,128)(2,1)S(1)} %pad_maximum_fusion.1.refs_0_), channel_id=1, source_target_pairs={{0,8},{2,10},{4,12},{6,14},{8,0},{10,2},{12,4},{14,6},{16,24},{18,... | collective-permute-start | bytes 663560 | tf_op jit(solution)/shard_map/ppermute | solution.py:826
  338.5 9.2 %collective-permute-start.29 = (bf16[96,1152]{1,0:T(8,128)(2,1)S(1)}, bf16[96,1152]{1,0:T(8,128)(2,1)S(1)}, u32[]{:S(2)}, u32[]{:S(2)}) collective-permute-start(bf16[96,1152]{1,0:T(8,128)(2,1)S(1)} %pad_maximum_fusion.1.refs_0_), channel_id=1, source_target_pairs={{0,4},{2,6},{4,0},{6,2},{8,12},{10,14},{12,8},{14,10},{16,20},{18,... | collective-permute-start | bytes 663560 | tf_op jit(solution)/shard_map/ppermute | solution.py:826
  347.7 1.5 collective-permute-start.32
  347.7 1.8 collective-permute-start.33
  348.3 1.6 collective-permute-start.34
  348.3 1.8 collective-permute-start.35
  (38 other events, 141.1 us)
Sparse Core Ops, SparseCore 0:
  212.8 48.1 all-gather.4
  263.3 53.9 all-gather.6
